TPU v7x, 32 devices: a whole 2x2x4 slice. The times are simulated.
32 devices in a mesh: dp: 8 (over z, core), tensor: 4 (over y, x).
Axes of the slice: x: 2, y: 2, z: 4, core: 2. Of those that a mesh axis runs over, the one named last changes fastest.
Arguments:
- tokens: bfloat16 [16384, 1024], P(('dp', 'tensor')), may hold values from -6 to 6
- lengths: int32 [8, 3], P('dp'), may hold values from 1 to 1024, 2048 in all within a row
- first_values: bfloat16 [16384, 1024], P('dp', 'tensor'), may hold values from -6 to 6
- attn_gain: bfloat16 [1024], P(('dp', 'tensor')), may hold values from 0.25 to 1.75
- query_weight: bfloat16 [1024, 1024], P('dp', 'tensor'), may hold values from -0.1875 to 0.1875
- key_weight: bfloat16 [1024, 1024], P('dp', 'tensor'), may hold values from -0.1875 to 0.1875
- value_weight: bfloat16 [1024, 1024], P('dp', 'tensor'), may hold values from -0.1875 to 0.1875
- output_weight: bfloat16 [1024, 1024], P('dp', 'tensor'), may hold values from -1.5 to 1.5
- mlp_gain: bfloat16 [1024], P(('dp', 'tensor')), may hold values from 0.25 to 1.75
- gate_weight: bfloat16 [1024, 2816], P(('dp', 'tensor')), may hold values from -0.1875 to 0.1875
- up_weight: bfloat16 [1024, 2816], P(('dp', 'tensor')), may hold values from -0.1875 to 0.1875
- down_weight: bfloat16 [2816, 1024], P(('dp', 'tensor')), may hold values from -0.109375 to 0.109375
- out_cotangent: bfloat16 [16384, 1024], P(('dp', 'tensor')), may hold values from -6 to 6
Outputs:
- layer_out: bfloat16 [16384, 1024], P(('dp', 'tensor'))
- grad_input: float32 [16384, 1024], P(('dp', 'tensor'))
- grad_first_values: float32 [16384, 1024], P('dp', 'tensor')
- grad_attn_gain: float32 [1024], P(('dp', 'tensor'))
- grad_query: float32 [1024, 1024], P('dp', 'tensor')
- grad_key: float32 [1024, 1024], P('dp', 'tensor')
- grad_value: float32 [1024, 1024], P('dp', 'tensor')
- grad_output: float32 [1024, 1024], P('dp', 'tensor')
- grad_mlp_gain: float32 [1024], P(('dp', 'tensor'))
- grad_gate: float32 [1024, 2816], P(('dp', 'tensor'))
- grad_up: float32 [1024, 2816], P(('dp', 'tensor'))
- grad_down: float32 [2816, 1024], P(('dp', 'tensor'))
Inputs may be any that keep to these rules, and one draw needn't show every extreme that they name: Each row's 3 lengths sum to 2048; the longest of each row is exactly 1024.
All inputs are finite; a program needn't handle non-finite values.
Results may differ from a plain program's by a relative error of at most 0.019.
Values may be sent and summed in bfloat16 or wider, within the bound.
No kernel may reach another device: no remote copies, remote signals or barrier semaphores. Data moves between devices by JAX's collectives and lax.ppermute only.
A program may use at most 192 MiB of HBM per device.

v0:
```python
import jax
import jax.numpy as jnp
from jax import lax
from jax.sharding import PartitionSpec as P

HEAD_DIM = 64


eps = 1e-06
rope_base = 10000.0


def rms_norm(values, gain):
    return values * lax.rsqrt(jnp.mean(values * values, axis=-1, keepdims=True) + eps) * gain


def norm_back(values, gain, upstream):
    inverse = lax.rsqrt(jnp.mean(values * values, axis=-1, keepdims=True) + eps)
    scaled = upstream * gain
    grad_values = (
        inverse * scaled
        - values
        * inverse
        * inverse
        * inverse
        * jnp.sum(scaled * values, axis=-1, keepdims=True)
        / values.shape[-1]
    )
    grad_gain = jnp.sum(upstream * values * inverse, axis=0)
    return (grad_values, grad_gain)


def doc_layout(doc_lengths, total):
    doc_ends = jnp.cumsum(doc_lengths)
    position = jnp.arange(total, dtype=jnp.int32)
    passed = (position[:, None] >= doc_ends[None, :]).astype(jnp.int32)
    segment = jnp.sum(passed, axis=1)
    offsets = jnp.sum(passed * doc_lengths[None, :], axis=1)
    return (segment, position - offsets)


def rope_tables(positions):
    middle = HEAD_DIM // 2
    freqs = rope_base ** (-jnp.arange(middle, dtype=jnp.float32) * 2.0 / HEAD_DIM)
    angles = positions.astype(jnp.float32)[:, None] * freqs[None, :]
    return (jnp.cos(angles), jnp.sin(angles))


def rotate(values, cosine, sine):
    middle = values.shape[-1] // 2
    front_half = values[..., :middle]
    back_half = values[..., middle:]
    cos_b = cosine[:, None, :]
    sin_b = sine[:, None, :]
    return jnp.concatenate(
        [front_half * cos_b - back_half * sin_b, back_half * cos_b + front_half * sin_b], axis=-1
    )


def unrotate(grads, cosine, sine):
    middle = grads.shape[-1] // 2
    front_half = grads[..., :middle]
    back_half = grads[..., middle:]
    cos_b = cosine[:, None, :]
    sin_b = sine[:, None, :]
    return jnp.concatenate(
        [front_half * cos_b + back_half * sin_b, back_half * cos_b - front_half * sin_b], axis=-1
    )


def allowed_mask(segment, offset, block_rows, row_total):
    query_pos = offset + jnp.arange(block_rows, dtype=jnp.int32)
    key_pos = jnp.arange(row_total, dtype=jnp.int32)
    query_seg = lax.dynamic_slice_in_dim(segment, offset, block_rows, 0)
    return (key_pos[None, :] <= query_pos[:, None]) & (segment[None, :] == query_seg[:, None])


def contract_rows(left, right):
    return lax.dot_general(
        left, right, (((0,), (0,)), ((), ())), preferred_element_type=jnp.float32
    )


def contract_cols(left, right):
    return lax.dot_general(
        left, right, (((1,), (1,)), ((), ())), preferred_element_type=jnp.float32
    )


def body(
    tokens,
    lengths,
    first_values,
    attn_gain,
    query_weight,
    key_weight,
    value_weight,
    output_weight,
    mlp_gain,
    gate_weight,
    up_weight,
    down_weight,
    out_cotangent,
):
    local_rows = tokens.shape[0]
    row_total = local_rows * lax.axis_size("tensor")
    columns = query_weight.shape[1]
    heads_here = columns // HEAD_DIM
    block_rows = min(512, row_total)
    num_blocks = row_total // block_rows
    scale = HEAD_DIM ** (-0.5)
    gain_in, gain_mid, gate_full, up_full, down_full = (
        lax.all_gather(attn_gain, ("dp", "tensor"), axis=0, tiled=True),
        lax.all_gather(mlp_gain, ("dp", "tensor"), axis=0, tiled=True),
        lax.all_gather(gate_weight, ("dp", "tensor"), axis=0, tiled=True),
        lax.all_gather(up_weight, ("dp", "tensor"), axis=0, tiled=True),
        lax.all_gather(down_weight, ("dp", "tensor"), axis=0, tiled=True),
    )
    gain_in = gain_in.astype(jnp.float32)
    gain_mid = gain_mid.astype(jnp.float32)
    query_full, key_full, value_full, output_full = (
        lax.all_gather(query_weight, "dp", axis=0, tiled=True),
        lax.all_gather(key_weight, "dp", axis=0, tiled=True),
        lax.all_gather(value_weight, "dp", axis=0, tiled=True),
        lax.all_gather(output_weight, "dp", axis=0, tiled=True),
    )
    joint_weight = jnp.concatenate([query_full, key_full, value_full], axis=1)
    segment, positions = doc_layout(lengths[0], row_total)
    cosine, sine = rope_tables(positions)
    token_f = tokens.astype(jnp.float32)
    normed = rms_norm(token_f, gain_in).astype(jnp.bfloat16)
    normed_full = lax.all_gather(normed, "tensor", axis=0, tiled=True)
    joint = jnp.dot(normed_full, joint_weight, preferred_element_type=jnp.float32)
    query_rot = rotate(
        joint[:, :columns].reshape(row_total, heads_here, HEAD_DIM), cosine, sine
    ).astype(jnp.bfloat16)
    key_rot = rotate(
        joint[:, columns : 2 * columns].reshape(row_total, heads_here, HEAD_DIM), cosine, sine
    ).astype(jnp.bfloat16)
    mixed = (
        (0.5 * joint[:, 2 * columns :] + 0.5 * first_values.astype(jnp.float32))
        .astype(jnp.bfloat16)
        .reshape(row_total, heads_here, HEAD_DIM)
    )

    def forward_block(block_index):
        offset = block_index * block_rows
        query_block = lax.dynamic_slice_in_dim(query_rot, offset, block_rows, 0)
        scores = (
            jnp.einsum("qhd,khd->hqk", query_block, key_rot, preferred_element_type=jnp.float32)
            * scale
        )
        allowed = allowed_mask(segment, offset, block_rows, row_total)
        scores = jnp.where(allowed[None], scores, -1e30)
        peak = jnp.max(scores, axis=-1, keepdims=True)
        expd = jnp.exp(scores - peak)
        totals = jnp.sum(expd, axis=-1, keepdims=True)
        probs = (expd / totals).astype(jnp.bfloat16)
        result = jnp.einsum("hqk,khd->qhd", probs, mixed, preferred_element_type=jnp.float32)
        return (result, (peak + jnp.log(totals))[..., 0])

    attended, log_norm = lax.map(forward_block, jnp.arange(num_blocks, dtype=jnp.int32))
    attended_bf = attended.reshape(row_total, columns).astype(jnp.bfloat16)
    rows = attended_bf
    branch = lax.psum_scatter(
        contract_cols(rows, output_full), "tensor", scatter_dimension=0, tiled=True
    )
    hidden = token_f + branch
    normed_mid = rms_norm(hidden, gain_mid).astype(jnp.bfloat16)
    gate_value = jnp.dot(normed_mid, gate_full, preferred_element_type=jnp.float32)
    up_value = jnp.dot(normed_mid, up_full, preferred_element_type=jnp.float32)
    sigmoid_gate = jax.nn.sigmoid(gate_value)
    activated = gate_value * sigmoid_gate
    inner = (activated * up_value).astype(jnp.bfloat16)
    layer_out = (hidden + jnp.dot(inner, down_full, preferred_element_type=jnp.float32)).astype(
        jnp.bfloat16
    )
    gate_full, up_full, down_full = (
        lax.all_gather(gate_weight, ("dp", "tensor"), axis=0, tiled=True),
        lax.all_gather(up_weight, ("dp", "tensor"), axis=0, tiled=True),
        lax.all_gather(down_weight, ("dp", "tensor"), axis=0, tiled=True),
    )
    grad_down_w = contract_rows(inner, out_cotangent)
    grad_inner = contract_cols(out_cotangent, down_full)
    grad_gate_v = (
        grad_inner * up_value * sigmoid_gate * (1.0 + gate_value * (1.0 - sigmoid_gate))
    ).astype(jnp.bfloat16)
    grad_up_v = (grad_inner * activated).astype(jnp.bfloat16)
    grad_gate_w = contract_rows(normed_mid, grad_gate_v)
    grad_up_w = contract_rows(normed_mid, grad_up_v)
    grad_normed_mid = contract_cols(grad_gate_v, gate_full) + contract_cols(grad_up_v, up_full)
    grad_hidden_norm, grad_gain_mid = norm_back(hidden, gain_mid, grad_normed_mid)
    grad_hidden = out_cotangent.astype(jnp.float32) + grad_hidden_norm
    branch_full = lax.all_gather(grad_hidden.astype(jnp.bfloat16), "tensor", axis=0, tiled=True)
    grad_output_w = contract_rows(branch_full, attended_bf)
    grad_attended = (
        jnp.dot(branch_full, output_full, preferred_element_type=jnp.float32)
        .astype(jnp.bfloat16)
        .reshape(row_total, heads_here, HEAD_DIM)
    )

    def backward_block(carry, block_index):
        grad_key_acc, grad_mixed_acc = carry
        offset = block_index * block_rows
        query_block = lax.dynamic_slice_in_dim(query_rot, offset, block_rows, 0)
        grad_block = lax.dynamic_slice_in_dim(grad_attended, offset, block_rows, 0)
        scores = (
            jnp.einsum("qhd,khd->hqk", query_block, key_rot, preferred_element_type=jnp.float32)
            * scale
        )
        allowed = allowed_mask(segment, offset, block_rows, row_total)
        scores = jnp.where(allowed[None], scores, -1e30)
        probs = jnp.exp(scores - log_norm[block_index][..., None])
        grad_probs = jnp.einsum(
            "qhd,khd->hqk", grad_block, mixed, preferred_element_type=jnp.float32
        )
        grad_scores = (
            probs * (grad_probs - jnp.sum(probs * grad_probs, axis=-1, keepdims=True))
        ).astype(jnp.bfloat16)
        grad_query_block = (
            jnp.einsum("hqk,khd->qhd", grad_scores, key_rot, preferred_element_type=jnp.float32)
            * scale
        )
        grad_key_acc = (
            grad_key_acc
            + jnp.einsum(
                "hqk,qhd->khd", grad_scores, query_block, preferred_element_type=jnp.float32
            )
            * scale
        )
        grad_mixed_acc = grad_mixed_acc + jnp.einsum(
            "hqk,qhd->khd",
            probs.astype(jnp.bfloat16),
            grad_block,
            preferred_element_type=jnp.float32,
        )
        return ((grad_key_acc, grad_mixed_acc), grad_query_block)

    zeros_heads = jnp.zeros((row_total, heads_here, HEAD_DIM), jnp.float32)
    (grad_key_rot, grad_mixed), grad_query_rot = lax.scan(
        backward_block, (zeros_heads, zeros_heads), jnp.arange(num_blocks, dtype=jnp.int32)
    )
    grad_query_v = unrotate(
        grad_query_rot.reshape(row_total, heads_here, HEAD_DIM), cosine, sine
    ).reshape(row_total, columns)
    grad_key_v = unrotate(grad_key_rot, cosine, sine).reshape(row_total, columns)
    grad_first = 0.5 * grad_mixed.reshape(row_total, columns)
    grad_joint = jnp.concatenate([grad_query_v, grad_key_v, grad_first], axis=1).astype(
        jnp.bfloat16
    )
    grad_joint_w = contract_rows(normed_full, grad_joint)
    rows = grad_joint
    grad_normed = lax.psum_scatter(
        contract_cols(rows, joint_weight).astype(jnp.bfloat16),
        "tensor",
        scatter_dimension=0,
        tiled=True,
    ).astype(jnp.float32)
    grad_tokens_norm, grad_gain_in = norm_back(token_f, gain_in, grad_normed)
    grad_tokens = grad_hidden + grad_tokens_norm
    attn_sums = (
        lax.psum_scatter(
            grad_joint_w[:, :columns].astype(jnp.bfloat16), "dp", scatter_dimension=0, tiled=True
        ).astype(jnp.float32),
        lax.psum_scatter(
            grad_joint_w[:, columns : 2 * columns].astype(jnp.bfloat16),
            "dp",
            scatter_dimension=0,
            tiled=True,
        ).astype(jnp.float32),
        lax.psum_scatter(
            grad_joint_w[:, 2 * columns :].astype(jnp.bfloat16),
            "dp",
            scatter_dimension=0,
            tiled=True,
        ).astype(jnp.float32),
        lax.psum_scatter(
            grad_output_w.astype(jnp.bfloat16), "dp", scatter_dimension=0, tiled=True
        ).astype(jnp.float32),
    )
    mlp_sums = (
        lax.psum_scatter(grad_gain_in, ("dp", "tensor"), scatter_dimension=0, tiled=True),
        lax.psum_scatter(grad_gain_mid, ("dp", "tensor"), scatter_dimension=0, tiled=True),
        lax.psum_scatter(grad_gate_w, ("dp", "tensor"), scatter_dimension=0, tiled=True),
        lax.psum_scatter(grad_up_w, ("dp", "tensor"), scatter_dimension=0, tiled=True),
        lax.psum_scatter(grad_down_w, ("dp", "tensor"), scatter_dimension=0, tiled=True),
    )
    return (
        layer_out,
        grad_tokens,
        grad_first,
        mlp_sums[0],
        attn_sums[0],
        attn_sums[1],
        attn_sums[2],
        attn_sums[3],
        mlp_sums[1],
        mlp_sums[2],
        mlp_sums[3],
        mlp_sums[4],
    )


def solution(mesh):
    in_specs = (
        P(("dp", "tensor"), None),
        P("dp", None),
        P("dp", "tensor"),
        P(("dp", "tensor")),
        P("dp", "tensor"),
        P("dp", "tensor"),
        P("dp", "tensor"),
        P("dp", "tensor"),
        P(("dp", "tensor")),
        P(("dp", "tensor"), None),
        P(("dp", "tensor"), None),
        P(("dp", "tensor"), None),
        P(("dp", "tensor"), None),
    )
    out_specs = (
        P(("dp", "tensor"), None),
        P(("dp", "tensor"), None),
        P("dp", "tensor"),
        P(("dp", "tensor")),
        P("dp", "tensor"),
        P("dp", "tensor"),
        P("dp", "tensor"),
        P("dp", "tensor"),
        P(("dp", "tensor")),
        P(("dp", "tensor"), None),
        P(("dp", "tensor"), None),
        P(("dp", "tensor"), None),
    )
    return jax.shard_map(body, mesh=mesh, in_specs=in_specs, out_specs=out_specs, check_vma=False)
```

profile of v0, /device:TPU:11, one launch (start us, length us, event | category | flops | bytes accessed | tf_op | source)
XLA Modules:
  0.0 1704.2 jit_solution(7277528435482366140)
XLA Ops:
  11.4 39.8 %all-reduce.5 = (bf16[1024]{0:T(1024)(128)(2,1)S(1)}, bf16[1024]{0:T(1024)(128)(2,1)}) all-reduce(bf16[1024]{0:T(1024)(128)(2,1)S(1)} %dynamic-update-slice, bf16[1024]{0:T(1024)(128)(2,1)S(1)} %dynamic-update-slice.1), channel_id=1, replica_groups=mesh['dp'=8,'tensor'=4] {'dp','tensor'}, use_global_device_ids=true, to_apply=%add | all-reduce | flops 2048 | bytes 8192
  55.4 15.8 all_gather.38
  71.2 14.8 all_gather.39
  86.1 14.8 all_gather.40
  102.2 15.9 all_gather.41
  119.1 6.1 fusion.57
  128.1 67.8 %while.27 = (s32[]{:T(128)}, bf16[4,512,4,64]{1,3,2,0:T(8,128)(2,1)}, f32[4,4,512]{2,1,0:T(4,128)}, s32[4]{0:T(128)S(1)}, s32[2048]{0:T(1024)S(1)}, /*index=5*/b...) while((s32[]{:T(128)}, ...), condition=%wide.region_7.8_spmd, body=%wide.region_4.7_spmd.sunk | while | flops 1127217664 | bytes 65882372 | solution.py:162
  133.8 4.3 fusion.124
  138.1 6.0 fusion.125
  150.7 4.3 fusion.124
  155.1 6.0 fusion.125
  167.7 4.3 fusion.124
  172.0 6.0 fusion.125
  184.6 4.3 fusion.124
  189.0 6.0 fusion.125
  198.7 4.7 fusion.58
  205.2 97.7 %reduce-scatter.10.cloned.1.call-done = f32[512,1024]{1,0:T(8,128)} async-done(((f32[2048,1024]{1,0:T(8,128)}), f32[512,1024]{1,0:T(8,128)}) %reduce-scatter.10.cloned.1.call-update) | async-done | bytes 2097168 | tf_op jit(solution)/shard_map/reduce_scatter | solution.py:165
  307.4 8.0 fusion.60
  315.4 43.9 %all-gather.8.cloned.1.call-done = bf16[1024,2816]{1,0:T(8,128)(2,1)} async-done(((bf16[32,2816]{1,0:T(8,128)(2,1)}), bf16[1024,2816]{1,0:T(8,128)(2,1)}) %all-gather.8.cloned.1.call-update) | async-done | bytes 5767184 | tf_op jit(solution)/shard_map/all_gather | solution.py:115
  359.3 8.5 fusion.59
  367.9 61.0 %all-gather.12.cloned.1.call-done = bf16[2816,1024]{1,0:T(8,128)(2,1)} async-done(((bf16[88,1024]{1,0:T(8,128)(2,1)}), bf16[2816,1024]{1,0:T(8,128)(2,1)}) %all-gather.12.cloned.1.call-update) | async-done | bytes 5767184 | tf_op jit(solution)/shard_map/all_gather | solution.py:117
  428.8 10.9 multiply_convert_fusion.1
  443.0 6.2 multiply_reduce_fusion.1
  451.8 51.0 %all-gather.14.cloned.1.call-done = bf16[2048,1024]{1,0:T(8,128)(2,1)} async-done(((bf16[512,1024]{1,0:T(8,128)(2,1)}), bf16[2048,1024]{1,0:T(8,128)(2,1)}) %all-gather.14.cloned.1.call-update) | async-done | bytes 4194320 | tf_op jit(solution)/shard_map/all_gather | solution.py:194
  502.8 4.5 convolution_convert_fusion.1
  507.3 244.6 %while.28 = (s32[]{:T(128)}, f32[2048,4,64]{0,2,1:T(8,128)}, f32[2048,4,64]{0,2,1:T(8,128)}, f32[4,512,4,64]{1,0,3,2:T(4,128)}, s32[4]{0:T(128)S(1)}, /*index=5*...) while((s32[]{:T(128)}, f32[2048,4,64]{0,2,1:T(8,128)}, ...), condition=%wide.region_13.14_spmd.clone, body=%wide.region_11.13_spmd.clone.sunk | while | flops 2753165824 | bytes 183118224 | solution.py:240
  512.4 3.5 fusion.135
  516.0 7.2 fusion.138
  523.2 11.6 multiply_reduce_fusion.5
  534.8 11.0 multiply_convert_fusion.6
  545.8 6.2 fusion.139
  552.0 4.0 fusion.137
  556.5 11.1 dynamic_update_slice.19
  576.2 7.6 fusion.138
  583.8 11.6 multiply_reduce_fusion.5
  595.4 11.0 multiply_convert_fusion.6
  606.3 6.2 fusion.139
  612.6 4.7 fusion.137
  617.9 11.1 dynamic_update_slice.19
  637.5 7.6 fusion.138
  645.1 11.6 multiply_reduce_fusion.5
  656.7 11.0 multiply_convert_fusion.6
  667.7 6.2 fusion.139
  673.9 4.7 fusion.137
  679.2 11.1 dynamic_update_slice.19
  698.9 7.6 fusion.138
  706.5 11.6 multiply_reduce_fusion.5
  718.1 11.0 multiply_convert_fusion.6
  729.0 6.2 fusion.139
  735.3 4.7 fusion.137
  740.5 11.1 dynamic_update_slice.19
  754.6 4.3 convolution_convert_fusion.3
  771.4 6.5 convolution_convert_fusion
  779.1 7.8 fusion.64
  788.1 8.0 fusion.63
  796.1 7.8 fusion.62
  805.6 7.7 add_convert_fusion
  819.3 26.7 %reduce-scatter.16.cloned.1.call-done = bf16[128,256]{1,0:T(8,128)(2,1)} async-done(((bf16[1024,256]{1,0:T(8,128)(2,1)}), bf16[128,256]{1,0:T(8,128)(2,1)}) %reduce-scatter.16.cloned.1.call-update) | async-done | bytes 65552 | tf_op jit(solution)/shard_map/reduce_scatter | solution.py:265
  847.5 30.0 %reduce-scatter.18.cloned.1.call-done = bf16[128,256]{1,0:T(8,128)(2,1)} async-done(((bf16[1024,256]{1,0:T(8,128)(2,1)}), bf16[128,256]{1,0:T(8,128)(2,1)}) %reduce-scatter.18.cloned.1.call-update) | async-done | bytes 65552 | tf_op jit(solution)/shard_map/reduce_scatter | solution.py:271
  879.0 59.3 %reduce-scatter.12.cloned.1.call-done = bf16[512,1024]{1,0:T(8,128)(2,1)} async-done(((bf16[2048,1024]{1,0:T(8,128)(2,1)}), bf16[512,1024]{1,0:T(8,128)(2,1)}) %reduce-scatter.12.cloned.1.call-update) | async-done | bytes 1048592 | tf_op jit(solution)/shard_map/reduce_scatter | solution.py:253
  940.4 42.3 %all-reduce.4 = (f32[1024]{0:T(1024)S(1)}, f32[1024]{0:T(1024)S(1)}) all-reduce(f32[1024]{0:T(1024)S(1)} %get-tuple-element.193, f32[1024]{0:T(1024)S(1)} %copy-done.37), channel_id=4, replica_groups=mesh['dp'=8,'tensor'=4] {'dp','tensor'}, use_global_device_ids=true, to_apply=%region_17.18.clone | all-reduce | flops 2048 | bytes 16384
  987.3 203.9 %reduce-scatter.26.cloned.1.call-done = f32[88,1024]{1,0:T(8,128)} async-done(((f32[2816,1024]{1,0:T(8,128)}), f32[88,1024]{1,0:T(8,128)}) %reduce-scatter.26.cloned.1.call-update) | async-done | bytes 360464 | tf_op jit(solution)/shard_map/reduce_scatter | solution.py:286
  1191.2 252.4 %reduce-scatter.24.cloned.1.call-done = f32[32,2816]{1,0:T(8,128)} async-done(((f32[1024,2816]{1,0:T(8,128)}), f32[32,2816]{1,0:T(8,128)}) %reduce-scatter.24.cloned.1.call-update) | async-done | bytes 360464 | tf_op jit(solution)/shard_map/reduce_scatter | solution.py:285
  1443.6 252.9 %reduce-scatter.22.cloned.1.call-done = f32[32,2816]{1,0:T(8,128)} async-done(((f32[1024,2816]{1,0:T(8,128)}), f32[32,2816]{1,0:T(8,128)}) %reduce-scatter.22.cloned.1.call-update) | async-done | bytes 360464 | tf_op jit(solution)/shard_map/reduce_scatter | solution.py:284
  (259 shorter events, 108.1 us)
Async XLA Ops:
  8.0 46.4 %copy-start.39 = (s32[1,3]{1,0:T(1,128)S(1)}, s32[1,3]{1,0:T(1,128)}, u32[]{:S(2)}) copy-start(s32[1,3]{1,0:T(1,128)} %param.18) | copy-start | bytes 40
  8.0 46.5 %copy-start.23 = (bf16[2048,256]{1,0:T(8,128)(2,1)S(1)}, bf16[2048,256]{1,0:T(8,128)(2,1)}, u32[]{:S(2)}) copy-start(bf16[2048,256]{1,0:T(8,128)(2,1)} %param.19) | copy-start | bytes 3145732
  8.0 111.1 %all-gather.6.cloned.1.call-start = ((), (), s32[]{:S(2)}) async-start(), calls=%async_computation.9 | async-start | bytes 5242880 | tf_op jit(solution)/shard_map/all_gather | solution.py:132
  9.7 45.7 %copy-start.31 = (bf16[128,256]{1,0:T(8,128)(2,1)S(1)}, bf16[128,256]{1,0:T(8,128)(2,1)}, u32[]{:S(2)}) copy-start(bf16[128,256]{1,0:T(8,128)(2,1)} %param.21) | copy-start | bytes 196612
  9.7 45.6 %copy-start.35 = (f32[512]{0:T(512)}, f32[512]{0:T(512)S(1)}, u32[]{:S(2)}) copy-start(f32[512]{0:T(512)S(1)} %add_rsqrt_fusion.1) | copy-start | bytes 6148
  54.3 16.9 copy-start.32
  54.3 31.8 %copy-start.33 = (bf16[128,256]{1,0:T(8,128)(2,1)S(1)}, bf16[128,256]{1,0:T(8,128)(2,1)}, u32[]{:S(2)}) copy-start(bf16[128,256]{1,0:T(8,128)(2,1)} %param.23) | copy-start | bytes 196612
  54.3 248.6 %reduce-scatter.10.cloned.1.call-start = ((), (), s32[]{:S(2)}) async-start(), calls=%async_computation.10 | async-start | bytes 10485760 | tf_op jit(solution)/shard_map/reduce_scatter | solution.py:165
  55.2 47.0 %copy-start.34 = (bf16[128,256]{1,0:T(8,128)(2,1)S(1)}, bf16[128,256]{1,0:T(8,128)(2,1)}, u32[]{:S(2)}) copy-start(bf16[128,256]{1,0:T(8,128)(2,1)} %param.24) | copy-start | bytes 196612
  119.1 8.2 copy-start.13
  119.1 8.2 copy-start.15
  133.7 4.3 copy-start.26
  150.7 4.3 copy-start.26
  167.7 4.3 copy-start.26
  184.6 4.3 copy-start.26
  196.0 7.4 copy-start.5
  196.0 2.7 copy-start.17
  198.7 4.7 copy-start.11
  203.4 1.8 copy-start.38
  203.4 99.6 %copy-start.3 = (bf16[512,1024]{1,0:T(8,128)(2,1)S(1)}, bf16[512,1024]{1,0:T(8,128)(2,1)}, u32[]{:S(2)}) copy-start(bf16[512,1024]{1,0:T(8,128)(2,1)} %param.17) | copy-start | bytes 3145732
  203.4 103.1 %all-gather.10.cloned.1.call-start = ((), (), s32[]{:S(2)}) async-start(), calls=%async_computation.12 | async-start | bytes 5947392 | tf_op jit(solution)/shard_map/all_gather | solution.py:116
  204.0 155.3 %all-gather.8.cloned.1.call-start = ((), (), s32[]{:S(2)}) async-start(), calls=%async_computation.11 | async-start | bytes 5947392 | tf_op jit(solution)/shard_map/all_gather | solution.py:115
  204.6 224.3 %all-gather.12.cloned.1.call-start = ((), (), s32[]{:S(2)}) async-start(), calls=%async_computation.13 | async-start | bytes 5947392 | tf_op jit(solution)/shard_map/all_gather | solution.py:117
  205.2 297.6 %all-gather.14.cloned.1.call-start = ((), (), s32[]{:S(2)}) async-start(), calls=%async_computation.14 | async-start | bytes 5242880 | tf_op jit(solution)/shard_map/all_gather | solution.py:194
  315.4 113.4 %copy-start.21 = (bf16[512,1024]{1,0:T(8,128)(2,1)S(1)}, bf16[512,1024]{1,0:T(8,128)(2,1)}, u32[]{:S(2)}) copy-start(bf16[512,1024]{1,0:T(8,128)(2,1)} %param.29) | copy-start | bytes 3145732
  428.8 10.9 copy-start.40
  439.8 3.2 copy-start.42
  439.8 3.2 copy-start.43
  439.8 3.2 copy-start.7
  449.2 53.6 %copy-start.18 = (bf16[1024,256]{1,0:T(8,128)(2,1)S(1)}, bf16[1024,256]{1,0:T(8,128)(2,1)}, u32[]{:S(2)}) copy-start(bf16[1024,256]{1,0:T(8,128)(2,1)} %all_gather.41) | copy-start | bytes 1572868
  451.7 364.6 %reduce-scatter.20.cloned.1.call-start = ((), (), s32[]{:S(2)}) async-start(), calls=%async_computation.19 | async-start | bytes 589824 | tf_op jit(solution)/shard_map/reduce_scatter | solution.py:277
  507.4 4.0 copy-start.19
  512.4 3.6 copy-start.1
  545.8 6.2 copy-start
  552.0 15.7 copy-start.20
  567.6 4.0 copy-start.19
  572.6 3.6 copy-start.1
  606.3 6.2 copy-start
  612.6 16.4 copy-start.20
  629.0 4.0 copy-start.19
  634.0 3.6 copy-start.1
  667.7 6.2 copy-start
  673.9 16.4 copy-start.20
  690.3 4.0 copy-start.19
  695.3 3.6 copy-start.1
  729.0 6.2 copy-start
  735.2 16.4 copy-start.20
  751.8 2.8 copy-start.12
  759.0 58.9 %reduce-scatter.14.cloned.1.call-start = ((), (), s32[]{:S(2)}) async-start(), calls=%async_computation.16 | async-start | bytes 589824 | tf_op jit(solution)/shard_map/reduce_scatter | solution.py:262
  759.0 3.3 copy-start.2
  759.0 3.3 copy-start.14
  759.0 3.3 copy-start.16
  763.1 2.2 copy-start.41
  770.0 76.0 %reduce-scatter.16.cloned.1.call-start = ((), (), s32[]{:S(2)}) async-start(), calls=%async_computation.17 | async-start | bytes 589824 | tf_op jit(solution)/shard_map/reduce_scatter | solution.py:265
  770.6 106.9 %reduce-scatter.18.cloned.1.call-start = ((), (), s32[]{:S(2)}) async-start(), calls=%async_computation.18 | async-start | bytes 589824 | tf_op jit(solution)/shard_map/reduce_scatter | solution.py:271
  771.3 167.0 %reduce-scatter.12.cloned.1.call-start = ((), (), s32[]{:S(2)}) async-start(), calls=%async_computation.15 | async-start | bytes 5242880 | tf_op jit(solution)/shard_map/reduce_scatter | solution.py:253
  777.9 413.3 %reduce-scatter.26.cloned.1.call-start = ((), (), s32[]{:S(2)}) async-start(), calls=%async_computation.22 | async-start | bytes 11894784 | tf_op jit(solution)/shard_map/reduce_scatter | solution.py:286
  786.9 656.7 %reduce-scatter.24.cloned.1.call-start = ((), (), s32[]{:S(2)}) async-start(), calls=%async_computation.21 | async-start | bytes 11894784 | tf_op jit(solution)/shard_map/reduce_scatter | solution.py:285
  796.1 900.4 %reduce-scatter.22.cloned.1.call-start = ((), (), s32[]{:S(2)}) async-start(), calls=%async_computation.20 | async-start | bytes 11894784 | tf_op jit(solution)/shard_map/reduce_scatter | solution.py:284
  813.3 125.1 %copy-start.4 = (bf16[512,1024]{1,0:T(8,128)(2,1)S(1)}, bf16[512,1024]{1,0:T(8,128)(2,1)}, u32[]{:S(2)}) copy-start(bf16[512,1024]{1,0:T(8,128)(2,1)} %param.17) | copy-start | bytes 3145732
  813.3 125.1 %copy-start.30 = (f32[1024]{0:T(1024)S(1)}, f32[1024]{0:T(1024)}, u32[]{:S(2)}) copy-start(f32[1024]{0:T(1024)} %copy-done.29) | copy-start | bytes 12292
  813.3 125.1 %copy-start.36 = (f32[512]{0:T(512)S(1)}, f32[512]{0:T(512)}, u32[]{:S(2)}) copy-start(f32[512]{0:T(512)} %copy-done.35) | copy-start | bytes 6148
  813.3 127.2 %copy-start.37 = (f32[1024]{0:T(1024)S(1)}, f32[1024]{0:T(1024)}, u32[]{:S(2)}) copy-start(f32[1024]{0:T(1024)} %get-tuple-element.191) | copy-start | bytes 12292
  813.3 170.7 %copy-start.10 = (f32[512,1024]{1,0:T(8,128)S(1)}, f32[512,1024]{1,0:T(8,128)}, u32[]{:S(2)}) copy-start(f32[512,1024]{1,0:T(8,128)} %get-tuple-element.240) | copy-start | bytes 6291460
  (12 other events, 13.3 us)
Sparse Core Ops, SparseCore 0:
  54.4 53.4 all-gather.5
  203.5 99.3 reduce-scatter.9
  451.8 50.9 all-gather.13
  759.1 24.1 reduce-scatter.19
  785.4 29.1 reduce-scatter.13
  816.8 29.1 reduce-scatter.15
  848.3 29.1 reduce-scatter.17
  880.7 57.5 reduce-scatter.11
  941.2 249.8 reduce-scatter.25
  1193.9 249.6 reduce-scatter.23
  1446.5 249.9 reduce-scatter.21
Sparse Core Ops, SparseCore 1:
  207.2 82.6 all-gather.9
  293.0 66.3 all-gather.7
  362.5 66.3 all-gather.11
where the time goes:
time: 1710 us; the launch traced here: 1700 us
  waiting for transfers between devices  1080 us (63%)
  matrix products  268 us (16%)
  blocking collectives  143 us (8%)
  other arithmetic  99.1 us (6%)
  local copies, waits for them, and re-layouts  80.7 us (5%)
    reduce_scatter x1, waiting for transfers between devices, body(): lax.psum_scatter(grad_gate_w, ('dp', 'tensor'), scatter_dimension=0, tile...  253 us
    reduce_scatter x1, waiting for transfers between devices, body(): lax.psum_scatter(grad_up_w, ('dp', 'tensor'), scatter_dimension=0, tiled=...  252 us
    reduce_scatter x1, waiting for transfers between devices, body(): lax.psum_scatter(grad_down_w, ('dp', 'tensor'), scatter_dimension=0, tile...  204 us
    reduce_scatter x1, waiting for transfers between devices, body(): lax.psum_scatter(contract_cols(rows, output_full), 'tensor', scatter_dime...  97.7 us
    unnamed x2, blocking collectives  82.1 us
    all_gather x1, waiting for transfers between devices, body(): lax.all_gather(down_weight, ('dp', 'tensor'), axis=0, tiled=True)  61 us
    reduce_scatter x1, waiting for transfers between devices, body(): lax.psum_scatter(contract_cols(rows, joint_weight).astype(jnp.bfloat16),...  59.3 us
    all_gather x1, waiting for transfers between devices, body(): lax.all_gather(grad_hidden.astype(jnp.bfloat16), 'tensor', axis=0, tiled=...  51 us
  transfers between devices with their start and end apart: 14, of which 10 were waited for; matrix products, arithmetic and copies ran while one was open for 5% of the time, Pallas kernels for 0%

commit v1 on v0

v1 whole, which is shorter than its diff:
```python
import functools

import jax
import jax.numpy as jnp
from jax import lax
from jax.experimental import pallas as pl
from jax.experimental.pallas import tpu as pltpu
from jax.sharding import PartitionSpec as P

HEAD_DIM = 64
HALF = HEAD_DIM // 2
BLOCK = 256
VMEM_LIMIT = 60 * 1024 * 1024

eps = 1e-06
rope_base = 10000.0
bf16 = jnp.bfloat16
f32 = jnp.float32

NN = (((1,), (0,)), ((), ()))
NT = (((1,), (1,)), ((), ()))
TN = (((0,), (0,)), ((), ()))


def mm(left, right, dims=NN):
    return lax.dot_general(left, right, dims, preferred_element_type=f32)


def swap_tensor(value, mask):
    size = lax.axis_size("tensor")
    return lax.ppermute(value, "tensor", [(i, i ^ mask) for i in range(size)])


def swap_core(value):
    size = lax.axis_size("dp")
    return lax.ppermute(value, "dp", [(i, i ^ 1) for i in range(size)])


def shift_z(value, step):
    size = lax.axis_size("dp")
    return lax.ppermute(value, "dp", [(i, (i + 2 * step) % size) for i in range(size)])


def bit_orders():
    bits = [1 << b for b in range(lax.axis_size("tensor").bit_length() - 1)]
    return bits, bits[1:] + bits[:1]


def gather_tensor(value, bits):
    have = {0: value}
    for bit in bits:
        have.update({mask ^ bit: swap_tensor(piece, bit) for mask, piece in list(have.items())})
    return have


def scatter_tensor(parts, bits):
    parts = dict(parts)
    for bit in bits:
        for mask in [m for m in parts if not m & bit]:
            got = swap_tensor(parts.pop(mask | bit), bit)
            parts[mask] = (parts[mask].astype(f32) + got.astype(f32)).astype(bf16)
    return parts[0]


def gather_z(value):
    depth = lax.axis_size("dp") // 2
    here = lax.axis_index("dp") // 2
    buffer = jnp.zeros((depth,) + value.shape, value.dtype)
    for step in range(depth):
        piece = value if step == 0 else shift_z(value, step)
        buffer = lax.dynamic_update_index_in_dim(buffer, piece, (here - step) % depth, 0)
    return buffer


def scatter_z(value):
    depth = value.shape[0]
    here = lax.axis_index("dp") // 2
    take = lambda step: lax.dynamic_index_in_dim(value, (here + step) % depth, 0, False)
    total = take(0).astype(f32)
    for step in range(1, depth):
        total = total + shift_z(take(step), step).astype(f32)
    return total


def attend_forward_kernel(
    heads, lo_ref, full_ref, x_ref, w_ref, fv_ref, cos_ref, sin_ref, start_ref,
    qt_ref, kt_ref, kn_ref, vn_ref, ot_ref, o_ref, lse_ref, wt, vt, acc,
):
    cols = heads * HEAD_DIM
    blocks = x_ref.shape[0] // BLOCK
    wt[...] = w_ref[...].T

    def project(i, carry):
        at = pl.ds(pl.multiple_of(i * BLOCK, BLOCK), BLOCK)
        joint = mm(wt[...], x_ref[at, :], NT)
        cosine, sine = cos_ref[:, at], sin_ref[:, at]
        first = fv_ref[at, :].astype(f32).T
        for h in range(heads):
            lo, mid, hi = h * HEAD_DIM, h * HEAD_DIM + HALF, (h + 1) * HEAD_DIM
            qa, qb = joint[lo:mid], joint[mid:hi]
            q = jnp.concatenate([qa * cosine - qb * sine, qb * cosine + qa * sine], axis=0)
            qt_ref[lo:hi, at] = (q * HEAD_DIM ** (-0.5)).astype(bf16)
            ka, kb = joint[cols + lo : cols + mid], joint[cols + mid : cols + hi]
            k = jnp.concatenate([ka * cosine - kb * sine, kb * cosine + ka * sine], axis=0)
            kt_ref[lo:hi, at] = k.astype(bf16)
            kn_ref[h, at, :] = k.T.astype(bf16)
            v = 0.5 * joint[2 * cols + lo : 2 * cols + hi] + 0.5 * first[lo:hi]
            vt[lo:hi, at] = v.astype(bf16)
            vn_ref[h, at, :] = v.T.astype(bf16)
        return carry

    lax.fori_loop(0, blocks, project, 0)

    def query_block(i, carry):
        qs = pl.ds(pl.multiple_of(i * BLOCK, BLOCK), BLOCK)
        start = start_ref[:, qs]
        key_iota = lax.broadcasted_iota(jnp.int32, (BLOCK, BLOCK), 0)
        query_pos = lax.broadcasted_iota(jnp.int32, (BLOCK, BLOCK), 1) + i * BLOCK

        def tile(j, state, masked, opening):
            ks = pl.ds(pl.multiple_of(j * BLOCK, BLOCK), BLOCK)
            if masked:
                key_pos = key_iota + j * BLOCK
                allowed = (key_pos <= query_pos) & (key_pos >= start)
            result = []
            for h in range(heads):
                rows = slice(h * HEAD_DIM, (h + 1) * HEAD_DIM)
                scores = mm(kn_ref[h, ks, :], qt_ref[rows, qs])
                if masked:
                    scores = jnp.where(allowed, scores, -1e30)
                peak = jnp.max(scores, axis=0, keepdims=True)
                if not opening:
                    old_peak, old_total = state[h]
                    peak = jnp.maximum(old_peak, peak)
                    shrink = jnp.exp(old_peak - peak)
                probs = jnp.exp(scores - peak)
                total = jnp.sum(probs, axis=0, keepdims=True)
                out = mm(vt[rows, ks], probs.astype(bf16))
                if not opening:
                    total = total + old_total * shrink
                    out = out + acc[rows, :] * shrink
                acc[rows, :] = out
                result.append((peak, total))
            return tuple(result)

        lo, full = lo_ref[i], full_ref[i]
        state = tile(i, None, True, True)
        state = lax.fori_loop(full, i, lambda j, s: tile(j, s, False, False), state)
        state = lax.fori_loop(lo, full, lambda j, s: tile(j, s, True, False), state)
        for h in range(heads):
            rows = slice(h * HEAD_DIM, (h + 1) * HEAD_DIM)
            peak, total = state[h]
            acc[rows, :] = acc[rows, :] * (1.0 / total)
            lse_ref[h : h + 1, qs] = peak + jnp.log(total)
        out = acc[...]
        ot_ref[:, qs] = out.astype(bf16)
        o_ref[qs, :] = out.T.astype(bf16)
        return carry

    lax.fori_loop(0, blocks, query_block, 0)


def attend_backward_kernel(
    heads, lo_ref, full_ref, qt_ref, kt_ref, kn_ref, vn_ref, ot_ref, lse_ref, do_ref,
    cos_ref, sin_ref, start_ref, w_ref, gj_ref, gn_ref, gf_ref, dot_, delta, dq, dk, dv,
):
    cols = heads * HEAD_DIM
    blocks = do_ref.shape[0] // BLOCK
    dk[...] = jnp.zeros_like(dk)
    dv[...] = jnp.zeros_like(dv)

    def prepare(i, carry):
        at = pl.ds(pl.multiple_of(i * BLOCK, BLOCK), BLOCK)
        grads = do_ref[at, :].astype(f32).T
        dot_[:, at] = grads.astype(bf16)
        prod = grads * ot_ref[:, at].astype(f32)
        for h in range(heads):
            delta[h : h + 1, at] = jnp.sum(
                prod[h * HEAD_DIM : (h + 1) * HEAD_DIM], axis=0, keepdims=True
            )
        return carry

    lax.fori_loop(0, blocks, prepare, 0)

    def query_block(step, carry):
        i = blocks - 1 - step
        qs = pl.ds(pl.multiple_of(i * BLOCK, BLOCK), BLOCK)
        start = start_ref[:, qs]
        key_iota = lax.broadcasted_iota(jnp.int32, (BLOCK, BLOCK), 0)
        query_pos = lax.broadcasted_iota(jnp.int32, (BLOCK, BLOCK), 1) + i * BLOCK
        dq[...] = jnp.zeros_like(dq)

        def tile(j, carry, masked):
            ks = pl.ds(pl.multiple_of(j * BLOCK, BLOCK), BLOCK)
            if masked:
                key_pos = key_iota + j * BLOCK
                allowed = (key_pos <= query_pos) & (key_pos >= start)
            for h in range(heads):
                rows = slice(h * HEAD_DIM, (h + 1) * HEAD_DIM)
                q_h, do_h = qt_ref[rows, qs], dot_[rows, qs]
                scores = mm(kn_ref[h, ks, :], q_h)
                if masked:
                    scores = jnp.where(allowed, scores, -1e30)
                probs = jnp.exp(scores - lse_ref[h : h + 1, qs])
                grad_probs = mm(vn_ref[h, ks, :], do_h)
                grad_scores = (probs * (grad_probs - delta[h : h + 1, qs])).astype(bf16)
                dv[rows, ks] += mm(do_h, probs.astype(bf16), NT)
                dk[rows, ks] += mm(q_h, grad_scores, NT)
                dq[rows, :] += mm(kt_ref[rows, ks], grad_scores)
            return carry

        lo, full = lo_ref[i], full_ref[i]
        tile(i, 0, True)
        lax.fori_loop(full, i, lambda j, s: tile(j, s, False), 0)
        lax.fori_loop(lo, full, lambda j, s: tile(j, s, True), 0)

        cosine, sine = cos_ref[:, qs], sin_ref[:, qs]
        pieces = []
        for source, factor in ((dq, HEAD_DIM ** (-0.5)), (dk, 1.0)):
            for h in range(heads):
                lo_row, mid, hi = h * HEAD_DIM, h * HEAD_DIM + HALF, (h + 1) * HEAD_DIM
                where = slice(None) if source is dq else qs
                a, b = source[lo_row:mid, where] * factor, source[mid:hi, where] * factor
                pieces += [a * cosine + b * sine, b * cosine - a * sine]
        half_v = 0.5 * dv[:, qs]
        gf_ref[qs, :] = half_v.T
        grads = jnp.concatenate(pieces + [half_v], axis=0).T.astype(bf16)
        gj_ref[qs, :] = grads
        gn_ref[qs, :] = mm(grads, w_ref[...], NT).astype(bf16)
        return carry

    lax.fori_loop(0, blocks, query_block, 0)


def feed_forward_kernel(
    n_z, n_t, place_ref, xa_ref, xb_ref, ga_ref, gb_ref, wd_ref, *rest
):
    pieces = rest[: 2 * n_t]
    inner_ref, gvu_ref, u_ref, w, sems = rest[2 * n_t :]
    half_z = n_z // 2
    z, t = place_ref[0], place_ref[1]
    copies = []
    for part in range(2):
        for mask in range(n_t):
            for r in range(half_z):
                copy = pltpu.make_async_copy(
                    pieces[part * n_t + mask].at[r],
                    w.at[part * half_z + r, :, jnp.bitwise_xor(t, mask)],
                    sems.at[(part * n_t + mask) * half_z + r],
                )
                copy.start()
                copies.append(copy)
    for copy in copies:
        copy.wait()
    features = xa_ref.shape[1]
    ff = wd_ref.shape[0]
    tokens = xa_ref.shape[0]
    step = 256
    edges = list(range(0, ff, step)) + [ff]

    def weight(lo, hi):
        return w[:, :, :, :, lo:hi].reshape(features, hi - lo)

    for source, (x_ref, g_ref) in enumerate(((xa_ref, ga_ref), (xb_ref, gb_ref))):

        def rows_step(i, carry, x_ref=x_ref, g_ref=g_ref, source=source):
            rows = pl.ds(pl.multiple_of(i * step, step), step)
            outs = pl.ds(pl.multiple_of(source * tokens + i * step, step), step)
            x, g = x_ref[rows, :], g_ref[rows, :]
            for lo, hi in zip(edges[:-1], edges[1:]):
                gate = mm(x, weight(lo, hi))
                up = mm(x, weight(ff + lo, ff + hi))
                grad_inner = mm(g, wd_ref[lo:hi, :], NT)
                sig = jax.nn.sigmoid(gate)
                act = gate * sig
                inner_ref[outs, lo:hi] = (act * up).astype(bf16)
                gvu_ref[outs, lo:hi] = (
                    grad_inner * up * (sig * (1.0 + gate * (1.0 - sig)))
                ).astype(bf16)
                gvu_ref[outs, ff + lo : ff + hi] = (grad_inner * act).astype(bf16)
            u_ref[outs, :] = mm(gvu_ref[outs, :], weight(0, 2 * ff), NT)
            return carry

        lax.fori_loop(0, tokens // step, rows_step, 0)


def vmem(n):
    return [pl.BlockSpec(memory_space=pltpu.VMEM)] * n


def smem(n):
    return [pl.BlockSpec(memory_space=pltpu.SMEM)] * n


def params():
    return pltpu.CompilerParams(vmem_limit_bytes=VMEM_LIMIT)


def attend_forward(heads, lo, full, x, w, fv, cosine, sine, start):
    rows, cols = x.shape[0], heads * HEAD_DIM
    sds = jax.ShapeDtypeStruct
    return pl.pallas_call(
        functools.partial(attend_forward_kernel, heads),
        out_shape=(
            sds((cols, rows), bf16),
            sds((cols, rows), bf16),
            sds((heads, rows, HEAD_DIM), bf16),
            sds((heads, rows, HEAD_DIM), bf16),
            sds((cols, rows), bf16),
            sds((rows, cols), bf16),
            sds((heads, rows), f32),
        ),
        in_specs=smem(2) + vmem(6),
        out_specs=tuple(vmem(7)),
        scratch_shapes=[
            pltpu.VMEM((3 * cols, x.shape[1]), bf16),
            pltpu.VMEM((cols, rows), bf16),
            pltpu.VMEM((cols, BLOCK), f32),
        ],
        compiler_params=params(),
        cost_estimate=pl.CostEstimate(
            flops=30_000_000_000, bytes_accessed=20_000_000, transcendentals=0
        ),
        name="attend_forward",
    )(lo, full, x, w, fv, cosine, sine, start)


def attend_backward(heads, lo, full, saved, grads, cosine, sine, start, w):
    rows, cols = grads.shape[0], heads * HEAD_DIM
    sds = jax.ShapeDtypeStruct
    qt, kt, kn, vn, ot, lse = saved
    return pl.pallas_call(
        functools.partial(attend_backward_kernel, heads),
        out_shape=(
            sds((rows, 3 * cols), bf16),
            sds((rows, w.shape[0]), bf16),
            sds((rows, cols), f32),
        ),
        in_specs=smem(2) + vmem(11),
        out_specs=tuple(vmem(3)),
        scratch_shapes=[
            pltpu.VMEM((cols, rows), bf16),
            pltpu.VMEM((heads, rows), f32),
            pltpu.VMEM((cols, BLOCK), f32),
            pltpu.VMEM((cols, rows), f32),
            pltpu.VMEM((cols, rows), f32),
        ],
        compiler_params=params(),
        cost_estimate=pl.CostEstimate(
            flops=60_000_000_000, bytes_accessed=20_000_000, transcendentals=0
        ),
        name="attend_backward",
    )(lo, full, qt, kt, kn, vn, ot, lse, grads, cosine, sine, start, w)


def feed_forward(n_z, n_t, place, xa, xb, ga, gb, wd, pieces):
    tokens, features = xa.shape
    ff = wd.shape[0]
    sds = jax.ShapeDtypeStruct
    own_rows = pieces[0].shape[2]
    return pl.pallas_call(
        functools.partial(feed_forward_kernel, n_z, n_t),
        out_shape=(
            sds((2 * tokens, ff), bf16),
            sds((2 * tokens, 2 * ff), bf16),
            sds((2 * tokens, features), f32),
        ),
        in_specs=smem(1) + vmem(5) + [pl.BlockSpec(memory_space=pl.ANY)] * len(pieces),
        out_specs=tuple(vmem(3)),
        scratch_shapes=[
            pltpu.VMEM((n_z, 2, n_t, own_rows, 2 * ff), bf16),
            pltpu.SemaphoreType.DMA((n_z * n_t,)),
        ],
        compiler_params=params(),
        cost_estimate=pl.CostEstimate(
            flops=16_000_000_000, bytes_accessed=30_000_000, transcendentals=0
        ),
        name="feed_forward",
    )(place, xa, xb, ga, gb, wd, *pieces)


def doc_layout(doc_lengths, total):
    doc_ends = jnp.cumsum(doc_lengths)
    index = jnp.arange(total, dtype=jnp.int32)
    passed = (index[:, None] >= doc_ends[None, :]).astype(jnp.int32)
    return jnp.sum(passed * doc_lengths[None, :], axis=1)


def split_cols(weight, n_z):
    rows = weight.shape[0]
    return weight.reshape(rows, n_z, 2, -1).transpose(2, 0, 1, 3).reshape(2, rows, -1)


def join_cols(parts, n_z):
    rows = parts.shape[1]
    return parts.reshape(2, rows, n_z, -1).transpose(1, 2, 0, 3).reshape(rows, -1)


def body(
    tokens, lengths, first_values, attn_gain, query_weight, key_weight, value_weight,
    output_weight, mlp_gain, gate_weight, up_weight, down_weight, out_cotangent,
):
    n_t = lax.axis_size("tensor")
    n_dp = lax.axis_size("dp")
    n_z = n_dp // 2
    t = lax.axis_index("tensor")
    core = lax.axis_index("dp") % 2
    z = lax.axis_index("dp") // 2
    masks = range(n_t)
    bits_a, bits_b = bit_orders()
    count, features = tokens.shape
    rows = count * n_t
    cols = query_weight.shape[1]
    heads = cols // HEAD_DIM
    half = count // 2
    ff_core = gate_weight.shape[1] // 2

    def token_slice(value, mask, offset, size):
        return lax.dynamic_slice_in_dim(value, (t ^ mask) * count + offset, size, 0)

    token_f = tokens.astype(f32)
    inverse_in = lax.rsqrt(jnp.mean(token_f * token_f, axis=-1, keepdims=True) + eps)
    unit_in = (token_f * inverse_in).astype(bf16)
    x_full = jnp.zeros((rows, features), bf16)
    for offset, bits in ((0, bits_a), (half, bits_b)):
        for mask, piece in gather_tensor(unit_in[offset : offset + half], bits).items():
            x_full = lax.dynamic_update_slice_in_dim(
                x_full, piece, (t ^ mask) * count + offset, 0
            )

    own_gain = attn_gain.astype(f32)[None]
    row_index = lax.broadcasted_iota(jnp.int32, (n_t, own_gain.shape[1]), 0)
    gain_rows = jnp.zeros((n_t, own_gain.shape[1]), f32)
    for mask in masks:
        piece = swap_tensor(own_gain, mask) if mask else own_gain
        gain_rows = jnp.where(row_index == t ^ mask, piece, gain_rows)
    gain_rows = gain_rows.reshape(-1, 1)

    own_joint = jnp.concatenate([query_weight, key_weight, value_weight], axis=1).astype(f32)
    near = gather_z((own_joint * gain_rows).astype(bf16))
    far = swap_core(near)
    joint_weight = jnp.where(
        core == 0, jnp.stack([near, far], axis=1), jnp.stack([far, near], axis=1)
    ).reshape(features, 3 * cols)

    start = doc_layout(lengths[0], rows)
    position = (jnp.arange(rows, dtype=jnp.int32) - start).astype(f32)
    freqs = rope_base ** (-jnp.arange(HALF, dtype=f32) * 2.0 / HEAD_DIM)
    angles = freqs[:, None] * position[None, :]
    cosine, sine = jnp.cos(angles), jnp.sin(angles)
    block_starts = start.reshape(-1, BLOCK)
    lo = block_starts[:, 0] // BLOCK
    full = jnp.minimum(
        (block_starts[:, -1] + BLOCK - 1) // BLOCK,
        jnp.arange(rows // BLOCK, dtype=jnp.int32),
    )
    start = start[None]

    qt, kt, kn, vn, ot, attended, lse = attend_forward(
        heads, lo, full, x_full, joint_weight, first_values, cosine, sine, start
    )

    gain_mid = mlp_gain.astype(f32)[:, None]
    gate_parts = split_cols(gate_weight, n_z)
    up_parts = split_cols(up_weight, n_z)
    both = jnp.concatenate([gate_parts, up_parts], axis=2).astype(f32)
    both = (both * gain_mid[None]).astype(bf16)
    mine = lax.dynamic_index_in_dim(both, core, 0, False)
    theirs = swap_core(lax.dynamic_index_in_dim(both, 1 - core, 0, False))
    pair = jnp.where(core == 0, jnp.stack([mine, theirs]), jnp.stack([theirs, mine]))
    column = gather_z(pair)
    half_z = n_z // 2
    gathered = []
    for offset, bits in ((0, bits_a), (half_z, bits_b)):
        pieces = gather_tensor(column[offset : offset + half_z], bits)
        gathered += [pieces[mask] for mask in masks]

    down_column = gather_z(down_weight)
    down = jnp.zeros((n_z, n_t) + down_weight.shape, bf16)
    for offset, bits in ((0, bits_b), (half_z, bits_a)):
        for mask, piece in gather_tensor(down_column[offset : offset + half_z], bits).items():
            down = lax.dynamic_update_slice(
                down, piece[:, None], (offset, t ^ mask, 0, 0)
            )
    down = down.reshape(ff_core, features)

    out_column = gather_z(output_weight)
    out_parts = [{}, {}]
    for part, (offset, bits) in enumerate(((0, bits_a), (half_z, bits_b))):
        out_parts[part] = gather_tensor(out_column[offset : offset + half_z], bits)
    out_near = jnp.concatenate(
        [jnp.concatenate([out_parts[p][mask] for p in range(2)], axis=0) for mask in masks],
        axis=-1,
    )
    out_far = swap_core(out_near)
    out_weight = jnp.where(
        core == 0, jnp.stack([out_near, out_far], axis=1), jnp.stack([out_far, out_near], axis=1)
    ).reshape(features, n_t * cols)

    att = jnp.concatenate(
        [token_slice(attended, 0, 0, count)]
        + [swap_tensor(token_slice(attended, m, 0, count), m) for m in masks if m],
        axis=1,
    )
    hidden = token_f + mm(att, out_weight, NT)
    inverse_mid = lax.rsqrt(jnp.mean(hidden * hidden, axis=-1, keepdims=True) + eps)
    unit_mid = (hidden * inverse_mid).astype(bf16)

    unit_far = swap_core(unit_mid)
    grad_far = swap_core(out_cotangent)
    place = jnp.stack([z, t]).astype(jnp.int32)
    inner, gvu, u_part = feed_forward(
        n_z, n_t, place, unit_mid, unit_far, out_cotangent, grad_far, down, gathered
    )
    u = u_part[:count] + swap_core(u_part[count:].astype(bf16)).astype(f32)
    cotangent = out_cotangent.astype(f32)
    grad_hidden = (
        cotangent
        + inverse_mid * u
        - hidden
        * (inverse_mid ** 3 * jnp.sum(u * hidden, axis=-1, keepdims=True) / features)
    )
    grad_branch = grad_hidden.astype(bf16)
    grad_att = mm(grad_branch, out_weight).astype(bf16)
    grad_attended = jnp.zeros((rows, cols), bf16)
    for mask in masks:
        piece = grad_att[:, mask * cols : (mask + 1) * cols]
        piece = swap_tensor(piece, mask) if mask else piece
        grad_attended = lax.dynamic_update_slice_in_dim(
            grad_attended, piece, (t ^ mask) * count, 0
        )

    grad_joint, grad_unit, grad_first = attend_backward(
        heads, lo, full, (qt, kt, kn, vn, ot, lse), grad_attended, cosine, sine, start,
        joint_weight,
    )

    out_part = mm(inner, down)
    layer_out = (
        hidden + out_part[:count] + swap_core(out_part[count:].astype(bf16)).astype(f32)
    ).astype(bf16)

    unit_both = jnp.concatenate([unit_mid, unit_far], axis=0)
    grad_both = jnp.concatenate([out_cotangent, grad_far], axis=0)
    grad_gu = mm(unit_both, gvu, TN).astype(bf16).reshape(n_z, 2, n_t, -1, 2 * ff_core)
    grad_dn = mm(inner, grad_both, TN).astype(bf16).reshape(n_z, n_t, -1, features)

    def over_tensor(pick, orders):
        parts = []
        for offset, bits in zip((0, half_z), orders):
            parts.append(scatter_tensor({m: pick(m, offset) for m in masks}, bits))
        return jnp.concatenate(parts, axis=0)

    gu = over_tensor(
        lambda m, offset: lax.dynamic_index_in_dim(
            grad_gu[offset : offset + half_z], t ^ m, 2, False
        ),
        (bits_a, bits_b),
    )
    gu = scatter_z(gu)
    gu_mine = lax.dynamic_index_in_dim(gu, core, 0, False)
    gu_far = swap_core(lax.dynamic_index_in_dim(gu, 1 - core, 0, False))
    gu = jnp.where(core == 0, jnp.stack([gu_mine, gu_far]), jnp.stack([gu_far, gu_mine]))
    grad_gate = join_cols(gu[:, :, :ff_core], n_z)
    grad_up = join_cols(gu[:, :, ff_core:], n_z)
    grad_mlp_gain = jnp.sum(
        grad_gate * gate_weight.astype(f32) + grad_up * up_weight.astype(f32), axis=1
    )
    grad_gate = grad_gate * gain_mid
    grad_up = grad_up * gain_mid

    dn = over_tensor(
        lambda m, offset: lax.dynamic_index_in_dim(
            grad_dn[offset : offset + half_z], t ^ m, 1, False
        ),
        (bits_b, bits_a),
    )
    grad_down = scatter_z(dn)

    grad_ow = mm(grad_branch, att, TN).astype(bf16).reshape(n_z, 2, -1, n_t * cols)
    keep = lax.dynamic_index_in_dim(grad_ow, core, 1, False)
    give = lax.dynamic_index_in_dim(grad_ow, 1 - core, 1, False)
    grad_ow = (keep.astype(f32) + swap_core(give).astype(f32)).astype(bf16)
    ow = over_tensor(
        lambda m, offset: grad_ow[offset : offset + half_z, :, m * cols : (m + 1) * cols],
        (bits_a, bits_b),
    )
    grad_output = scatter_z(ow)

    u_halves = []
    for offset, bits in ((0, bits_a), (half, bits_b)):
        parts = {m: token_slice(grad_unit, m, offset, half) for m in masks}
        u_halves.append(scatter_tensor(parts, bits).astype(f32))
    u_in = jnp.concatenate(u_halves, axis=0)
    grad_input = (
        grad_hidden
        + inverse_in * u_in
        - token_f
        * (inverse_in ** 3 * jnp.sum(u_in * token_f, axis=-1, keepdims=True) / features)
    )

    grad_jw = mm(x_full, grad_joint, TN).astype(bf16).reshape(n_z, 2, -1, 3 * cols)
    keep = lax.dynamic_index_in_dim(grad_jw, core, 1, False)
    give = lax.dynamic_index_in_dim(grad_jw, 1 - core, 1, False)
    grad_jw = scatter_z((keep.astype(f32) + swap_core(give).astype(f32)).astype(bf16))
    gain_part = jnp.sum(grad_jw * own_joint, axis=1).reshape(n_t, -1)
    grad_attn_gain = lax.dynamic_index_in_dim(gain_part, t, 0, True)
    for mask in masks:
        if mask:
            grad_attn_gain = grad_attn_gain + swap_tensor(
                lax.dynamic_index_in_dim(gain_part, t ^ mask, 0, True), mask
            )
    grad_jw = grad_jw * gain_rows

    return (
        layer_out,
        grad_input,
        grad_first,
        grad_attn_gain[0],
        grad_jw[:, :cols],
        grad_jw[:, cols : 2 * cols],
        grad_jw[:, 2 * cols :],
        grad_output,
        grad_mlp_gain,
        grad_gate,
        grad_up,
        grad_down,
    )


def solution(mesh):
    both = ("dp", "tensor")
    in_specs = (
        P(both, None),
        P("dp", None),
        P("dp", "tensor"),
        P(both),
        P("dp", "tensor"),
        P("dp", "tensor"),
        P("dp", "tensor"),
        P("dp", "tensor"),
        P(both),
        P(both, None),
        P(both, None),
        P(both, None),
        P(both, None),
    )
    out_specs = (
        P(both, None),
        P(both, None),
        P("dp", "tensor"),
        P(both),
        P("dp", "tensor"),
        P("dp", "tensor"),
        P("dp", "tensor"),
        P("dp", "tensor"),
        P(both),
        P(both, None),
        P(both, None),
        P(both, None),
    )
    return jax.shard_map(body, mesh=mesh, in_specs=in_specs, out_specs=out_specs, check_vma=False)
```

time: 1710 us -> 553 us (0.32)
  waiting for transfers between devices: 1080 us -> 199 us
  matrix products: 268 us -> 28 us
  blocking collectives: 143 us -> 0 us
  starting transfers between devices: 0.57 us -> 111 us
  Pallas kernels: 0 us -> 100 us
  other arithmetic: 99.1 us -> 47.2 us
  local copies, waits for them, and re-layouts: 80.7 us -> 55.2 us
    reduce_scatter x9 -> x0, waiting for transfers between devices: 923 us -> none  [the longest x1 253 us: body(): lax.psum_scatter(grad_gate_w, ('dp', 'tensor'), scatter_dimension=0, tile...]
    dot_general x43 -> x7, matrix products: 268 us -> 28 us  [mm(): return lax.dot_general(left, right, dims, preferred_element_type=f32)]
    ppermute x0 -> x94, waiting for transfers between devices: none -> 199 us  [the longest x60 140 us: swap_tensor(): return lax.ppermute(value, 'tensor', [(i, i ^ mask) for i in range(size)])]
    all_gather x5 -> x0, waiting for transfers between devices: 156 us -> none  [the longest x1 61 us: body(): lax.all_gather(down_weight, ('dp', 'tensor'), axis=0, tiled=True)]
    ppermute x0 -> x94, starting transfers between devices: none -> 111 us  [the longest x60 51.5 us: swap_tensor(): return lax.ppermute(value, 'tensor', [(i, i ^ mask) for i in range(size)])]
    pallas_call x0 -> x3, Pallas kernels: none -> 100 us  [the longest x1 38 us: attend_forward(): pl.pallas_call(functools.partial(attend_forward_kernel, heads), out_shape...]
    unnamed x2 -> x0, blocking collectives: 82.1 us -> none
    all_gather x4 -> x0, blocking collectives: 61.4 us -> none  [the longest x1 15.9 us: body(): lax.all_gather(output_weight, 'dp', axis=0, tiled=True)]
  transfers between devices with their start and end apart: 14 -> 94, of which waited for: 10 -> 31; matrix products, arithmetic and copies ran while one was open for 5% -> 20% of each run, Pallas kernels for 0% -> 14%
where the time goes in v1:
time: 553 us; the launch traced here: 543 us
  waiting for transfers between devices  199 us (36%)
  starting transfers between devices  111 us (20%)
  Pallas kernels  100 us (18%)
  local copies, waits for them, and re-layouts  55.2 us (10%)
  other arithmetic  47.2 us (9%)
  matrix products  28 us (5%)
    ppermute x60, waiting for transfers between devices, swap_tensor(): return lax.ppermute(value, 'tensor', [(i, i ^ mask) for i in range(size)])  140 us
    ppermute x24, waiting for transfers between devices, shift_z(): lax.ppermute(value, 'dp', [(i, (i + 2 * step) % size) for i in range(size)])  58.5 us
    ppermute x60, starting transfers between devices, swap_tensor(): return lax.ppermute(value, 'tensor', [(i, i ^ mask) for i in range(size)])  51.5 us
    ppermute x24, starting transfers between devices, shift_z(): lax.ppermute(value, 'dp', [(i, (i + 2 * step) % size) for i in range(size)])  38 us
    pallas_call x1, Pallas kernels, attend_forward(): pl.pallas_call(functools.partial(attend_forward_kernel, heads), out_shape...  38 us
    pallas_call x1, Pallas kernels, attend_backward(): pl.pallas_call(functools.partial(attend_backward_kernel, heads), out_shap...  36.2 us
    dot_general x7, matrix products, mm(): return lax.dot_general(left, right, dims, preferred_element_type=f32)  28 us
    pallas_call x1, Pallas kernels, feed_forward(): pl.pallas_call(functools.partial(feed_forward_kernel, n_z, n_t), out_shap...  25.9 us
  transfers between devices with their start and end apart: 94, of which 31 were waited for; matrix products, arithmetic and copies ran while one was open for 20% of the time, Pallas kernels for 14%

profile of v1, /device:TPU:11, one launch (start us, length us, event | category | flops | bytes accessed | tf_op | source)
XLA Modules:
  0.0 543.0 jit_solution(31242716297801223)
XLA Ops:
  3.1 1.4 collective-permute-start.30
  10.4 1.5 fusion.2
  17.1 2.4 multiply_sine_fusion
  20.2 2.5 broadcast_in_dim.138
  26.8 1.8 collective-permute-start.17
  34.0 2.0 collective-permute-done.18
  36.0 3.0 collective-permute-start.37
  41.0 2.6 collective-permute-start.10
  48.7 2.0 broadcast_in_dim.157
  52.7 4.4 collective-permute-done.10
  58.3 3.0 collective-permute-done.19
  65.3 10.6 %collective-permute-done.21 = bf16[2,128,256]{2,1,0:T(8,128)(2,1)S(1)} collective-permute-done((bf16[2,128,256]{2,1,0:T(8,128)(2,1)S(1)}, bf16[2,128,256]{2,1,0:T(8,128)(2,1)S(1)}, u32[]{:S(2)}, u32[]{:S(2)}) %collective-permute-start.21) | collective-permute-done | bytes 131104 | tf_op jit(solution)/shard_map/ppermute | solution.py:31
  77.1 1.6 collective-permute-done.23
  82.1 3.1 collective-permute-start.39
  86.1 2.0 collective-permute-start.40
  90.1 18.8 %collective-permute-done.39 = bf16[2,32,2816]{2,1,0:T(8,128)(2,1)S(1)} collective-permute-done((bf16[2,32,2816]{2,1,0:T(8,128)(2,1)S(1)}, bf16[2,32,2816]{2,1,0:T(8,128)(2,1)S(1)}, u32[]{:S(2)}, u32[]{:S(2)}) %collective-permute-start.39) | collective-permute-done | bytes 360480 | tf_op jit(solution)/shard_map/ppermute | solution.py:41
  108.9 4.2 collective-permute-start.12
  113.1 2.1 collective-permute-done.40
  118.4 1.7 bitcast_dynamic-update-slice_fusion.5
  122.2 6.1 %collective-permute-done.2 = bf16[256,1024]{1,0:T(8,128)(2,1)S(1)} collective-permute-done((bf16[256,1024]{1,0:T(8,128)(2,1)S(1)}, bf16[256,1024]{1,0:T(8,128)(2,1)S(1)}, u32[]{:S(2)}, u32[]{:S(2)}) %collective-permute-start.2) | collective-permute-done | bytes 524320 | tf_op jit(solution)/shard_map/ppermute | solution.py:31
  132.2 8.4 %collective-permute-done.5 = bf16[256,1024]{1,0:T(8,128)(2,1)S(1)} collective-permute-done((bf16[256,1024]{1,0:T(8,128)(2,1)S(1)}, bf16[256,1024]{1,0:T(8,128)(2,1)S(1)}, u32[]{:S(2)}, u32[]{:S(2)}) %collective-permute-start.5) | collective-permute-done | bytes 524320 | tf_op jit(solution)/shard_map/ppermute | solution.py:31
  141.4 38.0 %attend_forward.1 = (bf16[256,2048]{1,0:T(8,128)(2,1)}, bf16[256,2048]{1,0:T(8,128)(2,1)}, bf16[4,2048,64]{2,1,0:T(8,128)(2,1)}, bf16[4,2048,64]{2,1,0:T(8,128)(...) custom-call(s32[8]{0:T(128)} %get-tuple-element.118.lo_ref, ...), custom_call_target="tpu_custom_call" | custom-call | flops 30000001024 | bytes 20000000 | tf_op jit(solution)/shard_map/attend_forward/pallas_call | solution.py:302
  184.7 1.9 maximum_select_fusion
  189.0 4.0 collective-permute-done.15
  194.9 4.9 collective-permute-done.34
  202.6 20.3 %collective-permute-done.33 = bf16[2,88,1024]{2,1,0:T(8,128)(2,1)S(1)} collective-permute-done((bf16[2,88,1024]{2,1,0:T(8,128)(2,1)}, bf16[2,88,1024]{2,1,0:T(8,128)(2,1)S(1)}, u32[]{:S(2)}, u32[]{:S(2)}) %collective-permute-start.33) | collective-permute-done | bytes 360480 | tf_op jit(solution)/shard_map/ppermute | solution.py:31
  223.0 3.1 collective-permute-start.26
  232.9 12.5 %collective-permute-done.42.rest_2_ = bf16[2,2,32,2816]{3,2,1,0:T(8,128)(2,1)S(1)} collective-permute-done((bf16[2,2,32,2816]{3,2,1,0:T(8,128)(2,1)S(1)}, bf16[2,2,32,2816]{3,2,1,0:T(8,128)(2,1)S(1)}, u32[]{:S(2)}, u32[]{:S(2)}) %collective-permute-start.42) | collective-permute-done | bytes 720928 | tf_op jit(solution)/shard_map/ppermute | solution.py:31
  246.3 14.5 %collective-permute-done.43.rest_3_ = bf16[2,2,32,2816]{3,2,1,0:T(8,128)(2,1)S(1)} collective-permute-done((bf16[2,2,32,2816]{3,2,1,0:T(8,128)(2,1)S(1)}, bf16[2,2,32,2816]{3,2,1,0:T(8,128)(2,1)S(1)}, u32[]{:S(2)}, u32[]{:S(2)}) %collective-permute-start.43) | collective-permute-done | bytes 720928 | tf_op jit(solution)/shard_map/ppermute | solution.py:31
  263.6 25.9 %feed_forward.1 = (bf16[1024,1408]{1,0:T(8,128)(2,1)}, bf16[1024,2816]{1,0:T(8,128)(2,1)}, f32[1024,1024]{1,0:T(8,128)}) custom-call(s32[2]{0:T(128)} %pad_add_fusion.place_ref, bf16[512,1024]{1,0:T(8,128)(2,1)} %copy-done.12, bf16[512,1024]{1,0:T(8,128)(2,1)} %copy-done.46, bf16[512,1024]{1,0:T(8,128)(2,1)} %ga_ref.1, ...), custom_call_target="tpu_custom_call" | custom-call | flops 16000000000 | bytes 30000000 | tf_op jit(solution)/shard_map/feed_forward/pallas_call | solution.py:361
  289.5 6.2 %fusion.84 = f32[1024,1024]{1,0:T(8,128)S(1)} fusion(bf16[1024,1408]{1,0:T(8,128)(2,1)} %get-tuple-element.26, bf16[1408,1024]{1,0:T(8,128)(2,1)} %bitcast.45.wd_ref), kind=kOutput, calls=%fused_computation.267 | convolution fusion | flops 2952790016 | bytes 9961472 | tf_op jit(solution)/shard_map/dot_general | solution.py:26
  295.8 4.8 convolution_convert_fusion.1
  304.8 7.1 %convolution_convert_fusion = bf16[1024,2816]{1,0:T(8,128)(2,1)S(1)} fusion(bf16[1024,2816]{1,0:T(8,128)(2,1)S(1)} %bitcast.268, bf16[512,1024]{1,0:T(8,128)(2,1)S(1)} %copy-done.47, bf16[512,1024]{1,0:T(8,128)(2,1)S(1)} %copy-done.13), kind=kOutput, calls=%fused_computation | convolution fusion | flops 5912657920 | bytes 13631488 | tf_op jit(solution)/shard_map/dot_general | solution.py:26
  319.5 23.0 %collective-permute-done.90 = bf16[2,88,1024]{2,1,0:T(8,128)(2,1)S(1)} collective-permute-done((bf16[2,88,1024]{2,1,0:T(8,128)(2,1)S(1)}, bf16[2,88,1024]{2,1,0:T(8,128)(2,1)S(1)}, u32[]{:S(2)}, u32[]{:S(2)}) %collective-permute-start.90) | collective-permute-done | bytes 360480 | tf_op jit(solution)/shard_map/ppermute | solution.py:31
  342.5 2.6 collective-permute-start.47
  345.8 2.0 collective-permute-start.91
  352.1 10.8 %collective-permute-done.92 = bf16[88,1024]{1,0:T(8,128)(2,1)S(1)} collective-permute-done((bf16[88,1024]{1,0:T(8,128)(2,1)S(1)}, bf16[88,1024]{1,0:T(8,128)(2,1)S(1)}, u32[]{:S(2)}, u32[]{:S(2)}) %collective-permute-start.92) | collective-permute-done | bytes 180256 | tf_op jit(solution)/shard_map/ppermute | solution.py:41
  365.4 3.1 multiply_subtract_fusion
  372.7 1.6 collective-permute-start.51
  377.1 7.9 %collective-permute-done.49 = bf16[512,256]{1,0:T(8,128)(2,1)S(1)} collective-permute-done((bf16[512,256]{1,0:T(8,128)(2,1)S(1)}, bf16[512,256]{1,0:T(8,128)(2,1)S(1)}, u32[]{:S(2)}, u32[]{:S(2)}) %collective-permute-start.49) | collective-permute-done | bytes 262176 | tf_op jit(solution)/shard_map/ppermute | solution.py:31
  387.9 3.0 collective-permute-done.51
  390.8 4.1 collective-permute-start.65
  395.7 36.2 %attend_backward.1 = (bf16[2048,768]{1,0:T(8,128)(2,1)}, bf16[2048,1024]{1,0:T(8,128)(2,1)}, f32[2048,256]{1,0:T(8,128)}) custom-call(s32[8]{0:T(128)} %get-tuple-element.118.lo_ref, s32[8]{0:T(128)} %get-tuple-element.119.full_ref, bf16[256,2048]{1,0:T(8,128)(2,1)} %get-tuple-element.28.qt_ref, bf16[256,2048]{1,0:T(8,128)(2,1)} %get-tuple-element.29.kt_ref, ...), custom_call_target="tpu_custom_call" | custom-call | flops 60000002048 | bytes 20000000 | tf_op jit(solution)/shard_map/attend_backward/pallas_call | solution.py:332
  431.9 1.8 add_convert_fusion
  433.8 2.0 add_convert_fusion.1
  436.7 7.2 %collective-permute-start.82 = (bf16[2,32,2816]{2,1,0:T(8,128)(2,1)S(1)}, bf16[2,32,2816]{2,1,0:T(8,128)(2,1)S(1)}, u32[]{:S(2)}, u32[]{:S(2)}) collective-permute-start(bf16[2,32,2816]{2,1,0:T(8,128)(2,1)S(1)} %get-tuple-element.61), channel_id=1, source_target_pairs={{0,16},{4,20},{8,24},{12,28},{16,0},{20,4},{24,8},{28,12},{1,17},{... | collective-permute-start | bytes 1081352 | tf_op jit(solution)/shard_map/ppermute | solution.py:41
  443.9 1.4 collective-permute-start.83
  445.2 5.9 %convolution_convert_fusion.3 = bf16[1024,768]{1,0:T(8,128)(2,1)S(1)} fusion(bf16[2048,1024]{1,0:T(8,128)(2,1)} %constant_dynamic-update-slice_fusion.3.x_ref, bf16[2048,768]{1,0:T(8,128)(2,1)S(1)} %copy-done.61), kind=kOutput, calls=%fused_computation.41 | convolution fusion | flops 3222011904 | bytes 8912896 | tf_op jit(solution)/shard_map/dot_general | solution.py:26
  453.4 14.2 %collective-permute-done.82 = bf16[2,32,2816]{2,1,0:T(8,128)(2,1)S(1)} collective-permute-done((bf16[2,32,2816]{2,1,0:T(8,128)(2,1)S(1)}, bf16[2,32,2816]{2,1,0:T(8,128)(2,1)S(1)}, u32[]{:S(2)}, u32[]{:S(2)}) %collective-permute-start.82) | collective-permute-done | bytes 360480 | tf_op jit(solution)/shard_map/ppermute | solution.py:41
  470.8 3.6 collective-permute-start.84
  477.8 5.1 collective-permute-start.59
  486.2 2.2 reshape.383
  490.7 1.4 reshape.385
  492.2 2.7 broadcast_multiply_fusion.1
  496.2 1.6 add_convert_fusion.11
  499.2 1.8 collective-permute-done.61
  504.6 8.9 %collective-permute-done.69 = bf16[2,128,256]{2,1,0:T(8,128)(2,1)} collective-permute-done((bf16[2,128,256]{2,1,0:T(8,128)(2,1)}, bf16[2,128,256]{2,1,0:T(8,128)(2,1)}, u32[]{:S(2)}, u32[]{:S(2)}) %collective-permute-start.69) | collective-permute-done | bytes 131104 | tf_op jit(solution)/shard_map/ppermute | solution.py:31
  518.1 2.0 add_convert_fusion.5
  520.1 1.7 collective-permute-start.64
  521.8 6.5 %collective-permute-done.68 = bf16[2,128,256]{2,1,0:T(8,128)(2,1)S(1)} collective-permute-done((bf16[2,128,256]{2,1,0:T(8,128)(2,1)S(1)}, bf16[2,128,256]{2,1,0:T(8,128)(2,1)S(1)}, u32[]{:S(2)}, u32[]{:S(2)}) %collective-permute-start.68) | collective-permute-done | bytes 131104 | tf_op jit(solution)/shard_map/ppermute | solution.py:31
  529.6 3.3 collective-permute-start.73
  533.4 1.8 collective-permute-done.73
  537.0 1.9 collective-permute-done.57
  540.7 1.8 fusion.1
  (402 shorter events, 139.1 us)
Async XLA Ops:
  0.7 38.4 %collective-permute-start.28 = (bf16[88,1024]{1,0:T(8,128)(2,1)}, bf16[88,1024]{1,0:T(8,128)(2,1)}, u32[]{:S(2)}, u32[]{:S(2)}) collective-permute-start(bf16[88,1024]{1,0:T(8,128)(2,1)} %param.24), channel_id=1, source_target_pairs={{0,8},{4,12},{8,16},{12,20},{16,24},{20,28},{24,0},{28,4},{1,9},{5... | collective-permute-start | bytes 540680 | tf_op jit(solution)/shard_map/ppermute | solution.py:41
  2.0 39.0 %collective-permute-start.29 = (bf16[88,1024]{1,0:T(8,128)(2,1)}, bf16[88,1024]{1,0:T(8,128)(2,1)}, u32[]{:S(2)}, u32[]{:S(2)}) collective-permute-start(bf16[88,1024]{1,0:T(8,128)(2,1)} %param.24), channel_id=1, source_target_pairs={{0,16},{4,20},{8,24},{12,28},{16,0},{20,4},{24,8},{28,12},{1,17},{... | collective-permute-start | bytes 540680 | tf_op jit(solution)/shard_map/ppermute | solution.py:41
  3.1 41.4 %collective-permute-start.30 = (bf16[88,1024]{1,0:T(8,128)(2,1)}, bf16[88,1024]{1,0:T(8,128)(2,1)}, u32[]{:S(2)}, u32[]{:S(2)}) collective-permute-start(bf16[88,1024]{1,0:T(8,128)(2,1)} %param.24), channel_id=1, source_target_pairs={{0,24},{4,28},{8,0},{12,4},{16,8},{20,12},{24,16},{28,20},{1,25},{... | collective-permute-start | bytes 540680 | tf_op jit(solution)/shard_map/ppermute | solution.py:41
  5.7 18.5 %collective-permute-start.6 = (f32[1,32]{1,0:T(1,128)}, f32[1,32]{1,0:T(1,128)}, u32[]{:S(2)}, u32[]{:S(2)}) collective-permute-start(f32[1,32]{1,0:T(1,128)} %get-tuple-element.114), channel_id=1, source_target_pairs={{0,3},{1,2},{2,1},{3,0},{4,7},{5,6},{6,5},{7,4},{8,11},{9,10},{10,... | collective-permute-start | bytes 392 | tf_op jit(solution)/shard_map/ppermute | solution.py:31
  6.9 18.6 %collective-permute-start.7 = (f32[1,32]{1,0:T(1,128)}, f32[1,32]{1,0:T(1,128)}, u32[]{:S(2)}, u32[]{:S(2)}) collective-permute-start(f32[1,32]{1,0:T(1,128)} %get-tuple-element.114), channel_id=1, source_target_pairs={{0,2},{1,3},{2,0},{3,1},{4,6},{5,7},{6,4},{7,5},{8,10},{9,11},{10,... | collective-permute-start | bytes 392 | tf_op jit(solution)/shard_map/ppermute | solution.py:31
  32.7 49.4 %collective-permute-start = (bf16[256,1024]{1,0:T(8,128)(2,1)}, bf16[256,1024]{1,0:T(8,128)(2,1)S(1)}, u32[]{:S(2)}, u32[]{:S(2)}) collective-permute-start(bf16[256,1024]{1,0:T(8,128)(2,1)} %get-tuple-element.83), channel_id=1, source_target_pairs={{0,1},{1,0},{2,3},{3,2},{4,5},{5,4},{6,7},{7,6},{8,9},{9,8},{10,11... | collective-permute-start | bytes 1572872 | tf_op jit(solution)/shard_map/ppermute | solution.py:31
  41.0 16.0 %collective-permute-start.10 = (bf16[128,768]{1,0:T(8,128)(2,1)S(1)}, bf16[128,768]{1,0:T(8,128)(2,1)S(1)}, u32[]{:S(2)}, u32[]{:S(2)}) collective-permute-start(bf16[128,768]{1,0:T(8,128)(2,1)S(1)} %fusion.27), channel_id=1, source_target_pairs={{0,16},{4,20},{8,24},{12,28},{16,0},{20,4},{24,8},{28,12},{1,17},{... | collective-permute-start | bytes 589832 | tf_op jit(solution)/shard_map/ppermute | solution.py:41
  44.5 19.5 %collective-permute-start.11 = (bf16[128,768]{1,0:T(8,128)(2,1)S(1)}, bf16[128,768]{1,0:T(8,128)(2,1)S(1)}, u32[]{:S(2)}, u32[]{:S(2)}) collective-permute-start(bf16[128,768]{1,0:T(8,128)(2,1)S(1)} %fusion.27), channel_id=1, source_target_pairs={{0,24},{4,28},{8,0},{12,4},{16,8},{20,12},{24,16},{28,20},{1,25},{... | collective-permute-start | bytes 589832 | tf_op jit(solution)/shard_map/ppermute | solution.py:41
  47.2 15.3 %collective-permute-start.22 = (bf16[2,128,256]{2,1,0:T(8,128)(2,1)S(1)}, bf16[2,128,256]{2,1,0:T(8,128)(2,1)S(1)}, u32[]{:S(2)}, u32[]{:S(2)}) collective-permute-start(bf16[2,128,256]{2,1,0:T(8,128)(2,1)S(1)} %get-tuple-element.108), channel_id=1, source_target_pairs={{0,2},{1,3},{2,0},{3,1},{4,6},{5,7},{6,4},{7,5},{8,10},{9,11},{10,... | collective-permute-start | bytes 393224 | tf_op jit(solution)/shard_map/ppermute | solution.py:31
  61.3 24.8 %collective-permute-start.1 = (bf16[256,1024]{1,0:T(8,128)(2,1)S(1)}, bf16[256,1024]{1,0:T(8,128)(2,1)S(1)}, u32[]{:S(2)}, u32[]{:S(2)}) collective-permute-start(bf16[256,1024]{1,0:T(8,128)(2,1)S(1)} %copy-done.24), channel_id=1, source_target_pairs={{0,2},{1,3},{2,0},{3,1},{4,6},{5,7},{6,4},{7,5},{8,10},{9,11},{10,... | collective-permute-start | bytes 1572872 | tf_op jit(solution)/shard_map/ppermute | solution.py:31
  62.6 13.3 %collective-permute-start.21 = (bf16[2,128,256]{2,1,0:T(8,128)(2,1)S(1)}, bf16[2,128,256]{2,1,0:T(8,128)(2,1)S(1)}, u32[]{:S(2)}, u32[]{:S(2)}) collective-permute-start(bf16[2,128,256]{2,1,0:T(8,128)(2,1)S(1)} %get-tuple-element.107), channel_id=1, source_target_pairs={{0,2},{1,3},{2,0},{3,1},{4,6},{5,7},{6,4},{7,5},{8,10},{9,11},{10,... | collective-permute-start | bytes 393224 | tf_op jit(solution)/shard_map/ppermute | solution.py:31
  62.8 15.9 %collective-permute-start.23 = (bf16[2,128,256]{2,1,0:T(8,128)(2,1)S(1)}, bf16[2,128,256]{2,1,0:T(8,128)(2,1)S(1)}, u32[]{:S(2)}, u32[]{:S(2)}) collective-permute-start(bf16[2,128,256]{2,1,0:T(8,128)(2,1)S(1)} %collective-permute-done.19), channel_id=1, source_target_pairs={{0,2},{1,3},{2,0},{3,1},{4,6},{5,7},{6,4},{7,5},{8,10},{9,11},{10,... | collective-permute-start | bytes 393224 | tf_op jit(solution)/shard_map/ppermute | solution.py:31
  64.0 15.9 %collective-permute-start.24 = (bf16[2,128,256]{2,1,0:T(8,128)(2,1)S(1)}, bf16[2,128,256]{2,1,0:T(8,128)(2,1)S(1)}, u32[]{:S(2)}, u32[]{:S(2)}) collective-permute-start(bf16[2,128,256]{2,1,0:T(8,128)(2,1)S(1)} %collective-permute-done.22), channel_id=1, source_target_pairs={{0,1},{1,0},{2,3},{3,2},{4,5},{5,4},{6,7},{7,6},{8,9},{9,8},{10,11... | collective-permute-start | bytes 393224 | tf_op jit(solution)/shard_map/ppermute | solution.py:31
  75.9 46.1 %collective-permute-start.3 = (bf16[256,1024]{1,0:T(8,128)(2,1)S(1)}, bf16[256,1024]{1,0:T(8,128)(2,1)S(1)}, u32[]{:S(2)}, u32[]{:S(2)}) collective-permute-start(bf16[256,1024]{1,0:T(8,128)(2,1)S(1)} %copy-done.23), channel_id=1, source_target_pairs={{0,2},{1,3},{2,0},{3,1},{4,6},{5,7},{6,4},{7,5},{8,10},{9,11},{10,... | collective-permute-start | bytes 1572872 | tf_op jit(solution)/shard_map/ppermute | solution.py:31
  78.7 52.6 %collective-permute-start.4 = (bf16[256,1024]{1,0:T(8,128)(2,1)S(1)}, bf16[256,1024]{1,0:T(8,128)(2,1)S(1)}, u32[]{:S(2)}, u32[]{:S(2)}) collective-permute-start(bf16[256,1024]{1,0:T(8,128)(2,1)S(1)} %copy-done.23), channel_id=1, source_target_pairs={{0,1},{1,0},{2,3},{3,2},{4,5},{5,4},{6,7},{7,6},{8,9},{9,8},{10,11... | collective-permute-start | bytes 1572872 | tf_op jit(solution)/shard_map/ppermute | solution.py:31
  82.1 26.8 %collective-permute-start.39 = (bf16[2,32,2816]{2,1,0:T(8,128)(2,1)S(1)}, bf16[2,32,2816]{2,1,0:T(8,128)(2,1)S(1)}, u32[]{:S(2)}, u32[]{:S(2)}) collective-permute-start(bf16[2,32,2816]{2,1,0:T(8,128)(2,1)S(1)} %maximum_select_fusion.4), channel_id=1, source_target_pairs={{0,16},{4,20},{8,24},{12,28},{16,0},{20,4},{24,8},{28,12},{1,17},{... | collective-permute-start | bytes 1081352 | tf_op jit(solution)/shard_map/ppermute | solution.py:41
  86.1 29.2 %collective-permute-start.40 = (bf16[2,32,2816]{2,1,0:T(8,128)(2,1)S(1)}, bf16[2,32,2816]{2,1,0:T(8,128)(2,1)S(1)}, u32[]{:S(2)}, u32[]{:S(2)}) collective-permute-start(bf16[2,32,2816]{2,1,0:T(8,128)(2,1)S(1)} %maximum_select_fusion.4), channel_id=1, source_target_pairs={{0,24},{4,28},{8,0},{12,4},{16,8},{20,12},{24,16},{28,20},{1,25},{... | collective-permute-start | bytes 1081352 | tf_op jit(solution)/shard_map/ppermute | solution.py:41
  88.9 28.8 %collective-permute-start.31 = (bf16[2,88,1024]{2,1,0:T(8,128)(2,1)S(1)}, bf16[2,88,1024]{2,1,0:T(8,128)(2,1)}, u32[]{:S(2)}, u32[]{:S(2)}) collective-permute-start(bf16[2,88,1024]{2,1,0:T(8,128)(2,1)S(1)} %get-tuple-element.95), channel_id=1, source_target_pairs={{0,2},{1,3},{2,0},{3,1},{4,6},{5,7},{6,4},{7,5},{8,10},{9,11},{10,... | collective-permute-start | bytes 1081352 | tf_op jit(solution)/shard_map/ppermute | solution.py:31
  115.2 13.1 %collective-permute-start.2 = (bf16[256,1024]{1,0:T(8,128)(2,1)S(1)}, bf16[256,1024]{1,0:T(8,128)(2,1)S(1)}, u32[]{:S(2)}, u32[]{:S(2)}) collective-permute-start(bf16[256,1024]{1,0:T(8,128)(2,1)S(1)} %collective-permute-done), channel_id=1, source_target_pairs={{0,2},{1,3},{2,0},{3,1},{4,6},{5,7},{6,4},{7,5},{8,10},{9,11},{10,... | collective-permute-start | bytes 1572872 | tf_op jit(solution)/shard_map/ppermute | solution.py:31
  117.7 111.1 %collective-permute-start.27 = (bf16[512,1024]{1,0:T(8,128)(2,1)}, bf16[512,1024]{1,0:T(8,128)(2,1)}, u32[]{:S(2)}, u32[]{:S(2)}) collective-permute-start(bf16[512,1024]{1,0:T(8,128)(2,1)} %ga_ref.1), channel_id=1, source_target_pairs={{0,4},{4,0},{8,12},{12,8},{16,20},{20,16},{24,28},{28,24},{1,5},{5... | collective-permute-start | bytes 3145736 | tf_op jit(solution)/shard_map/ppermute | solution.py:36
  120.1 62.3 %collective-permute-start.32 = (bf16[2,88,1024]{2,1,0:T(8,128)(2,1)S(1)}, bf16[2,88,1024]{2,1,0:T(8,128)(2,1)S(1)}, u32[]{:S(2)}, u32[]{:S(2)}) collective-permute-start(bf16[2,88,1024]{2,1,0:T(8,128)(2,1)S(1)} %get-tuple-element.95), channel_id=1, source_target_pairs={{0,1},{1,0},{2,3},{3,2},{4,5},{5,4},{6,7},{7,6},{8,9},{9,8},{10,11... | collective-permute-start | bytes 1081352 | tf_op jit(solution)/shard_map/ppermute | solution.py:31
  121.9 62.3 %collective-permute-start.25 = (bf16[4,128,1024]{2,1,0:T(8,128)(2,1)}, bf16[4,128,1024]{2,1,0:T(8,128)(2,1)}, u32[]{:S(2)}, u32[]{:S(2)}) collective-permute-start(bf16[4,128,1024]{2,1,0:T(8,128)(2,1)} %maximum_maximum_fusion), channel_id=1, source_target_pairs={{0,4},{4,0},{8,12},{12,8},{16,20},{20,16},{24,28},{28,24},{1,5},{5... | collective-permute-start | bytes 3145736 | tf_op jit(solution)/shard_map/ppermute | solution.py:36
  184.2 15.6 %collective-permute-start.34 = (bf16[2,88,1024]{2,1,0:T(8,128)(2,1)}, bf16[2,88,1024]{2,1,0:T(8,128)(2,1)S(1)}, u32[]{:S(2)}, u32[]{:S(2)}) collective-permute-start(bf16[2,88,1024]{2,1,0:T(8,128)(2,1)} %get-tuple-element.94), channel_id=1, source_target_pairs={{0,1},{1,0},{2,3},{3,2},{4,5},{5,4},{6,7},{7,6},{8,9},{9,8},{10,11... | collective-permute-start | bytes 1081352 | tf_op jit(solution)/shard_map/ppermute | solution.py:31
  186.6 14.7 %collective-permute-start.35 = (bf16[2,88,1024]{2,1,0:T(8,128)(2,1)}, bf16[2,88,1024]{2,1,0:T(8,128)(2,1)S(1)}, u32[]{:S(2)}, u32[]{:S(2)}) collective-permute-start(bf16[2,88,1024]{2,1,0:T(8,128)(2,1)} %get-tuple-element.94), channel_id=1, source_target_pairs={{0,2},{1,3},{2,0},{3,1},{4,6},{5,7},{6,4},{7,5},{8,10},{9,11},{10,... | collective-permute-start | bytes 1081352 | tf_op jit(solution)/shard_map/ppermute | solution.py:31
  187.9 41.4 %collective-permute-start.41 = (bf16[2,2,32,2816]{3,2,1,0:T(8,128)(2,1)S(1)}, bf16[2,2,32,2816]{3,2,1,0:T(8,128)(2,1)S(1)}, u32[]{:S(2)}, u32[]{:S(2)}) collective-permute-start(bf16[2,2,32,2816]{3,2,1,0:T(8,128)(2,1)S(1)} %copy-done.18), channel_id=1, source_target_pairs={{0,1},{1,0},{2,3},{3,2},{4,5},{5,4},{6,7},{7,6},{8,9},{9,8},{10,11... | collective-permute-start | bytes 2162696 | tf_op jit(solution)/shard_map/ppermute | solution.py:31
  193.0 29.9 %collective-permute-start.33 = (bf16[2,88,1024]{2,1,0:T(8,128)(2,1)}, bf16[2,88,1024]{2,1,0:T(8,128)(2,1)S(1)}, u32[]{:S(2)}, u32[]{:S(2)}) collective-permute-start(bf16[2,88,1024]{2,1,0:T(8,128)(2,1)} %collective-permute-done.31), channel_id=1, source_target_pairs={{0,1},{1,0},{2,3},{3,2},{4,5},{5,4},{6,7},{7,6},{8,9},{9,8},{10,11... | collective-permute-start | bytes 1081352 | tf_op jit(solution)/shard_map/ppermute | solution.py:31
  199.8 29.8 %collective-permute-start.45 = (bf16[2,2,32,2816]{3,2,1,0:T(8,128)(2,1)S(1)}, bf16[2,2,32,2816]{3,2,1,0:T(8,128)(2,1)S(1)}, u32[]{:S(2)}, u32[]{:S(2)}) collective-permute-start(bf16[2,2,32,2816]{3,2,1,0:T(8,128)(2,1)S(1)} %copy-done.17), channel_id=1, source_target_pairs={{0,2},{1,3},{2,0},{3,1},{4,6},{5,7},{6,4},{7,5},{8,10},{9,11},{10,... | collective-permute-start | bytes 2162696 | tf_op jit(solution)/shard_map/ppermute | solution.py:31
  201.3 26.3 %collective-permute-start.36 = (bf16[2,88,1024]{2,1,0:T(8,128)(2,1)S(1)}, bf16[2,88,1024]{2,1,0:T(8,128)(2,1)S(1)}, u32[]{:S(2)}, u32[]{:S(2)}) collective-permute-start(bf16[2,88,1024]{2,1,0:T(8,128)(2,1)S(1)} %collective-permute-done.34), channel_id=1, source_target_pairs={{0,2},{1,3},{2,0},{3,1},{4,6},{5,7},{6,4},{7,5},{8,10},{9,11},{10,... | collective-permute-start | bytes 1081352 | tf_op jit(solution)/shard_map/ppermute | solution.py:31
  223.0 38.8 %collective-permute-start.26 = (bf16[512,1024]{1,0:T(8,128)(2,1)S(1)}, bf16[512,1024]{1,0:T(8,128)(2,1)S(1)}, u32[]{:S(2)}, u32[]{:S(2)}) collective-permute-start(bf16[512,1024]{1,0:T(8,128)(2,1)S(1)} %multiply_convert_fusion.xa_ref), channel_id=1, source_target_pairs={{0,4},{4,0},{8,12},{12,8},{16,20},{20,16},{24,28},{28,24},{1,5},{5... | collective-permute-start | bytes 3145736 | tf_op jit(solution)/shard_map/ppermute | solution.py:36
  227.6 17.8 %collective-permute-start.42 = (bf16[2,2,32,2816]{3,2,1,0:T(8,128)(2,1)S(1)}, bf16[2,2,32,2816]{3,2,1,0:T(8,128)(2,1)S(1)}, u32[]{:S(2)}, u32[]{:S(2)}) collective-permute-start(bf16[2,2,32,2816]{3,2,1,0:T(8,128)(2,1)S(1)} %copy-done.18), channel_id=1, source_target_pairs={{0,2},{1,3},{2,0},{3,1},{4,6},{5,7},{6,4},{7,5},{8,10},{9,11},{10,... | collective-permute-start | bytes 2162696 | tf_op jit(solution)/shard_map/ppermute | solution.py:31
  228.9 17.4 %collective-permute-start.44 = (bf16[2,2,32,2816]{3,2,1,0:T(8,128)(2,1)S(1)}, bf16[2,2,32,2816]{3,2,1,0:T(8,128)(2,1)S(1)}, u32[]{:S(2)}, u32[]{:S(2)}) collective-permute-start(bf16[2,2,32,2816]{3,2,1,0:T(8,128)(2,1)S(1)} %copy-done.17), channel_id=1, source_target_pairs={{0,1},{1,0},{2,3},{3,2},{4,5},{5,4},{6,7},{7,6},{8,9},{9,8},{10,11... | collective-permute-start | bytes 2162696 | tf_op jit(solution)/shard_map/ppermute | solution.py:31
  229.3 31.5 %collective-permute-start.43 = (bf16[2,2,32,2816]{3,2,1,0:T(8,128)(2,1)S(1)}, bf16[2,2,32,2816]{3,2,1,0:T(8,128)(2,1)S(1)}, u32[]{:S(2)}, u32[]{:S(2)}) collective-permute-start(bf16[2,2,32,2816]{3,2,1,0:T(8,128)(2,1)S(1)} %collective-permute-done.41.rest_1_), channel_id=1, source_target_pairs={{0,2},{1,3},{2,0},{3,1},{4,6},{5,7},{6,4},{7,5},{8,10},{9,11},{10,... | collective-permute-start | bytes 2162696 | tf_op jit(solution)/shard_map/ppermute | solution.py:31
  229.6 32.2 %collective-permute-start.46 = (bf16[2,2,32,2816]{3,2,1,0:T(8,128)(2,1)S(1)}, bf16[2,2,32,2816]{3,2,1,0:T(8,128)(2,1)S(1)}, u32[]{:S(2)}, u32[]{:S(2)}) collective-permute-start(bf16[2,2,32,2816]{3,2,1,0:T(8,128)(2,1)S(1)} %collective-permute-done.45.rest_6_), channel_id=1, source_target_pairs={{0,1},{1,0},{2,3},{3,2},{4,5},{5,4},{6,7},{7,6},{8,9},{9,8},{10,11... | collective-permute-start | bytes 2162696 | tf_op jit(solution)/shard_map/ppermute | solution.py:31
  302.2 16.2 %collective-permute-start.88 = (bf16[2,88,1024]{2,1,0:T(8,128)(2,1)}, bf16[2,88,1024]{2,1,0:T(8,128)(2,1)S(1)}, u32[]{:S(2)}, u32[]{:S(2)}) collective-permute-start(bf16[2,88,1024]{2,1,0:T(8,128)(2,1)} %get-tuple-element.56), channel_id=1, source_target_pairs={{0,1},{1,0},{2,3},{3,2},{4,5},{5,4},{6,7},{7,6},{8,9},{9,8},{10,11... | collective-permute-start | bytes 1081352 | tf_op jit(solution)/shard_map/ppermute | solution.py:31
  303.9 41.4 %collective-permute-start.85 = (bf16[2,88,1024]{2,1,0:T(8,128)(2,1)S(1)}, bf16[2,88,1024]{2,1,0:T(8,128)(2,1)S(1)}, u32[]{:S(2)}, u32[]{:S(2)}) collective-permute-start(bf16[2,88,1024]{2,1,0:T(8,128)(2,1)S(1)} %get-tuple-element.58), channel_id=1, source_target_pairs={{0,2},{1,3},{2,0},{3,1},{4,6},{5,7},{6,4},{7,5},{8,10},{9,11},{10,... | collective-permute-start | bytes 1081352 | tf_op jit(solution)/shard_map/ppermute | solution.py:31
  313.5 34.3 %collective-permute-start.79 = (bf16[2,2,32,2816]{3,2,1,0:T(8,128)(2,1)S(1)}, bf16[2,2,32,2816]{3,2,1,0:T(8,128)(2,1)S(1)}, u32[]{:S(2)}, u32[]{:S(2)}) collective-permute-start(bf16[2,2,32,2816]{3,2,1,0:T(8,128)(2,1)S(1)} %get-tuple-element.51), channel_id=1, source_target_pairs={{0,2},{1,3},{2,0},{3,1},{4,6},{5,7},{6,4},{7,5},{8,10},{9,11},{10,... | collective-permute-start | bytes 2162696 | tf_op jit(solution)/shard_map/ppermute | solution.py:31
  314.2 28.3 %collective-permute-start.90 = (bf16[2,88,1024]{2,1,0:T(8,128)(2,1)S(1)}, bf16[2,88,1024]{2,1,0:T(8,128)(2,1)S(1)}, u32[]{:S(2)}, u32[]{:S(2)}) collective-permute-start(bf16[2,88,1024]{2,1,0:T(8,128)(2,1)S(1)} %fusion.19), channel_id=1, source_target_pairs={{0,2},{1,3},{2,0},{3,1},{4,6},{5,7},{6,4},{7,5},{8,10},{9,11},{10,... | collective-permute-start | bytes 1081352 | tf_op jit(solution)/shard_map/ppermute | solution.py:31
  315.3 30.1 %collective-permute-start.87 = (bf16[2,88,1024]{2,1,0:T(8,128)(2,1)S(1)}, bf16[2,88,1024]{2,1,0:T(8,128)(2,1)S(1)}, u32[]{:S(2)}, u32[]{:S(2)}) collective-permute-start(bf16[2,88,1024]{2,1,0:T(8,128)(2,1)S(1)} %fusion.21), channel_id=1, source_target_pairs={{0,1},{1,0},{2,3},{3,2},{4,5},{5,4},{6,7},{7,6},{8,9},{9,8},{10,11... | collective-permute-start | bytes 1081352 | tf_op jit(solution)/shard_map/ppermute | solution.py:31
  318.4 30.5 %collective-permute-start.76 = (bf16[2,2,32,2816]{3,2,1,0:T(8,128)(2,1)S(1)}, bf16[2,2,32,2816]{3,2,1,0:T(8,128)(2,1)S(1)}, u32[]{:S(2)}, u32[]{:S(2)}) collective-permute-start(bf16[2,2,32,2816]{3,2,1,0:T(8,128)(2,1)S(1)} %get-tuple-element.53), channel_id=1, source_target_pairs={{0,1},{1,0},{2,3},{3,2},{4,5},{5,4},{6,7},{7,6},{8,9},{9,8},{10,11... | collective-permute-start | bytes 2162696 | tf_op jit(solution)/shard_map/ppermute | solution.py:31
  342.5 22.9 %collective-permute-start.47 = (bf16[512,1024]{1,0:T(8,128)(2,1)S(1)}, bf16[512,1024]{1,0:T(8,128)(2,1)S(1)}, u32[]{:S(2)}, u32[]{:S(2)}) collective-permute-start(bf16[512,1024]{1,0:T(8,128)(2,1)S(1)} %slice.231), channel_id=1, source_target_pairs={{0,4},{4,0},{8,12},{12,8},{16,20},{20,16},{24,28},{28,24},{1,5},{5... | collective-permute-start | bytes 3145736 | tf_op jit(solution)/shard_map/ppermute | solution.py:36
  345.3 19.4 %collective-permute-start.48 = (bf16[512,1024]{1,0:T(8,128)(2,1)S(1)}, bf16[512,1024]{1,0:T(8,128)(2,1)S(1)}, u32[]{:S(2)}, u32[]{:S(2)}) collective-permute-start(bf16[512,1024]{1,0:T(8,128)(2,1)S(1)} %slice.230), channel_id=1, source_target_pairs={{0,4},{4,0},{8,12},{12,8},{16,20},{20,16},{24,28},{28,24},{1,5},{5... | collective-permute-start | bytes 3145736 | tf_op jit(solution)/shard_map/ppermute | solution.py:36
  347.8 15.0 %collective-permute-start.92 = (bf16[88,1024]{1,0:T(8,128)(2,1)S(1)}, bf16[88,1024]{1,0:T(8,128)(2,1)S(1)}, u32[]{:S(2)}, u32[]{:S(2)}) collective-permute-start(bf16[88,1024]{1,0:T(8,128)(2,1)S(1)} %get-tuple-element.88), channel_id=1, source_target_pairs={{0,16},{4,20},{8,24},{12,28},{16,0},{20,4},{24,8},{28,12},{1,17},{... | collective-permute-start | bytes 540680 | tf_op jit(solution)/shard_map/ppermute | solution.py:41
  348.9 14.9 %collective-permute-start.93 = (bf16[88,1024]{1,0:T(8,128)(2,1)S(1)}, bf16[88,1024]{1,0:T(8,128)(2,1)S(1)}, u32[]{:S(2)}, u32[]{:S(2)}) collective-permute-start(bf16[88,1024]{1,0:T(8,128)(2,1)S(1)} %get-tuple-element.89), channel_id=1, source_target_pairs={{0,24},{4,28},{8,0},{12,4},{16,8},{20,12},{24,16},{28,20},{1,25},{... | collective-permute-start | bytes 540680 | tf_op jit(solution)/shard_map/ppermute | solution.py:41
  351.5 80.4 %collective-permute-start.78 = (bf16[2,2,32,2816]{3,2,1,0:T(8,128)(2,1)}, bf16[2,2,32,2816]{3,2,1,0:T(8,128)(2,1)}, u32[]{:S(2)}, u32[]{:S(2)}) collective-permute-start(bf16[2,2,32,2816]{3,2,1,0:T(8,128)(2,1)} %get-tuple-element.50), channel_id=1, source_target_pairs={{0,2},{1,3},{2,0},{3,1},{4,6},{5,7},{6,4},{7,5},{8,10},{9,11},{10,... | collective-permute-start | bytes 2162696 | tf_op jit(solution)/shard_map/ppermute | solution.py:31
  362.8 70.9 %collective-permute-start.75 = (bf16[2,2,32,2816]{3,2,1,0:T(8,128)(2,1)}, bf16[2,2,32,2816]{3,2,1,0:T(8,128)(2,1)}, u32[]{:S(2)}, u32[]{:S(2)}) collective-permute-start(bf16[2,2,32,2816]{3,2,1,0:T(8,128)(2,1)} %get-tuple-element.52), channel_id=1, source_target_pairs={{0,1},{1,0},{2,3},{3,2},{4,5},{5,4},{6,7},{7,6},{8,9},{9,8},{10,11... | collective-permute-start | bytes 2162696 | tf_op jit(solution)/shard_map/ppermute | solution.py:31
  371.6 13.4 %collective-permute-start.49 = (bf16[512,256]{1,0:T(8,128)(2,1)S(1)}, bf16[512,256]{1,0:T(8,128)(2,1)S(1)}, u32[]{:S(2)}, u32[]{:S(2)}) collective-permute-start(bf16[512,256]{1,0:T(8,128)(2,1)S(1)} %get-tuple-element.75), channel_id=1, source_target_pairs={{0,1},{1,0},{2,3},{3,2},{4,5},{5,4},{6,7},{7,6},{8,9},{9,8},{10,11... | collective-permute-start | bytes 786440 | tf_op jit(solution)/shard_map/ppermute | solution.py:31
  372.2 14.4 %collective-permute-start.50 = (bf16[512,256]{1,0:T(8,128)(2,1)S(1)}, bf16[512,256]{1,0:T(8,128)(2,1)S(1)}, u32[]{:S(2)}, u32[]{:S(2)}) collective-permute-start(bf16[512,256]{1,0:T(8,128)(2,1)S(1)} %get-tuple-element.74), channel_id=1, source_target_pairs={{0,2},{1,3},{2,0},{3,1},{4,6},{5,7},{6,4},{7,5},{8,10},{9,11},{10,... | collective-permute-start | bytes 786440 | tf_op jit(solution)/shard_map/ppermute | solution.py:31
  372.7 18.1 %collective-permute-start.51 = (bf16[512,256]{1,0:T(8,128)(2,1)S(1)}, bf16[512,256]{1,0:T(8,128)(2,1)S(1)}, u32[]{:S(2)}, u32[]{:S(2)}) collective-permute-start(bf16[512,256]{1,0:T(8,128)(2,1)S(1)} %get-tuple-element.73), channel_id=1, source_target_pairs={{0,3},{1,2},{2,1},{3,0},{4,7},{5,6},{6,5},{7,4},{8,11},{9,10},{10,... | collective-permute-start | bytes 786440 | tf_op jit(solution)/shard_map/ppermute | solution.py:31
  385.0 46.9 %collective-permute-start.80 = (bf16[2,2,32,2816]{3,2,1,0:T(8,128)(2,1)}, bf16[2,2,32,2816]{3,2,1,0:T(8,128)(2,1)}, u32[]{:S(2)}, u32[]{:S(2)}) collective-permute-start(bf16[2,2,32,2816]{3,2,1,0:T(8,128)(2,1)} %fusion.15), channel_id=1, source_target_pairs={{0,1},{1,0},{2,3},{3,2},{4,5},{5,4},{6,7},{7,6},{8,9},{9,8},{10,11... | collective-permute-start | bytes 2162696 | tf_op jit(solution)/shard_map/ppermute | solution.py:31
  386.6 47.1 %collective-permute-start.77 = (bf16[2,2,32,2816]{3,2,1,0:T(8,128)(2,1)}, bf16[2,2,32,2816]{3,2,1,0:T(8,128)(2,1)}, u32[]{:S(2)}, u32[]{:S(2)}) collective-permute-start(bf16[2,2,32,2816]{3,2,1,0:T(8,128)(2,1)} %fusion.17), channel_id=1, source_target_pairs={{0,2},{1,3},{2,0},{3,1},{4,6},{5,7},{6,4},{7,5},{8,10},{9,11},{10,... | collective-permute-start | bytes 2162696 | tf_op jit(solution)/shard_map/ppermute | solution.py:31
  390.8 84.6 %collective-permute-start.65 = (bf16[4,128,1024]{2,1,0:T(8,128)(2,1)S(1)}, bf16[4,128,1024]{2,1,0:T(8,128)(2,1)S(1)}, u32[]{:S(2)}, u32[]{:S(2)}) collective-permute-start(bf16[4,128,1024]{2,1,0:T(8,128)(2,1)S(1)} %dynamic-slice_bitcast_fusion), channel_id=1, source_target_pairs={{0,4},{4,0},{8,12},{12,8},{16,20},{20,16},{24,28},{28,24},{1,5},{5... | collective-permute-start | bytes 3145736 | tf_op jit(solution)/shard_map/ppermute | solution.py:36
  436.1 16.4 %collective-permute-start.81 = (bf16[2,32,2816]{2,1,0:T(8,128)(2,1)S(1)}, bf16[2,32,2816]{2,1,0:T(8,128)(2,1)S(1)}, u32[]{:S(2)}, u32[]{:S(2)}) collective-permute-start(bf16[2,32,2816]{2,1,0:T(8,128)(2,1)S(1)} %get-tuple-element.60), channel_id=1, source_target_pairs={{0,8},{4,12},{8,16},{12,20},{16,24},{20,28},{24,0},{28,4},{1,9},{5... | collective-permute-start | bytes 1081352 | tf_op jit(solution)/shard_map/ppermute | solution.py:41
  436.7 30.9 %collective-permute-start.82 = (bf16[2,32,2816]{2,1,0:T(8,128)(2,1)S(1)}, bf16[2,32,2816]{2,1,0:T(8,128)(2,1)S(1)}, u32[]{:S(2)}, u32[]{:S(2)}) collective-permute-start(bf16[2,32,2816]{2,1,0:T(8,128)(2,1)S(1)} %get-tuple-element.61), channel_id=1, source_target_pairs={{0,16},{4,20},{8,24},{12,28},{16,0},{20,4},{24,8},{28,12},{1,17},{... | collective-permute-start | bytes 1081352 | tf_op jit(solution)/shard_map/ppermute | solution.py:41
  443.9 25.9 %collective-permute-start.83 = (bf16[2,32,2816]{2,1,0:T(8,128)(2,1)S(1)}, bf16[2,32,2816]{2,1,0:T(8,128)(2,1)S(1)}, u32[]{:S(2)}, u32[]{:S(2)}) collective-permute-start(bf16[2,32,2816]{2,1,0:T(8,128)(2,1)S(1)} %get-tuple-element.62), channel_id=1, source_target_pairs={{0,24},{4,28},{8,0},{12,4},{16,8},{20,12},{24,16},{28,20},{1,25},{... | collective-permute-start | bytes 1081352 | tf_op jit(solution)/shard_map/ppermute | solution.py:41
  451.2 25.4 %collective-permute-start.58 = (bf16[4,128,768]{2,1,0:T(8,128)(2,1)S(1)}, bf16[4,128,768]{2,1,0:T(8,128)(2,1)S(1)}, u32[]{:S(2)}, u32[]{:S(2)}) collective-permute-start(bf16[4,128,768]{2,1,0:T(8,128)(2,1)S(1)} %dynamic-slice_bitcast_fusion.1), channel_id=1, source_target_pairs={{0,4},{4,0},{8,12},{12,8},{16,20},{20,16},{24,28},{28,24},{1,5},{5... | collective-permute-start | bytes 2359304 | tf_op jit(solution)/shard_map/ppermute | solution.py:36
  452.5 18.3 %collective-permute-start.53 = (bf16[256,1024]{1,0:T(8,128)(2,1)S(1)}, bf16[256,1024]{1,0:T(8,128)(2,1)S(1)}, u32[]{:S(2)}, u32[]{:S(2)}) collective-permute-start(bf16[256,1024]{1,0:T(8,128)(2,1)S(1)} %get-tuple-element.47), channel_id=1, source_target_pairs={{0,1},{1,0},{2,3},{3,2},{4,5},{5,4},{6,7},{7,6},{8,9},{9,8},{10,11... | collective-permute-start | bytes 1572872 | tf_op jit(solution)/shard_map/ppermute | solution.py:31
  467.6 48.4 %collective-permute-start.52 = (bf16[256,1024]{1,0:T(8,128)(2,1)}, bf16[256,1024]{1,0:T(8,128)(2,1)}, u32[]{:S(2)}, u32[]{:S(2)}) collective-permute-start(bf16[256,1024]{1,0:T(8,128)(2,1)} %get-tuple-element.44), channel_id=1, source_target_pairs={{0,1},{1,0},{2,3},{3,2},{4,5},{5,4},{6,7},{7,6},{8,9},{9,8},{10,11... | collective-permute-start | bytes 1572872 | tf_op jit(solution)/shard_map/ppermute | solution.py:31
  469.8 46.8 %collective-permute-start.56 = (bf16[256,1024]{1,0:T(8,128)(2,1)}, bf16[256,1024]{1,0:T(8,128)(2,1)}, u32[]{:S(2)}, u32[]{:S(2)}) collective-permute-start(bf16[256,1024]{1,0:T(8,128)(2,1)} %get-tuple-element.45), channel_id=1, source_target_pairs={{0,2},{1,3},{2,0},{3,1},{4,6},{5,7},{6,4},{7,5},{8,10},{9,11},{10,... | collective-permute-start | bytes 1572872 | tf_op jit(solution)/shard_map/ppermute | solution.py:31
  476.6 18.3 %collective-permute-start.70 = (bf16[2,128,256]{2,1,0:T(8,128)(2,1)}, bf16[2,128,256]{2,1,0:T(8,128)(2,1)}, u32[]{:S(2)}, u32[]{:S(2)}) collective-permute-start(bf16[2,128,256]{2,1,0:T(8,128)(2,1)} %get-tuple-element.70), channel_id=1, source_target_pairs={{0,2},{1,3},{2,0},{3,1},{4,6},{5,7},{6,4},{7,5},{8,10},{9,11},{10,... | collective-permute-start | bytes 393224 | tf_op jit(solution)/shard_map/ppermute | solution.py:31
  477.8 20.0 %collective-permute-start.59 = (bf16[128,768]{1,0:T(8,128)(2,1)}, bf16[128,768]{1,0:T(8,128)(2,1)}, u32[]{:S(2)}, u32[]{:S(2)}) collective-permute-start(bf16[128,768]{1,0:T(8,128)(2,1)} %get-tuple-element.84), channel_id=1, source_target_pairs={{0,8},{4,12},{8,16},{12,20},{16,24},{20,28},{24,0},{28,4},{1,9},{5... | collective-permute-start | bytes 589832 | tf_op jit(solution)/shard_map/ppermute | solution.py:41
  482.9 15.4 %collective-permute-start.60 = (bf16[128,768]{1,0:T(8,128)(2,1)}, bf16[128,768]{1,0:T(8,128)(2,1)}, u32[]{:S(2)}, u32[]{:S(2)}) collective-permute-start(bf16[128,768]{1,0:T(8,128)(2,1)} %get-tuple-element.86), channel_id=1, source_target_pairs={{0,16},{4,20},{8,24},{12,28},{16,0},{20,4},{24,8},{28,12},{1,17},{... | collective-permute-start | bytes 589832 | tf_op jit(solution)/shard_map/ppermute | solution.py:41
  497.8 19.8 %collective-permute-start.54 = (bf16[256,1024]{1,0:T(8,128)(2,1)}, bf16[256,1024]{1,0:T(8,128)(2,1)S(1)}, u32[]{:S(2)}, u32[]{:S(2)}) collective-permute-start(bf16[256,1024]{1,0:T(8,128)(2,1)} %add_convert_fusion.6), channel_id=1, source_target_pairs={{0,2},{1,3},{2,0},{3,1},{4,6},{5,7},{6,4},{7,5},{8,10},{9,11},{10,... | collective-permute-start | bytes 1572872 | tf_op jit(solution)/shard_map/ppermute | solution.py:31
  513.5 23.5 %collective-permute-start.55 = (bf16[256,1024]{1,0:T(8,128)(2,1)}, bf16[256,1024]{1,0:T(8,128)(2,1)S(1)}, u32[]{:S(2)}, u32[]{:S(2)}) collective-permute-start(bf16[256,1024]{1,0:T(8,128)(2,1)} %get-tuple-element.46), channel_id=1, source_target_pairs={{0,2},{1,3},{2,0},{3,1},{4,6},{5,7},{6,4},{7,5},{8,10},{9,11},{10,... | collective-permute-start | bytes 1572872 | tf_op jit(solution)/shard_map/ppermute | solution.py:31
  516.0 13.3 %collective-permute-start.62 = (f32[1,32]{1,0:T(1,128)S(1)}, f32[1,32]{1,0:T(1,128)S(1)}, u32[]{:S(2)}, u32[]{:S(2)}) collective-permute-start(f32[1,32]{1,0:T(1,128)S(1)} %get-tuple-element.111), channel_id=1, source_target_pairs={{0,1},{1,0},{2,3},{3,2},{4,5},{5,4},{6,7},{7,6},{8,9},{9,8},{10,11... | collective-permute-start | bytes 392 | tf_op jit(solution)/shard_map/ppermute | solution.py:31
  (95 other events, 851.3 us)

commit v2 on v1

v2 whole, which is shorter than its diff:
```python
import functools

import jax
import jax.numpy as jnp
from jax import lax
from jax.experimental import pallas as pl
from jax.experimental.pallas import tpu as pltpu
from jax.sharding import Mesh, PartitionSpec as P

HEAD_DIM = 64
HALF = HEAD_DIM // 2
BLOCK = 256
VMEM_LIMIT = 60 * 1024 * 1024

eps = 1e-06
rope_base = 10000.0
bf16 = jnp.bfloat16
f32 = jnp.float32

NN = (((1,), (0,)), ((), ()))
NT = (((1,), (1,)), ((), ()))
TN = (((0,), (0,)), ((), ()))


def mm(left, right, dims=NN):
    return lax.dot_general(left, right, dims, preferred_element_type=f32)


def swap_tensor(value, mask):
    size = lax.axis_size("tensor")
    return lax.ppermute(value, "tensor", [(i, i ^ mask) for i in range(size)])


def swap_core(value):
    return lax.ppermute(value, "core", [(0, 1), (1, 0)])


def shift_z(value, step):
    size = lax.axis_size("z")
    return lax.ppermute(value, "z", [(i, (i + step) % size) for i in range(size)])


def bit_orders():
    bits = [1 << b for b in range(lax.axis_size("tensor").bit_length() - 1)]
    return bits, bits[1:] + bits[:1]


def together(*values):
    return lax.optimization_barrier(values)


def halves(value):
    middle = value.shape[0] // 2
    return value[:middle], value[middle:]


def gather_near(value):
    if lax.axis_size("tensor") != 4:
        return []
    return [swap_tensor(value, 1), swap_tensor(value, 2)]


def pass_on(near):
    return [halves(near[0])[0], halves(near[1])[1]] if near else []


def gather_far(value, near, passed=()):
    if near:
        if not passed:
            passed = pass_on(near)
        far = [swap_tensor(passed[0], 2), swap_tensor(passed[1], 1)]
        return {0: [value], 1: [near[0]], 2: [near[1]], 3: far}
    parts = []
    for piece, bits in zip(halves(value), bit_orders()):
        have = {0: piece}
        for bit in bits:
            have.update({m ^ bit: swap_tensor(got, bit) for m, got in list(have.items())})
        parts.append(have)
    return {mask: [part[mask] for part in parts] for mask in parts[0]}


def add(left, right):
    return (left.astype(f32) + right.astype(f32)).astype(bf16)


def scatter_far(parts):
    if lax.axis_size("tensor") != 4:
        return []
    upper, lower = parts[3]
    return [swap_tensor(upper, 1), swap_tensor(lower, 2)]


def scatter_join(parts, far):
    if not far:
        return []
    to_x, to_y = parts[1][0], parts[2][0]
    middle = to_y.shape[0] // 2
    return [
        lax.dynamic_update_slice_in_dim(to_x, add(to_x[middle:], far[1]), middle, 0),
        lax.dynamic_update_slice_in_dim(to_y, add(to_y[:middle], far[0]), 0, 0),
    ]


def scatter_near(parts, joined):
    if joined:
        return [parts[0][0], swap_tensor(joined[0], 1), swap_tensor(joined[1], 2)]
    parts = {mask: jnp.concatenate(part, axis=0) for mask, part in parts.items()}
    sums = []
    for which, bits in enumerate(bit_orders()):
        left = {mask: halves(part)[which] for mask, part in parts.items()}
        for bit in bits:
            for mask in [m for m in left if not m & bit]:
                left[mask] = add(left[mask], swap_tensor(left.pop(mask | bit), bit))
        sums.append(left[0])
    return [jnp.concatenate(sums, axis=0)]


def spread_tensor(value):
    return swap_all([value] * lax.axis_size("tensor"))


def swap_all(pieces):
    return [swap_tensor(piece, mask) if mask else piece for mask, piece in enumerate(pieces)]


def by_index(pieces):
    here = lax.axis_index("tensor")
    order = []
    for place in range(len(pieces)):
        piece = pieces[0]
        for mask in range(1, len(pieces)):
            piece = jnp.where(here ^ place == mask, pieces[mask], piece)
        order.append(piece)
    return jnp.stack(order)


def send_z(value):
    return jnp.stack([value] + [shift_z(value, i) for i in range(1, lax.axis_size("z"))])


def sums_z(terms):
    depth = lax.axis_size("z")
    here = lax.axis_index("z")
    take = lambda term, i: lax.dynamic_index_in_dim(term, (here + i) % depth, 0, False)
    sums = [total([take(term, i) for term in terms]) for i in range(depth)]
    return [sums[0]] + [part.astype(bf16) for part in sums[1:]]


def scatter_z(sums):
    return [sums[0]] + [shift_z(part, i + 1) for i, part in enumerate(sums[1:])]


def exchange(value, axis):
    return lax.all_to_all(value, axis, 0, 0)


def spread(value, axis):
    return exchange(jnp.broadcast_to(value[None], (lax.axis_size(axis),) + value.shape), axis)


def piece_rows(mask, height, n_t):
    return [height // 2] * 2 if mask == 3 and n_t == 4 else [height]


def total(terms):
    terms = [terms[i].astype(f32) for i in range(len(terms))]
    return sum(terms[1:], terms[0])


def attend_forward_kernel(
    heads, n_t, x_at, place_ref, lo_ref, full_ref, fv_ref, cos_ref, sin_ref, start_ref, gain_ref, *rest
):
    x_in, w_in, rest = rest[: len(x_at)], rest[len(x_at) : len(x_at) + 2], rest[len(x_at) + 2 :]
    qt_ref, kt_ref, kn_ref, vn_ref, ot_ref, lse_ref, x_out, w_out = rest[:8]
    o_out, (x_ref, w_ref, wt, vt, o_ref, acc, sems) = rest[8 : 8 + n_t], rest[8 + n_t :]
    core, t = place_ref[1], place_ref[2]
    n_z = w_in[0].shape[0]
    height = w_ref.shape[0] // (2 * n_z)
    cols = heads * HEAD_DIM
    blocks = x_ref.shape[0] // BLOCK
    count = x_ref.shape[0] // n_t
    copies = []
    for other, ref in enumerate(w_in):
        for z in range(n_z):
            row = pl.multiple_of((2 * z + jnp.bitwise_xor(core, other)) * height, height)
            copies.append((ref.at[z, pl.ds(0, height)], w_ref.at[pl.ds(row, height)]))
    for ref, (mask, offset) in zip(x_in, x_at):
        row = jnp.bitwise_xor(t, mask) * count + offset
        size = ref.shape[0]
        copies.append((ref, x_ref.at[pl.ds(pl.multiple_of(row, size), size)]))
    copies = [pltpu.make_async_copy(a, b, sems.at[i]) for i, (a, b) in enumerate(copies)]
    for copy in copies:
        copy.start()
    for copy in copies:
        copy.wait()
    keep = [
        pltpu.make_async_copy(x_ref, x_out, sems.at[len(copies)]),
        pltpu.make_async_copy(w_ref, w_out, sems.at[len(copies) + 1]),
    ]
    for copy in keep:
        copy.start()
    wt[...] = (w_ref[...].astype(f32).T * gain_ref[...]).astype(bf16)

    def project(i, carry):
        at = pl.ds(pl.multiple_of(i * BLOCK, BLOCK), BLOCK)
        joint = mm(wt[...], x_ref[at, :], NT)
        cosine, sine = cos_ref[:, at], sin_ref[:, at]
        first = fv_ref[at, :].astype(f32).T
        for h in range(heads):
            lo, mid, hi = h * HEAD_DIM, h * HEAD_DIM + HALF, (h + 1) * HEAD_DIM
            qa, qb = joint[lo:mid], joint[mid:hi]
            q = jnp.concatenate([qa * cosine - qb * sine, qb * cosine + qa * sine], axis=0)
            qt_ref[lo:hi, at] = (q * HEAD_DIM ** (-0.5)).astype(bf16)
            ka, kb = joint[cols + lo : cols + mid], joint[cols + mid : cols + hi]
            k = jnp.concatenate([ka * cosine - kb * sine, kb * cosine + ka * sine], axis=0)
            kt_ref[lo:hi, at] = k.astype(bf16)
            kn_ref[h, at, :] = k.T.astype(bf16)
            v = 0.5 * joint[2 * cols + lo : 2 * cols + hi] + 0.5 * first[lo:hi]
            vt[lo:hi, at] = v.astype(bf16)
            vn_ref[h, at, :] = v.T.astype(bf16)
        return carry

    lax.fori_loop(0, blocks, project, 0)

    def query_block(i, carry):
        qs = pl.ds(pl.multiple_of(i * BLOCK, BLOCK), BLOCK)
        start = start_ref[:, qs]
        key_iota = lax.broadcasted_iota(jnp.int32, (BLOCK, BLOCK), 0)
        query_pos = lax.broadcasted_iota(jnp.int32, (BLOCK, BLOCK), 1) + i * BLOCK

        def tile(j, state, masked, opening):
            ks = pl.ds(pl.multiple_of(j * BLOCK, BLOCK), BLOCK)
            if masked:
                key_pos = key_iota + j * BLOCK
                allowed = (key_pos <= query_pos) & (key_pos >= start)
            result = []
            all_scores = [
                mm(kn_ref[h, ks, :], qt_ref[h * HEAD_DIM : (h + 1) * HEAD_DIM, qs])
                for h in range(heads)
            ]
            if masked:
                all_scores = [jnp.where(allowed, sc, -1e30) for sc in all_scores]
            peaks = [jnp.max(sc, axis=0, keepdims=True) for sc in all_scores]
            if not opening:
                shrinks = []
                for h in range(heads):
                    peaks[h] = jnp.maximum(state[h][0], peaks[h])
                    shrinks.append(jnp.exp(state[h][0] - peaks[h]))
            all_probs = [jnp.exp(sc - pk) for sc, pk in zip(all_scores, peaks)]
            for h in range(heads):
                rows = slice(h * HEAD_DIM, (h + 1) * HEAD_DIM)
                total = jnp.sum(all_probs[h], axis=0, keepdims=True)
                out = mm(vt[rows, ks], all_probs[h].astype(bf16))
                if not opening:
                    total = total + state[h][1] * shrinks[h]
                    out = out + acc[rows, :] * shrinks[h]
                acc[rows, :] = out
                result.append((peaks[h], total))
            return tuple(result)

        lo, full = lo_ref[i], full_ref[i]
        state = tile(i, None, True, True)
        state = lax.fori_loop(full, i, lambda j, s: tile(j, s, False, False), state)
        state = lax.fori_loop(lo, full, lambda j, s: tile(j, s, True, False), state)
        for h in range(heads):
            rows = slice(h * HEAD_DIM, (h + 1) * HEAD_DIM)
            peak, total = state[h]
            acc[rows, :] = acc[rows, :] * (1.0 / total)
            lse_ref[h : h + 1, qs] = peak + jnp.log(total)
        out = acc[...]
        ot_ref[:, qs] = out.astype(bf16)
        o_ref[qs, :] = out.T.astype(bf16)
        return carry

    lax.fori_loop(0, blocks, query_block, 0)
    for mask in range(n_t):
        row = pl.multiple_of(jnp.bitwise_xor(t, mask) * count, count)
        copy = pltpu.make_async_copy(o_ref.at[pl.ds(row, count)], o_out[mask], sems.at[mask])
        copy.start()
        keep.append(copy)
    for copy in keep:
        copy.wait()


def attend_backward_kernel(
    heads, n_t, place_ref, lo_ref, full_ref, qt_ref, kt_ref, kn_ref, vn_ref, ot_ref, lse_ref,
    cos_ref, sin_ref, start_ref, w_ref, gain_ref, *rest
):
    do_in, rest = rest[:n_t], rest[n_t:]
    gt_ref, gf_ref, *gn_out = rest[:-8]
    do_ref, gn_ref, dot_, delta, dq, dk, dv, sems = rest[-8:]
    t = place_ref[2]
    cols = heads * HEAD_DIM
    blocks = do_ref.shape[0] // BLOCK
    count = do_ref.shape[0] // n_t
    copies = []
    for mask in range(n_t):
        row = pl.multiple_of(jnp.bitwise_xor(t, mask) * count, count)
        copies.append(
            pltpu.make_async_copy(do_in[mask], do_ref.at[pl.ds(row, count)], sems.at[mask])
        )
        copies[-1].start()
    for copy in copies:
        copy.wait()
    dk[...] = jnp.zeros_like(dk)
    dv[...] = jnp.zeros_like(dv)

    def prepare(i, carry):
        at = pl.ds(pl.multiple_of(i * BLOCK, BLOCK), BLOCK)
        grads = do_ref[at, :].astype(f32).T
        dot_[:, at] = grads.astype(bf16)
        prod = grads * ot_ref[:, at].astype(f32)
        for h in range(heads):
            delta[h : h + 1, at] = jnp.sum(
                prod[h * HEAD_DIM : (h + 1) * HEAD_DIM], axis=0, keepdims=True
            )
        return carry

    lax.fori_loop(0, blocks, prepare, 0)

    def query_block(step, carry):
        i = blocks - 1 - step
        qs = pl.ds(pl.multiple_of(i * BLOCK, BLOCK), BLOCK)
        start = start_ref[:, qs]
        key_iota = lax.broadcasted_iota(jnp.int32, (BLOCK, BLOCK), 0)
        query_pos = lax.broadcasted_iota(jnp.int32, (BLOCK, BLOCK), 1) + i * BLOCK
        dq[...] = jnp.zeros_like(dq)

        def tile(j, carry, masked):
            ks = pl.ds(pl.multiple_of(j * BLOCK, BLOCK), BLOCK)
            if masked:
                key_pos = key_iota + j * BLOCK
                allowed = (key_pos <= query_pos) & (key_pos >= start)
            hs = range(heads)
            rows = [slice(h * HEAD_DIM, (h + 1) * HEAD_DIM) for h in hs]
            q_h = [qt_ref[rows[h], qs] for h in hs]
            do_h = [dot_[rows[h], qs] for h in hs]
            scores = [mm(kn_ref[h, ks, :], q_h[h]) for h in hs]
            gp = [mm(vn_ref[h, ks, :], do_h[h]) for h in hs]
            for h in hs:
                s = scores[h]
                if masked:
                    s = jnp.where(allowed, s, -1e30)
                probs = jnp.exp(s - lse_ref[h : h + 1, qs])
                grad_scores = (probs * (gp[h] - delta[h : h + 1, qs])).astype(bf16)
                dv[rows[h], ks] += mm(do_h[h], probs.astype(bf16), NT)
                dk[rows[h], ks] += mm(q_h[h], grad_scores, NT)
                dq[rows[h], :] += mm(kt_ref[rows[h], ks], grad_scores)
            return carry

        lo, full = lo_ref[i], full_ref[i]
        tile(i, 0, True)
        lax.fori_loop(full, i, lambda j, s: tile(j, s, False), 0)
        lax.fori_loop(lo, full, lambda j, s: tile(j, s, True), 0)

        cosine, sine = cos_ref[:, qs], sin_ref[:, qs]
        pieces = []
        for source, factor in ((dq, HEAD_DIM ** (-0.5)), (dk, 1.0)):
            for h in range(heads):
                lo_row, mid, hi = h * HEAD_DIM, h * HEAD_DIM + HALF, (h + 1) * HEAD_DIM
                where = slice(None) if source is dq else qs
                a, b = source[lo_row:mid, where] * factor, source[mid:hi, where] * factor
                pieces += [a * cosine + b * sine, b * cosine - a * sine]
        half_v = 0.5 * dv[:, qs]
        gf_ref[qs, :] = half_v.T
        grads = jnp.concatenate(pieces + [half_v], axis=0)
        gt_ref[:, qs] = grads.astype(bf16)
        gn_ref[qs, :] = (mm(grads.T.astype(bf16), w_ref[...], NT) * gain_ref[...]).astype(bf16)
        return carry

    lax.fori_loop(0, blocks, query_block, 0)
    copies, outs = [], list(gn_out)
    for mask in range(n_t):
        row = jnp.bitwise_xor(t, mask) * count
        for size in piece_rows(mask, count, n_t):
            copies.append(
                pltpu.make_async_copy(
                    gn_ref.at[pl.ds(pl.multiple_of(row, size), size)],
                    outs.pop(0),
                    sems.at[len(copies)],
                )
            )
            row = row + size
    for copy in copies:
        copy.start()
    for copy in copies:
        copy.wait()


def feed_forward_kernel(
    masks, place_ref, xa_ref, xb_ref, ga_ref, gb_ref, wd_ref, *rest
):
    count = len(masks)
    pieces, (inner_ref, gvu_ref, u_ref, u_far_ref, w, sems) = rest[:count], rest[count:]
    t = place_ref[2]
    copies = []
    for piece, (mask, first) in zip(pieces, masks):
        at = w.at[pl.ds(first, piece.shape[0]), :, jnp.bitwise_xor(t, mask)]
        copies.append(pltpu.make_async_copy(piece, at, sems.at[len(copies)]))
        copies[-1].start()
    for copy in copies:
        copy.wait()
    features = xa_ref.shape[1]
    tokens = xa_ref.shape[0]
    ff = wd_ref.shape[0]
    step, high = 256, min(512, tokens)
    edges = list(range(0, ff, step)) + [ff]

    def weight(lo, hi):
        return w[:, :, :, :, lo:hi].reshape(features, hi - lo)

    for source, (x_ref, g_ref) in enumerate(((xa_ref, ga_ref), (xb_ref, gb_ref))):

        def rows_step(i, carry, x_ref=x_ref, g_ref=g_ref, source=source):
            rows = pl.ds(pl.multiple_of(i * high, high), high)
            outs = pl.ds(pl.multiple_of(source * tokens + i * high, high), high)
            x, g = x_ref[rows, :], g_ref[rows, :]
            for lo, hi in zip(edges[:-1], edges[1:]):
                gate = mm(x, weight(lo, hi))
                up = mm(x, weight(ff + lo, ff + hi))
                grad_inner = mm(g, wd_ref[lo:hi, :], NT)
                sig = jax.nn.sigmoid(gate)
                act = gate * sig
                inner_ref[outs, lo:hi] = (act * up).astype(bf16)
                gvu_ref[outs, lo:hi] = (
                    grad_inner * up * (sig * (1.0 + gate * (1.0 - sig)))
                ).astype(bf16)
                gvu_ref[outs, ff + lo : ff + hi] = (grad_inner * act).astype(bf16)
            u = mm(gvu_ref[outs, :], weight(0, 2 * ff), NT)
            if source == 0:
                u_ref[rows, :] = u
            else:
                u_far_ref[rows, :] = u.astype(bf16)
            return carry

        lax.fori_loop(0, tokens // high, rows_step, 0)


def gate_up_grad_kernel(n_t, place_ref, xa_ref, xb_ref, gvu_ref, *rest):
    *outs, xt, grads, sems = rest
    t = place_ref[2]
    tokens, features = xa_ref.shape
    n_z = grads.shape[0]
    own = grads.shape[3]
    step = 256
    for i in range(0, tokens, step):
        xt[:, i : i + step] = xa_ref[i : i + step, :].T
        xt[:, tokens + i : tokens + i + step] = xb_ref[i : i + step, :].T

    def columns(i, carry):
        at = pl.ds(pl.multiple_of(i * step, step), step)
        part = mm(xt[...], gvu_ref[:, at]).astype(bf16)
        grads[:, :, :, :, at] = part.reshape(n_z, 2, n_t, own, step)
        return carry

    lax.fori_loop(0, gvu_ref.shape[1] // step, columns, 0)
    copies, outs = [], list(outs)
    for mask in range(n_t):
        copy = pltpu.make_async_copy(
            grads.at[:, :, jnp.bitwise_xor(t, mask)], outs[mask], sems.at[mask]
        )
        copy.start()
        copies.append(copy)
    for copy in copies:
        copy.wait()


def load_output_weight(place_ref, near, far, wo, sems):
    z, core = place_ref[0], place_ref[1]
    n_z = near.shape[0]
    copies = []
    for other, ref in enumerate((near, far)):
        for i in range(n_z):
            at = wo.at[2 * lax.rem(z - i + n_z, n_z) + jnp.bitwise_xor(core, other)]
            copies.append(pltpu.make_async_copy(ref.at[i], at, sems.at[len(copies)]))
            copies[-1].start()
    for copy in copies:
        copy.wait()


def project_out_kernel(n_t, place_ref, token_ref, near, far, *rest):
    *att, hidden_ref, unit_ref, wo, sems = rest
    load_output_weight(place_ref, near, far, wo, sems)
    t = place_ref[2]
    n_dp, _, height, cols = wo.shape
    step = 256

    def rows_step(i, carry):
        rows = pl.ds(pl.multiple_of(i * step, step), step)
        hidden = token_ref[rows, :].astype(f32)
        for mask, ref in enumerate(att):
            weight = wo[:, jnp.bitwise_xor(t, mask)].reshape(n_dp * height, cols)
            hidden = hidden + mm(ref[rows, :], weight, NT)
        hidden_ref[rows, :] = hidden
        mean = jnp.mean(hidden * hidden, axis=-1, keepdims=True)
        unit_ref[rows, :] = (hidden * lax.rsqrt(mean + eps)).astype(bf16)
        return carry

    lax.fori_loop(0, token_ref.shape[0] // step, rows_step, 0)


def norm_backward(values, scaled, inverse):
    dot = jnp.sum(scaled * values, axis=-1, keepdims=True) / values.shape[-1]
    return inverse * scaled - values * (inverse * inverse * inverse * dot)


def branch_grad_kernel(
    place_ref, hidden_ref, u_ref, u_got_ref, g_ref, near, far, grad_ref, branch_ref, *rest
):
    *outs, wo, sems = rest
    load_output_weight(place_ref, near, far, wo, sems)
    t = place_ref[2]
    n_dp, n_t, height, cols = wo.shape
    step = 256

    def rows_step(i, carry):
        rows = pl.ds(pl.multiple_of(i * step, step), step)
        hidden = hidden_ref[rows, :]
        scaled = u_ref[rows, :] + u_got_ref[rows, :].astype(f32)
        inverse = lax.rsqrt(jnp.mean(hidden * hidden, axis=-1, keepdims=True) + eps)
        grad = g_ref[rows, :].astype(f32) + norm_backward(hidden, scaled, inverse)
        grad_ref[rows, :] = grad
        branch = grad.astype(bf16)
        branch_ref[rows, :] = branch
        for mask, out in enumerate(outs):
            weight = wo[:, jnp.bitwise_xor(t, mask)].reshape(n_dp * height, cols)
            out[rows, :] = mm(branch, weight).astype(bf16)
        return carry

    lax.fori_loop(0, hidden_ref.shape[0] // step, rows_step, 0)


def output_grad_kernel(place_ref, branch_ref, *rest):
    *att, keep_ref, give_ref, turned, grads = rest
    core, t = place_ref[1], place_ref[2]
    n_z, n_t, height, cols = keep_ref.shape
    turned[...] = branch_ref[...].T
    for mask, ref in enumerate(att):
        part = mm(turned[...], ref[...]).astype(bf16).reshape(n_z, 2, height, cols)
        for which in range(2):
            grads[which, :, jnp.bitwise_xor(t, mask)] = part[:, which]
    keep_ref[...] = grads[core]
    give_ref[...] = grads[1 - core]


def projection_grad_kernel(place_ref, gt_ref, x_ref, keep_ref, give_ref, grads, sems):
    core = place_ref[1]
    _, n_z, height, _ = grads.shape

    def columns(i, carry):
        at = pl.ds(pl.multiple_of(i * 2 * height, 2 * height), 2 * height)
        part = mm(gt_ref[...], x_ref[:, at]).T.astype(bf16)
        grads[0, i] = part[:height]
        grads[1, i] = part[height:]
        return carry

    lax.fori_loop(0, n_z, columns, 0)
    copies = [
        pltpu.make_async_copy(grads.at[core], keep_ref, sems.at[0]),
        pltpu.make_async_copy(grads.at[1 - core], give_ref, sems.at[1]),
    ]
    for copy in copies:
        copy.start()
    for copy in copies:
        copy.wait()


def vmem(n):
    return [pl.BlockSpec(memory_space=pltpu.VMEM)] * n


def smem(n):
    return [pl.BlockSpec(memory_space=pltpu.SMEM)] * n


def hbm(n):
    return [pl.BlockSpec(memory_space=pl.ANY)] * n


sds = jax.ShapeDtypeStruct


def call(kernel, name, gflops, in_specs, out_specs, out_shape, scratch, args):
    return pl.pallas_call(
        kernel,
        out_shape=tuple(out_shape),
        in_specs=in_specs,
        out_specs=tuple(out_specs),
        scratch_shapes=scratch,
        compiler_params=pltpu.CompilerParams(vmem_limit_bytes=VMEM_LIMIT),
        cost_estimate=pl.CostEstimate(
            flops=int(gflops * 1e9), bytes_accessed=1000, transcendentals=0
        ),
        name=name,
    )(*args)


def attend_forward(
    heads, n_t, place, lo, full, x_pieces, near, far, fv, cosine, sine, start, gain
):
    rows, cols = fv.shape
    x_at = [(mask, offset) for mask, offset, _ in x_pieces]
    pieces = [piece for _, _, piece in x_pieces]
    features, width = pieces[0].shape[1], near.shape[2]
    return call(
        functools.partial(attend_forward_kernel, heads, n_t, x_at),
        "attend_forward",
        5,
        smem(3) + vmem(5) + hbm(len(pieces) + 2),
        vmem(6) + hbm(2 + n_t),
        [
            sds((cols, rows), bf16),
            sds((cols, rows), bf16),
            sds((heads, rows, HEAD_DIM), bf16),
            sds((heads, rows, HEAD_DIM), bf16),
            sds((cols, rows), bf16),
            sds((heads, rows), f32),
            sds((rows, features), bf16),
            sds((features, width), bf16),
        ]
        + [sds((rows // n_t, cols), bf16)] * n_t,
        [
            pltpu.VMEM((rows, features), bf16),
            pltpu.VMEM((features, width), bf16),
            pltpu.VMEM((width, features), bf16),
            pltpu.VMEM((cols, rows), bf16),
            pltpu.VMEM((rows, cols), bf16),
            pltpu.VMEM((cols, BLOCK), f32),
            pltpu.SemaphoreType.DMA((len(pieces) + 2 * near.shape[0] + 2,)),
        ],
        (place, lo, full, fv, cosine, sine, start, gain, *pieces, near, far),
    )


def attend_backward(
    heads, n_t, place, lo, full, saved, grads, cosine, sine, start, w, gain
):
    rows, cols = start.shape[1], heads * HEAD_DIM
    count = rows // n_t
    features = w.shape[0]
    sizes = {mask: piece_rows(mask, count, n_t) for mask in range(n_t)}
    flat = [size for mask in range(n_t) for size in sizes[mask]]
    outs = call(
        functools.partial(attend_backward_kernel, heads, n_t),
        "attend_backward",
        10,
        smem(3) + vmem(11) + hbm(n_t),
        vmem(2) + hbm(len(flat)),
        [sds((3 * cols, rows), bf16), sds((rows, cols), f32)]
        + [sds((size, features), bf16) for size in flat],
        [
            pltpu.VMEM((rows, cols), bf16),
            pltpu.VMEM((rows, features), bf16),
            pltpu.VMEM((cols, rows), bf16),
            pltpu.VMEM((heads, rows), f32),
            pltpu.VMEM((cols, BLOCK), f32),
            pltpu.VMEM((cols, rows), f32),
            pltpu.VMEM((cols, rows), f32),
            pltpu.SemaphoreType.DMA((len(flat),)),
        ],
        (place, lo, full, *saved, cosine, sine, start, w, gain, *grads),
    )
    pieces = list(outs[2:])
    return outs[0], outs[1], {m: [pieces.pop(0) for _ in sizes[m]] for m in range(n_t)}


def feed_forward(n_z, n_t, place, xa, xb, ga, gb, wd, gathered):
    tokens, features = xa.shape
    ff = wd.shape[0]
    pieces, masks = [], []
    for mask, parts in gathered.items():
        first = 0
        for part in parts:
            pieces.append(part)
            masks.append((mask, first))
            first += part.shape[0]
    return call(
        functools.partial(feed_forward_kernel, masks),
        "feed_forward",
        0,
        smem(1) + vmem(5) + hbm(len(pieces)),
        vmem(4),
        [
            sds((2 * tokens, ff), bf16),
            sds((2 * tokens, 2 * ff), bf16),
            sds((tokens, features), f32),
            sds((tokens, features), bf16),
        ],
        [
            pltpu.VMEM((n_z, 2, n_t, features // (2 * n_z * n_t), 2 * ff), bf16),
            pltpu.SemaphoreType.DMA((len(pieces),)),
        ],
        (place, xa, xb, ga, gb, wd, *pieces),
    )


def gate_up_grad(n_z, n_t, place, xa, xb, gvu):
    tokens, features = xa.shape
    own = features // (2 * n_z * n_t)
    outs = call(
        functools.partial(gate_up_grad_kernel, n_t),
        "gate_up_grad",
        0,
        smem(1) + vmem(3),
        hbm(n_t),
        [sds((n_z, 2, own, gvu.shape[1]), bf16)] * n_t,
        [
            pltpu.VMEM((features, 2 * tokens), bf16),
            pltpu.VMEM((n_z, 2, n_t, own, gvu.shape[1]), bf16),
            pltpu.SemaphoreType.DMA((n_t,)),
        ],
        (place, xa, xb, gvu),
    )
    return list(outs)


def output_weight_scratch(near):
    n_z, n_t, height, cols = near.shape
    return [
        pltpu.VMEM((2 * n_z, n_t, height, cols), bf16),
        pltpu.SemaphoreType.DMA((2 * n_z,)),
    ]


def project_out(place, tokens, att, near, far):
    return call(
        functools.partial(project_out_kernel, len(att)),
        "project_out",
        20,
        smem(1) + vmem(1) + hbm(2) + vmem(len(att)),
        vmem(2),
        [sds(tokens.shape, f32), sds(tokens.shape, bf16)],
        output_weight_scratch(near),
        (place, tokens, near, far, *att),
    )


def branch_grad(place, hidden, u, u_got, g, near, far):
    _, n_t, _, cols = near.shape
    outs = call(
        branch_grad_kernel,
        "branch_grad",
        0,
        smem(1) + vmem(4) + hbm(2),
        vmem(2 + n_t),
        [sds(hidden.shape, f32), sds(hidden.shape, bf16)]
        + [sds((hidden.shape[0], cols), bf16)] * n_t,
        output_weight_scratch(near),
        (place, hidden, u, u_got, g, near, far),
    )
    return outs[0], outs[1], list(outs[2:])


def output_grad(n_z, place, branch, att):
    n_t, cols = len(att), att[0].shape[1]
    shape = (n_z, n_t, branch.shape[1] // (2 * n_z), cols)
    return call(
        output_grad_kernel,
        "output_grad",
        0,
        smem(1) + vmem(1 + n_t),
        vmem(2),
        [sds(shape, bf16)] * 2,
        [pltpu.VMEM(branch.shape[::-1], bf16), pltpu.VMEM((2,) + shape, bf16)],
        (place, branch, *att),
    )


def projection_grad(n_z, place, gt, x):
    height = x.shape[1] // (2 * n_z)
    return call(
        projection_grad_kernel,
        "projection_grad",
        0,
        smem(1) + vmem(2),
        hbm(2),
        [sds((n_z, height, gt.shape[0]), bf16)] * 2,
        [
            pltpu.VMEM((2, n_z, height, gt.shape[0]), bf16),
            pltpu.SemaphoreType.DMA((2,)),
        ],
        (place, gt, x),
    )


def doc_layout(doc_lengths, total):
    doc_ends = jnp.cumsum(doc_lengths)
    index = jnp.arange(total, dtype=jnp.int32)
    passed = (index[:, None] >= doc_ends[None, :]).astype(jnp.int32)
    return jnp.sum(passed * doc_lengths[None, :], axis=1)


def split_cols(weight, n_z):
    rows = weight.shape[0]
    return weight.reshape(rows, n_z, 2, -1).transpose(2, 0, 1, 3).reshape(2, rows, -1)


def join_cols(parts, n_z):
    rows = parts.shape[1]
    return parts.reshape(2, rows, n_z, -1).transpose(1, 2, 0, 3).reshape(rows, -1)


def body(
    tokens, lengths, first_values, attn_gain, query_weight, key_weight, value_weight,
    output_weight, mlp_gain, gate_weight, up_weight, down_weight, out_cotangent,
):
    n_t = lax.axis_size("tensor")
    n_z = lax.axis_size("z")
    t = lax.axis_index("tensor")
    core = lax.axis_index("core")
    place = jnp.stack([lax.axis_index("z"), core, t]).astype(jnp.int32)
    masks = range(n_t)
    count, features = tokens.shape
    rows = count * n_t
    wrows, cols = query_weight.shape
    heads = cols // HEAD_DIM
    ff_core = gate_weight.shape[1] // 2

    def by_core(near, far, axis):
        return jnp.where(
            core == 0, jnp.stack([near, far], axis=axis), jnp.stack([far, near], axis=axis)
        )

    token_f = tokens.astype(f32)
    inverse_in = lax.rsqrt(jnp.mean(token_f * token_f, axis=-1, keepdims=True) + eps)
    unit_in = (token_f * inverse_in).astype(bf16)
    with jax.named_scope("normed_tokens"):
        x_near = gather_near(unit_in)

    own_joint = jnp.concatenate([query_weight, key_weight, value_weight], axis=1)
    own_gains = attn_gain.shape[0]
    gain_rows = jnp.pad(attn_gain[None], ((0, 15), (0, 3 * cols - own_gains)))
    with jax.named_scope("attention_weights_z"):
        near = spread(jnp.concatenate([own_joint, gain_rows]), "z")

    gain_mid = mlp_gain.astype(f32)[:, None]
    both = jnp.concatenate(
        [split_cols(gate_weight, n_z), split_cols(up_weight, n_z)], axis=2
    ).astype(f32)
    both = (both * gain_mid[None]).astype(bf16)
    mine = lax.dynamic_index_in_dim(both, core, 0, False)
    with jax.named_scope("gate_up_core"):
        theirs = swap_core(lax.dynamic_index_in_dim(both, 1 - core, 0, False))
    with jax.named_scope("core_tokens"):
        grad_far = swap_core(out_cotangent)
    pair = by_core(mine, theirs, 0)

    start = doc_layout(lengths[0], rows)
    position = (jnp.arange(rows, dtype=jnp.int32) - start).astype(f32)
    freqs = rope_base ** (-jnp.arange(HALF, dtype=f32) * 2.0 / HEAD_DIM)
    angles = freqs[:, None] * position[None, :]
    cosine, sine = jnp.cos(angles), jnp.sin(angles)
    block_starts = start.reshape(-1, BLOCK)
    lo = block_starts[:, 0] // BLOCK
    full = jnp.minimum(
        (block_starts[:, -1] + BLOCK - 1) // BLOCK,
        jnp.arange(rows // BLOCK, dtype=jnp.int32),
    )
    start = start[None]

    x_near, near, pair, grad_far, output_weight, down_weight = together(
        x_near, near, pair, grad_far, output_weight, down_weight
    )

    with jax.named_scope("gate_up_z"):
        column = spread(pair, "z")
    with jax.named_scope("normed_tokens"):
        x_far = gather_far(unit_in, x_near)
    with jax.named_scope("attention_weights_core"):
        far = swap_core(near)
    drows = down_weight.shape[0]
    brows = drows + output_weight.size // features
    column_gain = by_core(near[:, wrows, :own_gains], far[:, wrows, :own_gains], 1).reshape(1, -1)
    with jax.named_scope("output_down_tensor"):
        slab = [
            down_weight,
            output_weight.reshape(-1, features),
            jnp.pad(column_gain, ((0, 15), (0, features - column_gain.shape[1]))),
        ]
        slabs = spread_tensor(jnp.concatenate(slab, axis=0))

    x_far, far, slabs, column = together(x_far, far, slabs, column)

    slab = by_index(slabs)
    with jax.named_scope("down_z"):
        down = lax.all_gather(slab[:, :drows].reshape(-1, features), "z", tiled=True)
    with jax.named_scope("output_weight_z"):
        out_near = send_z(slab[:, drows:brows].reshape(n_t, wrows, cols))
    gain = slab[:, brows, : column_gain.shape[1]].reshape(n_t, 2 * n_z, own_gains)
    gain = gain.transpose(1, 0, 2).astype(f32)
    gain_rows = lax.dynamic_index_in_dim(gain, place[0] * 2 + core, 0, False).reshape(-1, 1)
    gain = gain.reshape(1, features)
    with jax.named_scope("gate_up_tensor"):
        gu_near = gather_near(column)
    x_pieces = []
    for mask, parts in x_far.items():
        offset = 0
        for part in parts:
            x_pieces.append((mask, offset, part))
            offset += part.shape[0]
    qt, kt, kn, vn, ot, lse, x_full, joint_weight, *attended = attend_forward(
        heads, n_t, place, lo, full, x_pieces, near, far, first_values, cosine, sine, start, gain
    )

    attended, gu_near = together(attended, gu_near)

    with jax.named_scope("attended"):
        att = swap_all(attended)
    lse, out_near = together(lse, out_near)
    with jax.named_scope("output_weight_core"):
        out_far = swap_core(out_near)
    att, out_far, passed = together(att, out_far, pass_on(gu_near))
    with jax.named_scope("gate_up_tensor"):
        gathered = gather_far(column, gu_near, passed)
    hidden, unit_mid = project_out(place, tokens, att, out_near, out_far)
    unit_mid, gathered = together(unit_mid, gathered)
    with jax.named_scope("core_tokens"):
        unit_far = swap_core(unit_mid)

    inner, gvu, u_own, u_give = feed_forward(
        n_z, n_t, place, unit_mid, unit_far, out_cotangent, grad_far, down, gathered
    )
    with jax.named_scope("u_core"):
        u_got = swap_core(u_give)
    grad_both = jnp.concatenate([out_cotangent, grad_far], axis=0)
    grad_dn = mm(inner, grad_both, TN).astype(bf16).reshape(n_z, -1, features)

    u_got, grad_dn = together(u_got, grad_dn)

    with jax.named_scope("grad_down_z"):
        dn = lax.psum_scatter(grad_dn.reshape(-1, features), "z", scatter_dimension=0, tiled=True)
    grad_hidden, branch, grad_att = branch_grad(
        place, hidden, u_own, u_got, out_cotangent, out_near, out_far
    )
    with jax.named_scope("grad_attended"):
        grad_att = swap_all(grad_att)
    gu_parts = gate_up_grad(n_z, n_t, place, unit_mid, unit_far, gvu)
    keep_ow, give_ow = output_grad(n_z, place, branch, att)
    with jax.named_scope("grad_output_core"):
        got_ow = swap_core(give_ow)

    grad_att, gu_parts, got_ow = together(grad_att, gu_parts, got_ow)

    with jax.named_scope("grad_gate_up_tensor"):
        gu_terms = swap_all(gu_parts)
    with jax.named_scope("grad_output_z"):
        ow_terms = exchange(add(keep_ow, got_ow), "z")
    gt, grad_first, in_parts = attend_backward(
        heads, n_t, place, lo, full, (qt, kt, kn, vn, ot, lse), grad_att, cosine, sine, start,
        joint_weight, gain,
    )

    near_terms, last_term = gu_terms[:-1], gu_terms[-1:]
    in_parts, gt, ow_terms, inner, near_terms = together(
        in_parts, gt, ow_terms, inner, near_terms
    )

    with jax.named_scope("grad_normed"):
        in_far = scatter_far(in_parts)
    keep_jw, give_jw = projection_grad(n_z, place, gt, x_full)
    with jax.named_scope("grad_projection_core"):
        got_jw = swap_core(give_jw)
    jw_sum = add(keep_jw, got_jw)
    with jax.named_scope("grad_projection_z"):
        jw_terms = exchange(jw_sum, "z")
    out_part = mm(inner, down)
    out_give = out_part[count:].astype(bf16)

    jw_terms, last_term, out_give, dn = together(jw_terms, last_term, out_give, dn)
    gu_terms = near_terms + last_term

    with jax.named_scope("layer_out"):
        out_got = swap_core(out_give)
    layer_out = (hidden + out_part[:count] + out_got.astype(f32)).astype(bf16)
    gu_sums = sums_z(gu_terms)
    gu_sums, in_far = together(gu_sums, in_far)
    with jax.named_scope("grad_gate_up_z"):
        gu_terms = scatter_z(gu_sums)
    in_joined = scatter_join(in_parts, in_far)
    in_joined, jw_terms, ow_terms, dn = together(in_joined, jw_terms, ow_terms, dn)
    with jax.named_scope("grad_normed"):
        in_terms = scatter_near(in_parts, in_joined)

    ow = total(ow_terms).astype(bf16).reshape(n_t, -1, features)
    with jax.named_scope("grad_output_down_tensor"):
        both_terms = exchange(jnp.concatenate([dn.reshape(n_t, -1, features), ow], axis=1), "tensor")

    in_terms, gu_terms, jw_terms, both_terms = together(in_terms, gu_terms, jw_terms, both_terms)
    grad_down = total(both_terms)
    grad_output = grad_down[drows:].reshape(wrows, cols)
    grad_down = grad_down[:drows]

    grad_jw = total(jw_terms)
    gain_part = jnp.sum(grad_jw * own_joint.astype(f32), axis=1).reshape(n_t, -1)
    with jax.named_scope("grad_gain"):
        grad_attn_gain = total(exchange(gain_part, "tensor"))[None]
    grad_jw = grad_jw * gain_rows

    gu = total(gu_terms)
    gu_mine = lax.dynamic_index_in_dim(gu, core, 0, False)
    with jax.named_scope("grad_gate_up_core"):
        gu_other = swap_core(lax.dynamic_index_in_dim(gu, 1 - core, 0, False))

    grad_input = grad_hidden + norm_backward(token_f, total(in_terms), inverse_in)

    gu = by_core(gu_mine, gu_other, 0)
    grad_gate = join_cols(gu[:, :, :ff_core], n_z)
    grad_up = join_cols(gu[:, :, ff_core:], n_z)
    grad_mlp_gain = jnp.sum(
        grad_gate * gate_weight.astype(f32) + grad_up * up_weight.astype(f32), axis=1
    )
    grad_gate = grad_gate * gain_mid
    grad_up = grad_up * gain_mid

    return (
        layer_out,
        grad_input,
        grad_first,
        grad_attn_gain[0],
        grad_jw[:, :cols],
        grad_jw[:, cols : 2 * cols],
        grad_jw[:, 2 * cols :],
        grad_output,
        grad_mlp_gain,
        grad_gate,
        grad_up,
        grad_down,
    )


def solution(mesh):
    n_dp, n_t = mesh.shape["dp"], mesh.shape["tensor"]
    mesh = Mesh(mesh.devices.reshape(n_dp // 2, 2, n_t), ("z", "core", "tensor"))
    dp = ("z", "core")
    both = ("z", "core", "tensor")
    in_specs = (
        P(both, None),
        P(dp, None),
        P(dp, "tensor"),
        P(both),
        P(dp, "tensor"),
        P(dp, "tensor"),
        P(dp, "tensor"),
        P(dp, "tensor"),
        P(both),
        P(both, None),
        P(both, None),
        P(both, None),
        P(both, None),
    )
    out_specs = (
        P(both, None),
        P(both, None),
        P(dp, "tensor"),
        P(both),
        P(dp, "tensor"),
        P(dp, "tensor"),
        P(dp, "tensor"),
        P(dp, "tensor"),
        P(both),
        P(both, None),
        P(both, None),
        P(both, None),
    )
    return jax.shard_map(body, mesh=mesh, in_specs=in_specs, out_specs=out_specs, check_vma=False)
```

time: 553 us -> 427 us (0.77)
  waiting for transfers between devices: 199 us -> 109 us
  starting transfers between devices: 111 us -> 81.1 us
  Pallas kernels: 100 us -> 126 us
  local copies, waits for them, and re-layouts: 55.2 us -> 35.3 us
  matrix products: 28 us -> 12.5 us
  between operations: 2.48 us -> 15.4 us
  other arithmetic: 47.2 us -> 38.7 us
    ppermute x60 -> x24, waiting for transfers between devices: 140 us -> 62 us  [swap_tensor(): return lax.ppermute(value, 'tensor', [(i, i ^ mask) for i in range(size)])]
    all_to_all x0 -> x6, starting transfers between devices: none -> 32 us  [exchange(): return lax.all_to_all(value, axis, 0, 0)]
    ppermute x60 -> x24, starting transfers between devices: 51.5 us -> 19.7 us  [swap_tensor(): return lax.ppermute(value, 'tensor', [(i, i ^ mask) for i in range(size)])]
    ppermute x34 -> x16, starting transfers between devices: 59.7 us -> 29.3 us  [the longest x10 19.7 us: swap_core(): return lax.ppermute(value, 'core', [(0, 1), (1, 0)])]
    pallas_call x3 -> x8, Pallas kernels: 100 us -> 126 us  [call(): pl.pallas_call(kernel, out_shape=tuple(out_shape), in_specs=in_specs, out...]
    dynamic_update_slice x32 -> x0, local copies, waits for them, and re-layouts: 20.7 us -> none  [the longest x8 7.11 us: body(): lax.dynamic_update_slice(down, piece[:, None], (offset, t ^ mask, 0, 0))]
    ppermute x34 -> x16, waiting for transfers between devices: 58.5 us -> 42.3 us  [the longest x6 37.3 us: shift_z(): lax.ppermute(value, 'z', [(i, (i + step) % size) for i in range(size)])]
    dot_general x7 -> x2, matrix products: 28 us -> 12.5 us  [mm(): return lax.dot_general(left, right, dims, preferred_element_type=f32)]
  transfers between devices with their start and end apart: 94 -> 48, of which waited for: 31 -> 22; matrix products, arithmetic and copies ran while one was open for 20% -> 15% of each run, Pallas kernels for 14% -> 25%
where the time goes in v2:
time: 427 us; the launch traced here: 418 us
  Pallas kernels  126 us (30%)
  waiting for transfers between devices  109 us (26%)
  starting transfers between devices  81.1 us (19%)
  other arithmetic  38.7 us (9%)
  local copies, waits for them, and re-layouts  35.3 us (8%)
  between operations  15.4 us (4%)
  matrix products  12.5 us (3%)
    pallas_call x8, Pallas kernels, call(): pl.pallas_call(kernel, out_shape=tuple(out_shape), in_specs=in_specs, out...  126 us
    ppermute x24, waiting for transfers between devices, swap_tensor(): return lax.ppermute(value, 'tensor', [(i, i ^ mask) for i in range(size)])  62 us
    ppermute x6, waiting for transfers between devices, shift_z(): lax.ppermute(value, 'z', [(i, (i + step) % size) for i in range(size)])  37.3 us
    all_to_all x6, starting transfers between devices, exchange(): return lax.all_to_all(value, axis, 0, 0)  32 us
    ppermute x10, starting transfers between devices, swap_core(): return lax.ppermute(value, 'core', [(0, 1), (1, 0)])  19.7 us
    ppermute x24, starting transfers between devices, swap_tensor(): return lax.ppermute(value, 'tensor', [(i, i ^ mask) for i in range(size)])  19.7 us
    dot_general x2, matrix products, mm(): return lax.dot_general(left, right, dims, preferred_element_type=f32)  12.5 us
    ppermute x6, starting transfers between devices, shift_z(): lax.ppermute(value, 'z', [(i, (i + step) % size) for i in range(size)])  9.6 us
  transfers between devices with their start and end apart: 48, of which 22 were waited for; matrix products, arithmetic and copies ran while one was open for 15% of the time, Pallas kernels for 25%

profile of v2, /device:TPU:11, one launch (start us, length us, event | category | flops | bytes accessed | tf_op | source)
XLA Modules:
  0.0 418.3 jit_solution(5934258578061669933)
XLA Ops:
  7.2 1.6 fusion
  9.4 1.5 fusion.1.rest_0_
  10.9 1.3 collective-permute-start.1
  14.2 4.8 %all-to-all-start = ((bf16[4,144,768]{2,1,0:T(8,128)(2,1)}), bf16[4,144,768]{2,1,0:T(8,128)(2,1)}, u32[]{:S(2)}, u32[]{:S(2)}) async-start(bf16[4,144,768]{2,1,0:T(8,128)(2,1)} %broadcast_in_dim.7), calls=%async_computation | async-start | bytes 1769472 | tf_op jit(solution)/shard_map/attention_weights_z/all_to_all | solution.py:154
  18.9 1.8 collective-permute-start.3
  20.7 2.0 reshape.247
  24.6 2.0 reshape.249
  30.3 1.6 collective-permute-done.2
  32.6 1.3 maximum_select_fusion.1
  37.9 7.6 %all-to-all-start.1 = ((bf16[4,2,32,2816]{3,2,1,0:T(8,128)(2,1)}), bf16[4,2,32,2816]{3,2,1,0:T(8,128)(2,1)S(1)}, u32[]{:S(2)}, u32[]{:S(2)}) async-start(bf16[4,2,32,2816]{3,2,1,0:T(8,128)(2,1)} %broadcast_in_dim.8), calls=%async_computation.1 | async-start | bytes 2883584 | tf_op jit(solution)/shard_map/gate_up_z/all_to_all | solution.py:154
  45.8 1.8 collective-permute-start.6
  47.8 1.8 multiply_sine_fusion
  53.4 1.3 collective-permute-start.5
  55.7 1.3 collective-permute-start.9
  59.6 7.5 %collective-permute-done.5.rest_4_ = bf16[256,1024]{1,0:T(8,128)(2,1)} collective-permute-done((bf16[256,1024]{1,0:T(8,128)(2,1)S(1)}, bf16[256,1024]{1,0:T(8,128)(2,1)}, u32[]{:S(2)}, u32[]{:S(2)}) %collective-permute-start.5) | collective-permute-done | bytes 524320 | tf_op jit(solution)/shard_map/normed_tokens/ppermute | solution.py:31
  67.1 6.9 %collective-permute-done.4.rest_3_ = bf16[256,1024]{1,0:T(8,128)(2,1)} collective-permute-done((bf16[256,1024]{1,0:T(8,128)(2,1)S(1)}, bf16[256,1024]{1,0:T(8,128)(2,1)}, u32[]{:S(2)}, u32[]{:S(2)}) %collective-permute-start.4) | collective-permute-done | bytes 524320 | tf_op jit(solution)/shard_map/normed_tokens/ppermute | solution.py:31
  74.0 5.9 %collective-permute-done.8 = bf16[136,1024]{1,0:T(8,128)(2,1)S(1)} collective-permute-done((bf16[136,1024]{1,0:T(8,128)(2,1)S(1)}, bf16[136,1024]{1,0:T(8,128)(2,1)S(1)}, u32[]{:S(2)}, u32[]{:S(2)}) %collective-permute-start.8) | collective-permute-done | bytes 278560 | tf_op jit(solution)/shard_map/output_down_tensor/ppermute | solution.py:31
  82.9 2.3 collective-permute-start.11
  85.2 2.1 collective-permute-start.10
  88.1 28.1 %attend_forward.1 = (bf16[256,2048]{1,0:T(8,128)(2,1)}, bf16[256,2048]{1,0:T(8,128)(2,1)}, bf16[4,2048,64]{2,1,0:T(8,128)(2,1)}, bf16[4,2048,64]{2,1,0:T(8,128)(...) custom-call(s32[3]{0:T(128)} %pad_add_fusion.place_ref, ...), custom_call_target="tpu_custom_call" | custom-call | flops 5000000000 | bytes 1000 | tf_op jit(solution)/shard_map/attend_forward/pallas_call | solution.py:584
  116.4 10.4 %collective-permute-done.10 = bf16[4,128,256]{2,1,0:T(8,128)(2,1)} collective-permute-done((bf16[4,128,256]{2,1,0:T(8,128)(2,1)S(1)}, bf16[4,128,256]{2,1,0:T(8,128)(2,1)}, u32[]{:S(2)}, u32[]{:S(2)}) %collective-permute-start.10) | collective-permute-done | bytes 262176 | tf_op jit(solution)/shard_map/output_weight_z/ppermute | solution.py:40
  128.0 6.7 %collective-permute-start.18 = (bf16[4,4,128,256]{3,2,1,0:T(8,128)(2,1)S(1)}, bf16[4,4,128,256]{3,2,1,0:T(8,128)(2,1)S(1)}, u32[]{:S(2)}, u32[]{:S(2)}) collective-permute-start(bf16[4,4,128,256]{3,2,1,0:T(8,128)(2,1)S(1)} %pad_maximum_fusion.near), channel_id=1, source_target_pairs={{0,4},{4,0},{1,5},{5,1},{2,6},{6,2},{3,7},{7,3},{8,12},{12,8},{9,1... | collective-permute-start | bytes 3145736 | tf_op jit(solution)/shard_map/output_weight_core/ppermute | solution.py:35
  134.8 1.8 collective-permute-start.15
  140.2 3.1 collective-permute-done.15.rest_1_
  143.3 5.3 %collective-permute-done.16.rest_2_ = bf16[512,256]{1,0:T(8,128)(2,1)S(1)} collective-permute-done((bf16[512,256]{1,0:T(8,128)(2,1)S(1)}, bf16[512,256]{1,0:T(8,128)(2,1)S(1)}, u32[]{:S(2)}, u32[]{:S(2)}) %collective-permute-start.16) | collective-permute-done | bytes 262176 | tf_op jit(solution)/shard_map/attended/ppermute | solution.py:31
  149.9 1.3 collective-permute-start.19
  151.7 6.5 %project_out.1 = (f32[512,1024]{1,0:T(8,128)}, bf16[512,1024]{1,0:T(8,128)(2,1)}) custom-call(s32[3]{0:T(128)} %pad_add_fusion.place_ref, bf16[512,1024]{1,0:T(8,128)(2,1)} %token_ref.1, bf16[4,4,128,256]{3,2,1,0:T(8,128)(2,1)} %copy-done.6, bf16[4,4,128,256]{3,2,1,0:T(8,128)(2,1)} %copy-done.22, bf16[512,256]{1,0:T(8,128)(2,1)} %get-tuple-element.166.rest_0_, ...), custom_call_target="tpu_custom_call" | custom-call | flops 20000000000 | bytes 1000 | tf_op jit(solution)/shard_map/project_out/pallas_call | solution.py:584
  158.3 8.2 %collective-permute-done.19.rest_3_ = bf16[2,2,32,2816]{3,2,1,0:T(8,128)(2,1)} collective-permute-done((bf16[2,2,32,2816]{3,2,1,0:T(8,128)(2,1)S(1)}, bf16[2,2,32,2816]{3,2,1,0:T(8,128)(2,1)}, u32[]{:S(2)}, u32[]{:S(2)}) %collective-permute-start.19) | collective-permute-done | bytes 720928 | tf_op jit(solution)/shard_map/gate_up_tensor/ppermute | solution.py:31
  167.6 2.2 collective-permute-start.21
  169.8 2.5 collective-permute-done.21.xb_ref
  173.3 23.5 %feed_forward.1 = (bf16[1024,1408]{1,0:T(8,128)(2,1)}, bf16[1024,2816]{1,0:T(8,128)(2,1)}, f32[512,1024]{1,0:T(8,128)}, bf16[512,1024]{1,0:T(8,128)(2,1)}) custom-call(s32[3]{0:T(128)} %pad_add_fusion.place_ref, bf16[512,1024]{1,0:T(8,128)(2,1)} %get-tuple-element.181.xa_ref, bf16[512,1024]{1,0:T(8,128)(2,1)} %copy-done.5, bf16[512,1024]{1,0:T(8,128)(2,1)} %g_ref.1, ...), custom_call_target="tpu_custom_call" | custom-call | bytes 1000 | tf_op jit(solution)/shard_map/feed_forward/pallas_call | solution.py:584
  197.3 6.4 %convolution_convert_fusion = bf16[1408,1024]{1,0:T(8,128)(2,1)} fusion(bf16[1024,1408]{1,0:T(8,128)(2,1)} %get-tuple-element.218, bf16[512,1024]{1,0:T(8,128)(2,1)S(1)} %copy-done.21, bf16[512,1024]{1,0:T(8,128)(2,1)S(1)} %copy-done.4), kind=kOutput, calls=%fused_computation | convolution fusion | flops 2958426112 | bytes 7864320 | tf_op jit(solution)/shard_map/dot_general | solution.py:26
  204.7 7.9 %branch_grad.1 = (f32[512,1024]{1,0:T(8,128)}, bf16[512,1024]{1,0:T(8,128)(2,1)}, bf16[512,256]{1,0:T(8,128)(2,1)}, bf16[512,256]{1,0:T(8,128)(2,1)}, bf16[512,2...) custom-call(s32[3]{0:T(128)} %pad_add_fusion.place_ref, f32[512,1024]{1,0:T(8,128)} %get-tuple-element.170.hidden_ref, ...), custom_call_target="tpu_custom_call" | custom-call | bytes 1000 | tf_op jit(solution)/shard_map/branch_grad/pallas_call | solution.py:584
  212.6 4.4 %output_grad.1 = (bf16[4,4,128,256]{3,2,1,0:T(8,128)(2,1)}, bf16[4,4,128,256]{3,2,1,0:T(8,128)(2,1)}) custom-call(s32[3]{0:T(128)} %pad_add_fusion.place_ref, bf16[512,1024]{1,0:T(8,128)(2,1)} %get-tuple-element.201.branch_ref, bf16[512,256]{1,0:T(8,128)(2,1)} %get-tuple-element.166.rest_0_, bf16[512,256]{1,0:T(8,128)(2,1)} %copy-done.29, ...), custom_call_target="tpu_custom_call" | custom-call | bytes 1000 | tf_op jit(solution)/shard_map/output_grad/pallas_call | solution.py:584
  218.4 1.3 collective-permute-start.25
  219.8 14.5 %gate_up_grad.1 = (bf16[4,2,32,2816]{3,2,1,0:T(8,128)(2,1)}, bf16[4,2,32,2816]{3,2,1,0:T(8,128)(2,1)}, bf16[4,2,32,2816]{3,2,1,0:T(8,128)(2,1)}, bf16[4,2,32,2816]{3,2,1,0:T(8,128)(2,1)}) custom-call(s32[3]{0:T(128)} %pad_add_fusion.place_ref, bf16[512,1024]{1,0:T(8,128)(2,1)} %get-tuple-element.181.xa_ref, bf16[512,1024]{1,0:T(8,128)(2,1)} %copy-done.5, ...), custom_call_target="tpu_custom_call" | custom-call | bytes 1000 | tf_op jit(solution)/shard_map/gate_up_grad/pallas_call | solution.py:584
  234.4 1.3 add_convert_fusion
  235.7 4.7 %all-to-all-start.2 = ((bf16[4,4,128,256]{3,2,1,0:T(8,128)(2,1)}), bf16[4,4,128,256]{3,2,1,0:T(8,128)(2,1)S(1)}, u32[]{:S(2)}, u32[]{:S(2)}) async-start(bf16[4,4,128,256]{3,2,1,0:T(8,128)(2,1)} %add_convert_fusion), calls=%async_computation.2 | async-start | bytes 2097152 | tf_op jit(solution)/shard_map/grad_output_z/all_to_all | solution.py:154
  241.7 32.7 %attend_backward.1 = (bf16[768,2048]{1,0:T(8,128)(2,1)}, f32[2048,256]{1,0:T(8,128)}, bf16[512,1024]{1,0:T(8,128)(2,1)}, bf16[512,1024]{1,0:T(8,128)(2,1)}, bf16...) custom-call(s32[3]{0:T(128)} %pad_add_fusion.place_ref, s32[8]{0:T(128)} %get-tuple-element.288.lo_ref, ...), custom_call_target="tpu_custom_call" | custom-call | flops 10000000000 | bytes 1000 | tf_op jit(solution)/shard_map/attend_backward/pallas_call | solution.py:584
  274.4 4.2 all-to-all-done.2
  278.6 8.7 %projection_grad.1 = (bf16[4,128,768]{2,1,0:T(8,128)(2,1)}, bf16[4,128,768]{2,1,0:T(8,128)(2,1)}) custom-call(s32[3]{0:T(128)} %pad_add_fusion.place_ref, bf16[768,2048]{1,0:T(8,128)(2,1)} %get-tuple-element.219.gt_ref, bf16[2048,1024]{1,0:T(8,128)(2,1)} %get-tuple-element.220.x_ref), custom_call_target="tpu_custom_call" | custom-call | bytes 1000 | tf_op jit(solution)/shard_map/projection_grad/pallas_call | solution.py:584
  290.4 2.2 add_convert_fusion.1
  292.6 6.7 %all-to-all-start.3 = ((bf16[4,128,768]{2,1,0:T(8,128)(2,1)}), bf16[4,128,768]{2,1,0:T(8,128)(2,1)S(1)}, u32[]{:S(2)}, u32[]{:S(2)}) async-start(bf16[4,128,768]{2,1,0:T(8,128)(2,1)} %add_convert_fusion.1), calls=%async_computation.3 | async-start | bytes 1572864 | tf_op jit(solution)/shard_map/grad_projection_z/all_to_all | solution.py:154
  301.0 6.1 %fusion.28 = f32[1024,1024]{1,0:T(8,128)S(1)} fusion(bf16[1024,1408]{1,0:T(8,128)(2,1)} %get-tuple-element.218, bf16[1408,1024]{1,0:T(8,128)(2,1)} %all-gather.2.cloned.1.call-done.wd_ref), kind=kOutput, calls=%fused_computation.105 | convolution fusion | flops 2952790016 | bytes 9961472 | tf_op jit(solution)/shard_map/dot_general | solution.py:26
  309.4 13.3 %collective-permute-done.30 = bf16[4,2,32,2816]{3,2,1,0:T(8,128)(2,1)} collective-permute-done((bf16[4,2,32,2816]{3,2,1,0:T(8,128)(2,1)}, bf16[4,2,32,2816]{3,2,1,0:T(8,128)(2,1)}, u32[]{:S(2)}, u32[]{:S(2)}) %collective-permute-start.30) | collective-permute-done | bytes 1441824 | tf_op jit(solution)/shard_map/grad_gate_up_tensor/ppermute | solution.py:31
  322.7 4.2 %fusion.17 = (bf16[2,32,2816]{2,1,0:T(8,128)(2,1)}, bf16[2,32,2816]{2,1,0:T(8,128)(2,1)}, bf16[2,32,2816]{2,1,0:T(8,128)(2,1)}, f32[2,32,2816]{2,1,0:T(8,128)}) fusion(bf16[4,2,32,2816]{3,2,1,0:T(8,128)(2,1)} %collective-permute-done.30, s32[]{:T(128)S(6)} %select_n.236, bf16[4,2,32,2816]{3,2,1,0:T(8,128)(2,1)} %collective-permute-done.28, ...), kind=kLoop, calls=%fused_computation.50 | loop fusion | flops 5586944 | bytes 7569424 | tf_op jit(solution)/shard_map/add | solution.py:167
  327.0 7.0 %collective-permute-done.32 = bf16[256,1024]{1,0:T(8,128)(2,1)} collective-permute-done((bf16[256,1024]{1,0:T(8,128)(2,1)}, bf16[256,1024]{1,0:T(8,128)(2,1)}, u32[]{:S(2)}, u32[]{:S(2)}) %collective-permute-start.32) | collective-permute-done | bytes 524320 | tf_op jit(solution)/shard_map/grad_normed/ppermute | solution.py:31
  334.3 2.2 fusion.11
  336.5 2.2 fusion.12
  340.5 2.2 pad_maximum_fusion.1
  342.6 4.6 %all-to-all-start.4 = ((bf16[4,120,1024]{2,1,0:T(8,128)(2,1)}), bf16[4,120,1024]{2,1,0:T(8,128)(2,1)S(1)}, u32[]{:S(2)}, u32[]{:S(2)}) async-start(bf16[4,120,1024]{2,1,0:T(8,128)(2,1)} %pad_maximum_fusion.1), calls=%async_computation.5 | async-start | bytes 1966080 | tf_op jit(solution)/shard_map/grad_output_down_tensor/all_to_all | solution.py:154
  348.5 3.9 collective-permute-start.37
  352.5 5.5 %collective-permute-done.36 = bf16[2,32,2816]{2,1,0:T(8,128)(2,1)} collective-permute-done((bf16[2,32,2816]{2,1,0:T(8,128)(2,1)}, bf16[2,32,2816]{2,1,0:T(8,128)(2,1)}, u32[]{:S(2)}, u32[]{:S(2)}) %collective-permute-start.36) | collective-permute-done | bytes 360480 | tf_op jit(solution)/shard_map/grad_gate_up_z/ppermute | solution.py:40
  358.0 3.5 collective-permute-start.31
  361.6 16.8 %collective-permute-done.37 = bf16[2,32,2816]{2,1,0:T(8,128)(2,1)} collective-permute-done((bf16[2,32,2816]{2,1,0:T(8,128)(2,1)}, bf16[2,32,2816]{2,1,0:T(8,128)(2,1)}, u32[]{:S(2)}, u32[]{:S(2)}) %collective-permute-start.37) | collective-permute-done | bytes 360480 | tf_op jit(solution)/shard_map/grad_gate_up_z/ppermute | solution.py:40
  378.4 4.6 %collective-permute-done.38 = bf16[2,32,2816]{2,1,0:T(8,128)(2,1)} collective-permute-done((bf16[2,32,2816]{2,1,0:T(8,128)(2,1)S(1)}, bf16[2,32,2816]{2,1,0:T(8,128)(2,1)}, u32[]{:S(2)}, u32[]{:S(2)}) %collective-permute-start.38) | collective-permute-done | bytes 360480 | tf_op jit(solution)/shard_map/grad_gate_up_z/ppermute | solution.py:40
  384.9 1.5 bitcast_multiply_fusion
  387.1 3.6 all-to-all-start.5
  390.7 1.6 convert_add_fusion.1
  393.3 2.0 collective-permute-start.39
  397.6 2.0 fusion.4
  399.7 1.6 copy-done.14
  401.2 2.8 fusion.6
  409.4 1.6 broadcast_multiply_fusion
  (238 shorter events, 59.4 us)
Async XLA Ops:
  10.8 27.0 %copy-start.25 = (bf16[512,1024]{1,0:T(8,128)(2,1)}, bf16[512,1024]{1,0:T(8,128)(2,1)S(1)}, u32[]{:S(2)}) copy-start(bf16[512,1024]{1,0:T(8,128)(2,1)S(1)} %fusion.1.rest_0_) | copy-start | bytes 3145732
  10.9 24.2 %collective-permute-start.1 = (bf16[512,1024]{1,0:T(8,128)(2,1)S(1)}, bf16[512,1024]{1,0:T(8,128)(2,1)}, u32[]{:S(2)}, u32[]{:S(2)}) collective-permute-start(bf16[512,1024]{1,0:T(8,128)(2,1)S(1)} %fusion.1.rest_0_), channel_id=1, source_target_pairs={{0,2},{1,3},{2,0},{3,1},{4,6},{5,7},{6,4},{7,5},{8,10},{9,11},{10,... | collective-permute-start | bytes 3145736 | tf_op jit(solution)/shard_map/normed_tokens/ppermute | solution.py:31
  12.2 23.8 %collective-permute-start = (bf16[512,1024]{1,0:T(8,128)(2,1)S(1)}, bf16[512,1024]{1,0:T(8,128)(2,1)}, u32[]{:S(2)}, u32[]{:S(2)}) collective-permute-start(bf16[512,1024]{1,0:T(8,128)(2,1)S(1)} %fusion.1.rest_0_), channel_id=1, source_target_pairs={{0,1},{1,0},{2,3},{3,2},{4,5},{5,4},{6,7},{7,6},{8,9},{9,8},{10,11... | collective-permute-start | bytes 3145736 | tf_op jit(solution)/shard_map/normed_tokens/ppermute | solution.py:31
  14.2 22.5 %all-to-all-start = ((bf16[4,144,768]{2,1,0:T(8,128)(2,1)}), bf16[4,144,768]{2,1,0:T(8,128)(2,1)}, u32[]{:S(2)}, u32[]{:S(2)}) async-start(bf16[4,144,768]{2,1,0:T(8,128)(2,1)} %broadcast_in_dim.7), calls=%async_computation | async-start | bytes 1769472 | tf_op jit(solution)/shard_map/attention_weights_z/all_to_all | solution.py:154
  18.9 17.1 %collective-permute-start.3 = (bf16[512,1024]{1,0:T(8,128)(2,1)S(1)}, bf16[512,1024]{1,0:T(8,128)(2,1)S(1)}, u32[]{:S(2)}, u32[]{:S(2)}) collective-permute-start(bf16[512,1024]{1,0:T(8,128)(2,1)S(1)} %copy-done.3), channel_id=1, source_target_pairs={{0,4},{4,0},{1,5},{5,1},{2,6},{6,2},{3,7},{7,3},{8,12},{12,8},{9,1... | collective-permute-start | bytes 3145736 | tf_op jit(solution)/shard_map/core_tokens/ppermute | solution.py:35
  20.7 13.1 %copy-start.42 = (f32[32]{0:T(128)}, f32[32]{0:T(128)S(1)}, u32[]{:S(2)}) copy-start(f32[32]{0:T(128)S(1)} %convert_element_type.234) | copy-start | bytes 388
  30.3 1.6 collective-permute-start.2
  33.9 11.6 %copy-start.45 = (s32[1,3]{1,0:T(1,128)S(1)}, s32[1,3]{1,0:T(1,128)}, u32[]{:S(2)}) copy-start(s32[1,3]{1,0:T(1,128)} %param.14) | copy-start | bytes 40
  37.9 41.9 %all-to-all-start.1 = ((bf16[4,2,32,2816]{3,2,1,0:T(8,128)(2,1)}), bf16[4,2,32,2816]{3,2,1,0:T(8,128)(2,1)S(1)}, u32[]{:S(2)}, u32[]{:S(2)}) async-start(bf16[4,2,32,2816]{3,2,1,0:T(8,128)(2,1)} %broadcast_in_dim.8), calls=%async_computation.1 | async-start | bytes 2883584 | tf_op jit(solution)/shard_map/gate_up_z/all_to_all | solution.py:154
  45.5 10.2 %copy-start.32 = (bf16[88,1024]{1,0:T(8,128)(2,1)S(1)}, bf16[88,1024]{1,0:T(8,128)(2,1)}, u32[]{:S(2)}) copy-start(bf16[88,1024]{1,0:T(8,128)(2,1)} %param.24) | copy-start | bytes 540676
  45.5 126.8 %all-gather.2.cloned.1.call-start = ((), (), s32[]{:S(2)}) async-start(), calls=%async_computation.7 | async-start | bytes 3604480 | tf_op jit(solution)/shard_map/down_z/all_gather | solution.py:886
  45.8 35.8 %copy-start.34 = (s32[2048]{0:T(1024)}, s32[2048]{0:T(1024)S(1)}, u32[]{:S(2)}) copy-start(s32[2048]{0:T(1024)S(1)} %select_reduce_fusion) | copy-start | bytes 24580
  45.8 9.1 %collective-permute-start.6 = (bf16[4,144,768]{2,1,0:T(8,128)(2,1)}, bf16[4,144,768]{2,1,0:T(8,128)(2,1)}, u32[]{:S(2)}, u32[]{:S(2)}) collective-permute-start(bf16[4,144,768]{2,1,0:T(8,128)(2,1)} %all-to-all-done.rest_5_), channel_id=1, source_target_pairs={{0,4},{4,0},{1,5},{5,1},{2,6},{6,2},{3,7},{7,3},{8,12},{12,8},{9,1... | collective-permute-start | bytes 2654216 | tf_op jit(solution)/shard_map/attention_weights_core/ppermute | solution.py:35
  53.4 13.7 %collective-permute-start.5 = (bf16[256,1024]{1,0:T(8,128)(2,1)S(1)}, bf16[256,1024]{1,0:T(8,128)(2,1)}, u32[]{:S(2)}, u32[]{:S(2)}) collective-permute-start(bf16[256,1024]{1,0:T(8,128)(2,1)S(1)} %slice.126), channel_id=1, source_target_pairs={{0,1},{1,0},{2,3},{3,2},{4,5},{5,4},{6,7},{7,6},{8,9},{9,8},{10,11... | collective-permute-start | bytes 1572872 | tf_op jit(solution)/shard_map/normed_tokens/ppermute | solution.py:31
  54.7 19.3 %collective-permute-start.4 = (bf16[256,1024]{1,0:T(8,128)(2,1)S(1)}, bf16[256,1024]{1,0:T(8,128)(2,1)}, u32[]{:S(2)}, u32[]{:S(2)}) collective-permute-start(bf16[256,1024]{1,0:T(8,128)(2,1)S(1)} %slice.125), channel_id=1, source_target_pairs={{0,2},{1,3},{2,0},{3,1},{4,6},{5,7},{6,4},{7,5},{8,10},{9,11},{10,... | collective-permute-start | bytes 1572872 | tf_op jit(solution)/shard_map/normed_tokens/ppermute | solution.py:31
  55.7 18.2 %collective-permute-start.9 = (bf16[136,1024]{1,0:T(8,128)(2,1)S(1)}, bf16[136,1024]{1,0:T(8,128)(2,1)S(1)}, u32[]{:S(2)}, u32[]{:S(2)}) collective-permute-start(bf16[136,1024]{1,0:T(8,128)(2,1)S(1)} %fusion.18), channel_id=1, source_target_pairs={{0,3},{1,2},{2,1},{3,0},{4,7},{5,6},{6,5},{7,4},{8,11},{9,10},{10,... | collective-permute-start | bytes 835592 | tf_op jit(solution)/shard_map/output_down_tensor/ppermute | solution.py:31
  57.0 22.8 %collective-permute-start.8 = (bf16[136,1024]{1,0:T(8,128)(2,1)S(1)}, bf16[136,1024]{1,0:T(8,128)(2,1)S(1)}, u32[]{:S(2)}, u32[]{:S(2)}) collective-permute-start(bf16[136,1024]{1,0:T(8,128)(2,1)S(1)} %fusion.18), channel_id=1, source_target_pairs={{0,2},{1,3},{2,0},{3,1},{4,6},{5,7},{6,4},{7,5},{8,10},{9,11},{10,... | collective-permute-start | bytes 835592 | tf_op jit(solution)/shard_map/output_down_tensor/ppermute | solution.py:31
  57.2 22.6 %collective-permute-start.7 = (bf16[136,1024]{1,0:T(8,128)(2,1)S(1)}, bf16[136,1024]{1,0:T(8,128)(2,1)}, u32[]{:S(2)}, u32[]{:S(2)}) collective-permute-start(bf16[136,1024]{1,0:T(8,128)(2,1)S(1)} %fusion.18), channel_id=1, source_target_pairs={{0,1},{1,0},{2,3},{3,2},{4,5},{5,4},{6,7},{7,6},{8,9},{9,8},{10,11... | collective-permute-start | bytes 835592 | tf_op jit(solution)/shard_map/output_down_tensor/ppermute | solution.py:31
  79.8 54.9 %collective-permute-start.14 = (bf16[4,2,32,2816]{3,2,1,0:T(8,128)(2,1)S(1)}, bf16[4,2,32,2816]{3,2,1,0:T(8,128)(2,1)}, u32[]{:S(2)}, u32[]{:S(2)}) collective-permute-start(bf16[4,2,32,2816]{3,2,1,0:T(8,128)(2,1)S(1)} %all-to-all-done.1.rest_0_), channel_id=1, source_target_pairs={{0,2},{1,3},{2,0},{3,1},{4,6},{5,7},{6,4},{7,5},{8,10},{9,11},{10,... | collective-permute-start | bytes 4325384 | tf_op jit(solution)/shard_map/gate_up_tensor/ppermute | solution.py:31
  80.1 54.6 %collective-permute-start.13 = (bf16[4,2,32,2816]{3,2,1,0:T(8,128)(2,1)S(1)}, bf16[4,2,32,2816]{3,2,1,0:T(8,128)(2,1)}, u32[]{:S(2)}, u32[]{:S(2)}) collective-permute-start(bf16[4,2,32,2816]{3,2,1,0:T(8,128)(2,1)S(1)} %all-to-all-done.1.rest_0_), channel_id=1, source_target_pairs={{0,1},{1,0},{2,3},{3,2},{4,5},{5,4},{6,7},{7,6},{8,9},{9,8},{10,11... | collective-permute-start | bytes 4325384 | tf_op jit(solution)/shard_map/gate_up_tensor/ppermute | solution.py:31
  82.7 33.7 %collective-permute-start.12 = (bf16[4,128,256]{2,1,0:T(8,128)(2,1)S(1)}, bf16[4,128,256]{2,1,0:T(8,128)(2,1)}, u32[]{:S(2)}, u32[]{:S(2)}) collective-permute-start(bf16[4,128,256]{2,1,0:T(8,128)(2,1)S(1)} %reshape.254), channel_id=1, source_target_pairs={{0,24},{8,0},{16,8},{24,16},{1,25},{9,1},{17,9},{25,17},{2,26},{10... | collective-permute-start | bytes 786440 | tf_op jit(solution)/shard_map/output_weight_z/ppermute | solution.py:40
  82.9 33.6 %collective-permute-start.11 = (bf16[4,128,256]{2,1,0:T(8,128)(2,1)S(1)}, bf16[4,128,256]{2,1,0:T(8,128)(2,1)}, u32[]{:S(2)}, u32[]{:S(2)}) collective-permute-start(bf16[4,128,256]{2,1,0:T(8,128)(2,1)S(1)} %reshape.254), channel_id=1, source_target_pairs={{0,16},{8,24},{16,0},{24,8},{1,17},{9,25},{17,1},{25,9},{2,18},{10... | collective-permute-start | bytes 786440 | tf_op jit(solution)/shard_map/output_weight_z/ppermute | solution.py:40
  85.2 41.6 %collective-permute-start.10 = (bf16[4,128,256]{2,1,0:T(8,128)(2,1)S(1)}, bf16[4,128,256]{2,1,0:T(8,128)(2,1)}, u32[]{:S(2)}, u32[]{:S(2)}) collective-permute-start(bf16[4,128,256]{2,1,0:T(8,128)(2,1)S(1)} %reshape.254), channel_id=1, source_target_pairs={{0,8},{8,16},{16,24},{24,0},{1,9},{9,17},{17,25},{25,1},{2,10},{10... | collective-permute-start | bytes 786440 | tf_op jit(solution)/shard_map/output_weight_z/ppermute | solution.py:40
  88.1 234.7 %reduce-scatter.2.cloned.1.call-start = ((), (), s32[]{:S(2)}) async-start(), calls=%async_computation.8 | async-start | bytes 3604480 | tf_op jit(solution)/shard_map/grad_down_z/reduce_scatter | solution.py:931
  116.4 18.4 %copy-start.51 = (bf16[512,256]{1,0:T(8,128)(2,1)S(1)}, bf16[512,256]{1,0:T(8,128)(2,1)}, u32[]{:S(2)}) copy-start(bf16[512,256]{1,0:T(8,128)(2,1)} %get-tuple-element.160) | copy-start | bytes 786436
  116.4 20.2 %copy-start.50 = (bf16[512,256]{1,0:T(8,128)(2,1)S(1)}, bf16[512,256]{1,0:T(8,128)(2,1)}, u32[]{:S(2)}) copy-start(bf16[512,256]{1,0:T(8,128)(2,1)} %get-tuple-element.161) | copy-start | bytes 786436
  116.4 21.4 %copy-start.48 = (bf16[512,256]{1,0:T(8,128)(2,1)S(1)}, bf16[512,256]{1,0:T(8,128)(2,1)}, u32[]{:S(2)}) copy-start(bf16[512,256]{1,0:T(8,128)(2,1)} %get-tuple-element.162) | copy-start | bytes 786436
  128.0 23.7 %copy-start.6 = (bf16[4,4,128,256]{3,2,1,0:T(8,128)(2,1)}, bf16[4,4,128,256]{3,2,1,0:T(8,128)(2,1)S(1)}, u32[]{:S(2)}) copy-start(bf16[4,4,128,256]{3,2,1,0:T(8,128)(2,1)S(1)} %pad_maximum_fusion.near) | copy-start | bytes 3145732
  128.0 12.1 %collective-permute-start.18 = (bf16[4,4,128,256]{3,2,1,0:T(8,128)(2,1)S(1)}, bf16[4,4,128,256]{3,2,1,0:T(8,128)(2,1)S(1)}, u32[]{:S(2)}, u32[]{:S(2)}) collective-permute-start(bf16[4,4,128,256]{3,2,1,0:T(8,128)(2,1)S(1)} %pad_maximum_fusion.near), channel_id=1, source_target_pairs={{0,4},{4,0},{1,5},{5,1},{2,6},{6,2},{3,7},{7,3},{8,12},{12,8},{9,1... | collective-permute-start | bytes 3145736 | tf_op jit(solution)/shard_map/output_weight_core/ppermute | solution.py:35
  134.8 8.6 %collective-permute-start.15 = (bf16[512,256]{1,0:T(8,128)(2,1)S(1)}, bf16[512,256]{1,0:T(8,128)(2,1)S(1)}, u32[]{:S(2)}, u32[]{:S(2)}) collective-permute-start(bf16[512,256]{1,0:T(8,128)(2,1)S(1)} %copy-done.51), channel_id=1, source_target_pairs={{0,1},{1,0},{2,3},{3,2},{4,5},{5,4},{6,7},{7,6},{8,9},{9,8},{10,11... | collective-permute-start | bytes 786440 | tf_op jit(solution)/shard_map/attended/ppermute | solution.py:31
  136.6 12.1 %collective-permute-start.16 = (bf16[512,256]{1,0:T(8,128)(2,1)S(1)}, bf16[512,256]{1,0:T(8,128)(2,1)S(1)}, u32[]{:S(2)}, u32[]{:S(2)}) collective-permute-start(bf16[512,256]{1,0:T(8,128)(2,1)S(1)} %copy-done.50), channel_id=1, source_target_pairs={{0,2},{1,3},{2,0},{3,1},{4,6},{5,7},{6,4},{7,5},{8,10},{9,11},{10,... | collective-permute-start | bytes 786440 | tf_op jit(solution)/shard_map/attended/ppermute | solution.py:31
  137.8 12.1 %collective-permute-start.17 = (bf16[512,256]{1,0:T(8,128)(2,1)S(1)}, bf16[512,256]{1,0:T(8,128)(2,1)S(1)}, u32[]{:S(2)}, u32[]{:S(2)}) collective-permute-start(bf16[512,256]{1,0:T(8,128)(2,1)S(1)} %copy-done.48), channel_id=1, source_target_pairs={{0,3},{1,2},{2,1},{3,0},{4,7},{5,6},{6,5},{7,4},{8,11},{9,10},{10,... | collective-permute-start | bytes 786440 | tf_op jit(solution)/shard_map/attended/ppermute | solution.py:31
  140.2 11.5 %copy-start.22 = (bf16[4,4,128,256]{3,2,1,0:T(8,128)(2,1)}, bf16[4,4,128,256]{3,2,1,0:T(8,128)(2,1)S(1)}, u32[]{:S(2)}) copy-start(bf16[4,4,128,256]{3,2,1,0:T(8,128)(2,1)S(1)} %collective-permute-done.18.far) | copy-start | bytes 3145732
  149.9 16.6 %collective-permute-start.19 = (bf16[2,2,32,2816]{3,2,1,0:T(8,128)(2,1)S(1)}, bf16[2,2,32,2816]{3,2,1,0:T(8,128)(2,1)}, u32[]{:S(2)}, u32[]{:S(2)}) collective-permute-start(bf16[2,2,32,2816]{3,2,1,0:T(8,128)(2,1)S(1)} %slice.131), channel_id=1, source_target_pairs={{0,2},{1,3},{2,0},{3,1},{4,6},{5,7},{6,4},{7,5},{8,10},{9,11},{10,... | collective-permute-start | bytes 2162696 | tf_op jit(solution)/shard_map/gate_up_tensor/ppermute | solution.py:31
  151.2 16.4 %collective-permute-start.20 = (bf16[2,2,32,2816]{3,2,1,0:T(8,128)(2,1)S(1)}, bf16[2,2,32,2816]{3,2,1,0:T(8,128)(2,1)}, u32[]{:S(2)}, u32[]{:S(2)}) collective-permute-start(bf16[2,2,32,2816]{3,2,1,0:T(8,128)(2,1)S(1)} %slice.132), channel_id=1, source_target_pairs={{0,1},{1,0},{2,3},{3,2},{4,5},{5,4},{6,7},{7,6},{8,9},{9,8},{10,11... | collective-permute-start | bytes 2162696 | tf_op jit(solution)/shard_map/gate_up_tensor/ppermute | solution.py:31
  167.6 29.7 %copy-start.4 = (bf16[512,1024]{1,0:T(8,128)(2,1)S(1)}, bf16[512,1024]{1,0:T(8,128)(2,1)}, u32[]{:S(2)}) copy-start(bf16[512,1024]{1,0:T(8,128)(2,1)} %g_ref.1) | copy-start | bytes 3145732
  167.6 29.7 %copy-start.21 = (bf16[512,1024]{1,0:T(8,128)(2,1)S(1)}, bf16[512,1024]{1,0:T(8,128)(2,1)}, u32[]{:S(2)}) copy-start(bf16[512,1024]{1,0:T(8,128)(2,1)} %copy-done.20) | copy-start | bytes 3145732
  167.6 4.7 %collective-permute-start.21 = (bf16[512,1024]{1,0:T(8,128)(2,1)}, bf16[512,1024]{1,0:T(8,128)(2,1)S(1)}, u32[]{:S(2)}, u32[]{:S(2)}) collective-permute-start(bf16[512,1024]{1,0:T(8,128)(2,1)} %get-tuple-element.181.xa_ref), channel_id=1, source_target_pairs={{0,4},{4,0},{1,5},{5,1},{2,6},{6,2},{3,7},{7,3},{8,12},{12,8},{9,1... | collective-permute-start | bytes 3145736 | tf_op jit(solution)/shard_map/core_tokens/ppermute | solution.py:35
  196.8 6.8 %collective-permute-start.22 = (bf16[512,1024]{1,0:T(8,128)(2,1)}, bf16[512,1024]{1,0:T(8,128)(2,1)S(1)}, u32[]{:S(2)}, u32[]{:S(2)}) collective-permute-start(bf16[512,1024]{1,0:T(8,128)(2,1)} %get-tuple-element.189), channel_id=1, source_target_pairs={{0,4},{4,0},{1,5},{5,1},{2,6},{6,2},{3,7},{7,3},{8,12},{12,8},{9,1... | collective-permute-start | bytes 3145736 | tf_op jit(solution)/shard_map/u_core/ppermute | solution.py:35
  217.0 17.4 %collective-permute-start.26 = (bf16[4,4,128,256]{3,2,1,0:T(8,128)(2,1)}, bf16[4,4,128,256]{3,2,1,0:T(8,128)(2,1)S(1)}, u32[]{:S(2)}, u32[]{:S(2)}) collective-permute-start(bf16[4,4,128,256]{3,2,1,0:T(8,128)(2,1)} %get-tuple-element.202), channel_id=1, source_target_pairs={{0,4},{4,0},{1,5},{5,1},{2,6},{6,2},{3,7},{7,3},{8,12},{12,8},{9,1... | collective-permute-start | bytes 3145736 | tf_op jit(solution)/shard_map/grad_output_core/ppermute | solution.py:35
  217.1 17.2 %collective-permute-start.23 = (bf16[512,256]{1,0:T(8,128)(2,1)S(1)}, bf16[512,256]{1,0:T(8,128)(2,1)S(1)}, u32[]{:S(2)}, u32[]{:S(2)}) collective-permute-start(bf16[512,256]{1,0:T(8,128)(2,1)S(1)} %copy-done.54), channel_id=1, source_target_pairs={{0,1},{1,0},{2,3},{3,2},{4,5},{5,4},{6,7},{7,6},{8,9},{9,8},{10,11... | collective-permute-start | bytes 786440 | tf_op jit(solution)/shard_map/grad_attended/ppermute | solution.py:31
  217.7 16.7 %collective-permute-start.24 = (bf16[512,256]{1,0:T(8,128)(2,1)S(1)}, bf16[512,256]{1,0:T(8,128)(2,1)S(1)}, u32[]{:S(2)}, u32[]{:S(2)}) collective-permute-start(bf16[512,256]{1,0:T(8,128)(2,1)S(1)} %copy-done.53), channel_id=1, source_target_pairs={{0,2},{1,3},{2,0},{3,1},{4,6},{5,7},{6,4},{7,5},{8,10},{9,11},{10,... | collective-permute-start | bytes 786440 | tf_op jit(solution)/shard_map/grad_attended/ppermute | solution.py:31
  218.4 15.9 %collective-permute-start.25 = (bf16[512,256]{1,0:T(8,128)(2,1)S(1)}, bf16[512,256]{1,0:T(8,128)(2,1)S(1)}, u32[]{:S(2)}, u32[]{:S(2)}) collective-permute-start(bf16[512,256]{1,0:T(8,128)(2,1)S(1)} %copy-done.52), channel_id=1, source_target_pairs={{0,3},{1,2},{2,1},{3,0},{4,7},{5,6},{6,5},{7,4},{8,11},{9,10},{10,... | collective-permute-start | bytes 786440 | tf_op jit(solution)/shard_map/grad_attended/ppermute | solution.py:31
  219.8 14.6 %copy-start.23 = (bf16[4,4,128,256]{3,2,1,0:T(8,128)(2,1)S(1)}, bf16[4,4,128,256]{3,2,1,0:T(8,128)(2,1)}, u32[]{:S(2)}) copy-start(bf16[4,4,128,256]{3,2,1,0:T(8,128)(2,1)} %get-tuple-element.213) | copy-start | bytes 3145732
  235.7 42.9 %all-to-all-start.2 = ((bf16[4,4,128,256]{3,2,1,0:T(8,128)(2,1)}), bf16[4,4,128,256]{3,2,1,0:T(8,128)(2,1)S(1)}, u32[]{:S(2)}, u32[]{:S(2)}) async-start(bf16[4,4,128,256]{3,2,1,0:T(8,128)(2,1)} %add_convert_fusion), calls=%async_computation.2 | async-start | bytes 2097152 | tf_op jit(solution)/shard_map/grad_output_z/all_to_all | solution.py:154
  240.4 34.0 %collective-permute-start.27 = (bf16[4,2,32,2816]{3,2,1,0:T(8,128)(2,1)}, bf16[4,2,32,2816]{3,2,1,0:T(8,128)(2,1)S(1)}, u32[]{:S(2)}, u32[]{:S(2)}) collective-permute-start(bf16[4,2,32,2816]{3,2,1,0:T(8,128)(2,1)} %get-tuple-element.216), channel_id=1, source_target_pairs={{0,1},{1,0},{2,3},{3,2},{4,5},{5,4},{6,7},{7,6},{8,9},{9,8},{10,11... | collective-permute-start | bytes 4325384 | tf_op jit(solution)/shard_map/grad_gate_up_tensor/ppermute | solution.py:31
  240.9 33.5 %collective-permute-start.28 = (bf16[4,2,32,2816]{3,2,1,0:T(8,128)(2,1)}, bf16[4,2,32,2816]{3,2,1,0:T(8,128)(2,1)}, u32[]{:S(2)}, u32[]{:S(2)}) collective-permute-start(bf16[4,2,32,2816]{3,2,1,0:T(8,128)(2,1)} %get-tuple-element.217), channel_id=1, source_target_pairs={{0,2},{1,3},{2,0},{3,1},{4,6},{5,7},{6,4},{7,5},{8,10},{9,11},{10,... | collective-permute-start | bytes 4325384 | tf_op jit(solution)/shard_map/grad_gate_up_tensor/ppermute | solution.py:31
  274.4 12.9 %copy-start.17 = (bf16[4,2,32,2816]{3,2,1,0:T(8,128)(2,1)}, bf16[4,2,32,2816]{3,2,1,0:T(8,128)(2,1)S(1)}, u32[]{:S(2)}) copy-start(bf16[4,2,32,2816]{3,2,1,0:T(8,128)(2,1)S(1)} %collective-permute-done.27) | copy-start | bytes 4325380
  287.3 3.1 collective-permute-start.29
  288.3 34.4 %collective-permute-start.30 = (bf16[4,2,32,2816]{3,2,1,0:T(8,128)(2,1)}, bf16[4,2,32,2816]{3,2,1,0:T(8,128)(2,1)}, u32[]{:S(2)}, u32[]{:S(2)}) collective-permute-start(bf16[4,2,32,2816]{3,2,1,0:T(8,128)(2,1)} %get-tuple-element.223), channel_id=1, source_target_pairs={{0,3},{1,2},{2,1},{3,0},{4,7},{5,6},{6,5},{7,4},{8,11},{9,10},{10,... | collective-permute-start | bytes 4325384 | tf_op jit(solution)/shard_map/grad_gate_up_tensor/ppermute | solution.py:31
  292.6 30.1 %all-to-all-start.3 = ((bf16[4,128,768]{2,1,0:T(8,128)(2,1)}), bf16[4,128,768]{2,1,0:T(8,128)(2,1)S(1)}, u32[]{:S(2)}, u32[]{:S(2)}) async-start(bf16[4,128,768]{2,1,0:T(8,128)(2,1)} %add_convert_fusion.1), calls=%async_computation.3 | async-start | bytes 1572864 | tf_op jit(solution)/shard_map/grad_projection_z/all_to_all | solution.py:154
  299.4 34.5 %collective-permute-start.32 = (bf16[256,1024]{1,0:T(8,128)(2,1)}, bf16[256,1024]{1,0:T(8,128)(2,1)}, u32[]{:S(2)}, u32[]{:S(2)}) collective-permute-start(bf16[256,1024]{1,0:T(8,128)(2,1)} %get-tuple-element.233), channel_id=1, source_target_pairs={{0,1},{1,0},{2,3},{3,2},{4,5},{5,4},{6,7},{7,6},{8,9},{9,8},{10,11... | collective-permute-start | bytes 1572872 | tf_op jit(solution)/shard_map/grad_normed/ppermute | solution.py:31
  299.8 34.5 %collective-permute-start.33 = (bf16[256,1024]{1,0:T(8,128)(2,1)}, bf16[256,1024]{1,0:T(8,128)(2,1)}, u32[]{:S(2)}, u32[]{:S(2)}) collective-permute-start(bf16[256,1024]{1,0:T(8,128)(2,1)} %get-tuple-element.234), channel_id=1, source_target_pairs={{0,2},{1,3},{2,0},{3,1},{4,6},{5,7},{6,4},{7,5},{8,10},{9,11},{10,... | collective-permute-start | bytes 1572872 | tf_op jit(solution)/shard_map/grad_normed/ppermute | solution.py:31
  307.1 15.7 %copy-start.16 = (bf16[4,2,32,2816]{3,2,1,0:T(8,128)(2,1)S(1)}, bf16[4,2,32,2816]{3,2,1,0:T(8,128)(2,1)}, u32[]{:S(2)}) copy-start(bf16[4,2,32,2816]{3,2,1,0:T(8,128)(2,1)} %get-tuple-element.229) | copy-start | bytes 4325380
  338.7 44.3 %collective-permute-start.34 = (bf16[512,1024]{1,0:T(8,128)(2,1)}, bf16[512,1024]{1,0:T(8,128)(2,1)S(1)}, u32[]{:S(2)}, u32[]{:S(2)}) collective-permute-start(bf16[512,1024]{1,0:T(8,128)(2,1)} %fusion.11), channel_id=1, source_target_pairs={{0,1},{1,0},{2,3},{3,2},{4,5},{5,4},{6,7},{7,6},{8,9},{9,8},{10,11... | collective-permute-start | bytes 3145736 | tf_op jit(solution)/shard_map/grad_normed/ppermute | solution.py:31
  338.9 44.0 %collective-permute-start.35 = (bf16[512,1024]{1,0:T(8,128)(2,1)}, bf16[512,1024]{1,0:T(8,128)(2,1)S(1)}, u32[]{:S(2)}, u32[]{:S(2)}) collective-permute-start(bf16[512,1024]{1,0:T(8,128)(2,1)} %fusion.12), channel_id=1, source_target_pairs={{0,2},{1,3},{2,0},{3,1},{4,6},{5,7},{6,4},{7,5},{8,10},{9,11},{10,... | collective-permute-start | bytes 3145736 | tf_op jit(solution)/shard_map/grad_normed/ppermute | solution.py:31
  340.5 11.9 %copy-start.28 = (bf16[2,32,2816]{2,1,0:T(8,128)(2,1)S(1)}, bf16[2,32,2816]{2,1,0:T(8,128)(2,1)}, u32[]{:S(2)}) copy-start(bf16[2,32,2816]{2,1,0:T(8,128)(2,1)} %get-tuple-element.246) | copy-start | bytes 1081348
  342.6 40.3 %all-to-all-start.4 = ((bf16[4,120,1024]{2,1,0:T(8,128)(2,1)}), bf16[4,120,1024]{2,1,0:T(8,128)(2,1)S(1)}, u32[]{:S(2)}, u32[]{:S(2)}) async-start(bf16[4,120,1024]{2,1,0:T(8,128)(2,1)} %pad_maximum_fusion.1), calls=%async_computation.5 | async-start | bytes 1966080 | tf_op jit(solution)/shard_map/grad_output_down_tensor/all_to_all | solution.py:154
  347.3 10.7 %collective-permute-start.36 = (bf16[2,32,2816]{2,1,0:T(8,128)(2,1)}, bf16[2,32,2816]{2,1,0:T(8,128)(2,1)}, u32[]{:S(2)}, u32[]{:S(2)}) collective-permute-start(bf16[2,32,2816]{2,1,0:T(8,128)(2,1)} %get-tuple-element.244), channel_id=1, source_target_pairs={{0,8},{8,16},{16,24},{24,0},{1,9},{9,17},{17,25},{25,1},{2,10},{10... | collective-permute-start | bytes 1081352 | tf_op jit(solution)/shard_map/grad_gate_up_z/ppermute | solution.py:40
  348.5 29.9 %collective-permute-start.37 = (bf16[2,32,2816]{2,1,0:T(8,128)(2,1)}, bf16[2,32,2816]{2,1,0:T(8,128)(2,1)}, u32[]{:S(2)}, u32[]{:S(2)}) collective-permute-start(bf16[2,32,2816]{2,1,0:T(8,128)(2,1)} %get-tuple-element.245), channel_id=1, source_target_pairs={{0,16},{8,24},{16,0},{24,8},{1,17},{9,25},{17,1},{25,9},{2,18},{10... | collective-permute-start | bytes 1081352 | tf_op jit(solution)/shard_map/grad_gate_up_z/ppermute | solution.py:40
  352.4 30.5 %collective-permute-start.38 = (bf16[2,32,2816]{2,1,0:T(8,128)(2,1)S(1)}, bf16[2,32,2816]{2,1,0:T(8,128)(2,1)}, u32[]{:S(2)}, u32[]{:S(2)}) collective-permute-start(bf16[2,32,2816]{2,1,0:T(8,128)(2,1)S(1)} %copy-done.28), channel_id=1, source_target_pairs={{0,24},{8,0},{16,8},{24,16},{1,25},{9,1},{17,9},{25,17},{2,26},{10... | collective-permute-start | bytes 1081352 | tf_op jit(solution)/shard_map/grad_gate_up_z/ppermute | solution.py:40
  358.0 41.7 %collective-permute-start.31 = (bf16[512,1024]{1,0:T(8,128)(2,1)}, bf16[512,1024]{1,0:T(8,128)(2,1)}, u32[]{:S(2)}, u32[]{:S(2)}) collective-permute-start(bf16[512,1024]{1,0:T(8,128)(2,1)} %slice.229), channel_id=1, source_target_pairs={{0,4},{4,0},{1,5},{5,1},{2,6},{6,2},{3,7},{7,3},{8,12},{12,8},{9,1... | collective-permute-start | bytes 3145736 | tf_op jit(solution)/shard_map/layer_out/ppermute | solution.py:35
  387.1 18.4 %all-to-all-start.5 = ((f32[4,1,32]{2,1,0:T(1,128)}), f32[4,1,32]{2,1,0:T(1,128)S(1)}, u32[]{:S(2)}, u32[]{:S(2)}) async-start(f32[4,1,32]{2,1,0:T(1,128)} %bitcast.29), calls=%async_computation.6 | async-start | bytes 4096 | tf_op jit(solution)/shard_map/grad_gain/all_to_all | solution.py:154
  393.3 12.7 %collective-permute-start.39 = (f32[32,2816]{1,0:T(8,128)}, f32[32,2816]{1,0:T(8,128)}, u32[]{:S(2)}, u32[]{:S(2)}) collective-permute-start(f32[32,2816]{1,0:T(8,128)} %get-tuple-element.275), channel_id=1, source_target_pairs={{0,4},{4,0},{1,5},{5,1},{2,6},{6,2},{3,7},{7,3},{8,12},{12,8},{9,1... | collective-permute-start | bytes 1081352 | tf_op jit(solution)/shard_map/grad_gate_up_core/ppermute | solution.py:35
  (40 other events, 140.8 us)
Sparse Core Ops, SparseCore 0:
  88.2 66.4 all-gather.1
  203.8 71.7 reduce-scatter.1
